TPU v7x, 128 devices: a whole 4x4x4 slice. The times are simulated.
128 devices in a mesh: head: 2 (over z_hi), blk: 64 (over z_lo, x, y, core).
Axes of the slice: x: 4, y: 4, z: 4 (z_hi: 2, z_lo: 2; z = z_hi * 2 + z_lo), core: 2. Of those that a mesh axis runs over, the one named last changes fastest.
Arguments:
- hidden_in: bfloat16 [16384, 2048], P(('head', 'blk')), may hold values from -6 to 6
- gain_attn: float32 [2048], replicated, may hold values from 0.1 to 1.9
- gain_ffn: float32 [2048], replicated, may hold values from 0.1 to 1.9
- w_query: bfloat16 [2048, 2048], P(('head', 'blk')), may hold values from -0.125 to 0.125
- w_key: bfloat16 [2048, 1024], P(('head', 'blk')), may hold values from -0.125 to 0.125
- w_value: bfloat16 [2048, 1024], P(('head', 'blk')), may hold values from -0.125 to 0.125
- w_out: bfloat16 [2048, 2048], P(('head', 'blk')), may hold values from -0.375 to 0.375
- w_gate: bfloat16 [2048, 8192], P(('head', 'blk')), may hold values from -0.125 to 0.125
- w_up: bfloat16 [2048, 8192], P(('head', 'blk')), may hold values from -0.125 to 0.125
- w_down: bfloat16 [8192, 2048], P(('head', 'blk')), may hold values from -0.0625 to 0.0625
- qkv_shrink: bfloat16 [2048, 384], replicated, may hold values from -0.125 to 0.125
- query_expand: bfloat16 [128, 2048], replicated, may hold values from -1.5 to 1.5
- key_expand: bfloat16 [128, 1024], replicated, may hold values from -1.5 to 1.5
- value_expand: bfloat16 [128, 1024], replicated, may hold values from -1.5 to 1.5
- out_shrink: bfloat16 [2048, 128], replicated, may hold values from -0.125 to 0.125
- out_expand: bfloat16 [128, 2048], replicated, may hold values from -1.5 to 1.5
- gateup_shrink: bfloat16 [2048, 256], replicated, may hold values from -0.125 to 0.125
- gate_expand: bfloat16 [128, 8192], replicated, may hold values from -1.5 to 1.5
- up_expand: bfloat16 [128, 8192], replicated, may hold values from -1.5 to 1.5
- down_shrink: bfloat16 [8192, 128], replicated, may hold values from -0.0625 to 0.0625
- down_expand: bfloat16 [128, 2048], replicated, may hold values from -1.5 to 1.5
- lengths: int32 [16], replicated, may hold values from 1 to 4096, 16384 in all
- adapter: int32 [16], replicated, may hold values from 0 to 7
- packed_pos: int32 [16384], replicated, may hold values from 0 to 16383, as said below
- cotangent: bfloat16 [16384, 2048], P(('head', 'blk')), may hold values from -6 to 6
Outputs:
- output: bfloat16 [16384, 2048], P(('head', 'blk'))
- grad_input: bfloat16 [16384, 2048], P(('head', 'blk'))
- grad_qkv_shrink: float32 [2048, 384], replicated
- grad_query_expand: float32 [128, 2048], replicated
- grad_key_expand: float32 [128, 1024], replicated
- grad_value_expand: float32 [128, 1024], replicated
- grad_out_shrink: float32 [2048, 128], replicated
- grad_out_expand: float32 [128, 2048], replicated
- grad_gateup_shrink: float32 [2048, 256], replicated
- grad_gate_expand: float32 [128, 8192], replicated
- grad_up_expand: float32 [128, 8192], replicated
- grad_down_shrink: float32 [8192, 128], replicated
- grad_down_expand: float32 [128, 2048], replicated
Inputs may be any that keep to these rules, and one draw needn't show every extreme that they name: The lengths sum to 16384; sequence s takes the packed positions after those of sequences 0 to s - 1; the longest is exactly 4096. packed_pos is a permutation of 0 to 16383. Each half of an aligned block of 128 rows holds one aligned run of 64 packed positions, in shuffled order; the block of 128 rows held by the device at head index i and blk index j (rows (i * 64 + j) * 128 onward) holds runs number (2 i) * 64 + (j + r) % 64 and (2 i + 1) * 64 + (j + r) % 64, for one r per draw.
All inputs are finite; a program needn't handle non-finite values.
Results may differ from a plain program's by a relative error of at most 0.028.
Values may be sent and summed in bfloat16 or wider, within the bound.
No kernel may reach another device: no remote copies, remote signals or barrier semaphores. Data moves between devices by JAX's collectives and lax.ppermute only.
A program may use at most 448 MiB of HBM per device.

v0:
```python
from functools import partial
import math

import jax
import jax.numpy as jnp
from jax import lax
from jax.sharding import PartitionSpec as P

HEAD_SIZE = 256
RANK = 16


norm_eps = 1e-06
rope_theta = 1000042.0
neg_big = -1e30


def product(left, right):
    return jnp.dot(left, right, preferred_element_type=jnp.float32)


def times_transposed(left, right):
    return lax.dot_general(
        left, right, (((1,), (1,)), ((), ())), preferred_element_type=jnp.float32
    )


def inner_rows(left, right):
    return lax.dot_general(
        left, right, (((0,), (0,)), ((), ())), preferred_element_type=jnp.float32
    )


def row_scale(value_matrix):
    return lax.rsqrt(jnp.mean(value_matrix * value_matrix, axis=-1, keepdims=True) + norm_eps)


def norm_back(value_matrix, scale, gain, grad):
    scaled = gain * grad
    return scale * scaled - value_matrix * (scale * scale * scale) * jnp.mean(
        value_matrix * scaled, axis=-1, keepdims=True
    )


def rotate(value_matrix):
    middle = value_matrix.shape[-1] // 2
    return jnp.concatenate([-value_matrix[..., middle:], value_matrix[..., :middle]], axis=-1)


def rope_tables(positions, width):
    middle = width // 2
    inverse = rope_theta ** (-(jnp.arange(middle, dtype=jnp.float32) * 2.0) / width)
    angles = positions.astype(jnp.float32)[:, None] * inverse[None, :]
    cos_table = jnp.concatenate([jnp.cos(angles), jnp.cos(angles)], axis=-1)[:, None, :]
    sin_table = jnp.concatenate([jnp.sin(angles), jnp.sin(angles)], axis=-1)[:, None, :]
    return (cos_table, sin_table)


def token_meta(lengths, adapter, packed):
    seq_ends = jnp.cumsum(lengths)
    starts = seq_ends - lengths
    seq_count = lengths.shape[0]
    member = (packed[:, None] >= starts[None, :]) & (packed[:, None] < seq_ends[None, :])
    member_int = member.astype(jnp.int32)
    seq_ids = jnp.sum(member_int * jnp.arange(seq_count, dtype=jnp.int32)[None, :], axis=1)
    positions = packed - jnp.sum(member_int * starts[None, :], axis=1)
    owners = jnp.sum(member_int * adapter[None, :], axis=1)
    return (seq_ids, positions, owners)


def block_allowed(q_seq, q_pos, k_seq, k_pos):
    return (k_seq[None, :] == q_seq[:, None]) & (k_pos[None, :] <= q_pos[:, None])


def unchanged(state_in):
    return state_in


def attend_block(state_in, query_block_slice, key_blk, value_blk, allowed, factor):
    top_old, total_old, accum_old = state_in
    scores = (
        jnp.einsum("qkgd,pkd->kgqp", query_block_slice, key_blk, preferred_element_type=jnp.float32)
        * factor
    )
    scores = jnp.where(allowed, scores, neg_big)
    top_new = jnp.maximum(top_old, jnp.max(scores, axis=-1))
    weights_p = jnp.where(allowed, jnp.exp(scores - top_new[..., None]), 0.0)
    damping = jnp.exp(top_old - top_new)
    total_new = total_old * damping + jnp.sum(weights_p, axis=-1)
    accum_new = accum_old * damping[..., None] + jnp.einsum(
        "kgqp,pkd->kgqd",
        weights_p.astype(jnp.bfloat16),
        value_blk,
        preferred_element_type=jnp.float32,
    )
    return (top_new, total_new, accum_new)


def probs_grads(
    query_block_slice, dout_blk, lse_blk, delta_blk, key_blk, value_blk, allowed, factor
):
    scores = (
        jnp.einsum("qkgd,pkd->kgqp", query_block_slice, key_blk, preferred_element_type=jnp.float32)
        * factor
    )
    weights_p = jnp.where(allowed, jnp.exp(scores - lse_blk[..., None]), 0.0)
    dprobs = jnp.einsum("qkgd,pkd->kgqp", dout_blk, value_blk, preferred_element_type=jnp.float32)
    dscores = (weights_p * (dprobs - delta_blk[..., None])).astype(jnp.bfloat16)
    return (weights_p.astype(jnp.bfloat16), dscores)


def query_block_grad(
    acc_in, query_block_slice, dout_blk, lse_blk, delta_blk, key_blk, value_blk, allowed, factor
):
    weights_p, dscores = probs_grads(
        query_block_slice, dout_blk, lse_blk, delta_blk, key_blk, value_blk, allowed, factor
    )
    return (
        acc_in
        + jnp.einsum("kgqp,pkd->qkgd", dscores, key_blk, preferred_element_type=jnp.float32)
        * factor
    )


def key_block_grad(
    acc_in, query_block_slice, dout_blk, lse_blk, delta_blk, key_blk, value_blk, allowed, factor
):
    weights_p, dscores = probs_grads(
        query_block_slice, dout_blk, lse_blk, delta_blk, key_blk, value_blk, allowed, factor
    )
    key_grad = (
        jnp.einsum("kgqp,qkgd->pkd", dscores, query_block_slice, preferred_element_type=jnp.float32)
        * factor
    )
    value_grad = jnp.einsum(
        "kgqp,qkgd->pkd", weights_p, dout_blk, preferred_element_type=jnp.float32
    )
    return (acc_in[0] + key_grad, acc_in[1] + value_grad)


def local(
    hidden_in,
    gain_attn,
    gain_ffn,
    w_query,
    w_key,
    w_value,
    w_out,
    w_gate,
    w_up,
    w_down,
    qkv_shrink,
    query_expand,
    key_expand,
    value_expand,
    out_shrink,
    out_expand,
    gateup_shrink,
    gate_expand,
    up_expand,
    down_shrink,
    down_expand,
    lengths,
    adapter,
    packed_pos,
    cotangent,
):
    tok_rows = hidden_in.shape[0]
    head_count = lax.axis_size("head")
    blk_count = lax.axis_size("blk")
    head_at = lax.axis_index("head")
    blk_at = lax.axis_index("blk")
    q_width = query_expand.shape[1]
    kv_width = key_expand.shape[1]
    low_rank = out_shrink.shape[1]
    q_heads = q_width // HEAD_SIZE
    kv_heads = kv_width // HEAD_SIZE
    query_group_ratio = q_heads // kv_heads
    local_q = q_heads // head_count
    local_kv = kv_heads // head_count
    att_rows = head_count * tok_rows
    spans = 1
    factor = HEAD_SIZE ** (-0.5)
    seq_all, pos_all, owner_all = token_meta(lengths, adapter, packed_pos)
    first_mine = (head_at * blk_count + blk_at) * tok_rows
    pos_mine = lax.dynamic_slice_in_dim(pos_all, first_mine, tok_rows)
    owner_mine = lax.dynamic_slice_in_dim(owner_all, first_mine, tok_rows)
    cycle_seq = jnp.transpose(seq_all.reshape(head_count, blk_count, tok_rows), (1, 0, 2)).reshape(
        -1
    )
    cycle_pos = jnp.transpose(pos_all.reshape(head_count, blk_count, tok_rows), (1, 0, 2)).reshape(
        -1
    )
    seq_spans = lax.dynamic_slice_in_dim(cycle_seq, blk_at * att_rows, att_rows).reshape(
        spans, att_rows
    )
    pos_spans = lax.dynamic_slice_in_dim(cycle_pos, blk_at * att_rows, att_rows).reshape(
        spans, att_rows
    )
    columns = jnp.arange(low_rank, dtype=jnp.int32) // RANK
    select = (owner_mine[:, None] == columns[None, :]).astype(jnp.float32)
    select_two = jnp.tile(select, (1, 2))
    select_three = jnp.tile(select, (1, 3))
    cos_table, sin_table = rope_tables(pos_mine, HEAD_SIZE)
    inputs = hidden_in.astype(jnp.float32)
    scale_in = row_scale(inputs)
    normed = (inputs * scale_in * gain_attn).astype(jnp.bfloat16)
    query_weight, key_weight, value_weight, out_weight = (
        lax.all_gather(w_query, ("head", "blk"), axis=0, tiled=True),
        lax.all_gather(w_key, ("head", "blk"), axis=0, tiled=True),
        lax.all_gather(w_value, ("head", "blk"), axis=0, tiled=True),
        lax.all_gather(w_out, ("head", "blk"), axis=0, tiled=True),
    )
    low_qkv = (product(normed, qkv_shrink) * select_three).astype(jnp.bfloat16)
    query_lin = product(normed, query_weight) + product(low_qkv[:, :low_rank], query_expand)
    key_lin = product(normed, key_weight) + product(low_qkv[:, low_rank : 2 * low_rank], key_expand)
    value_lin = product(normed, value_weight) + product(low_qkv[:, 2 * low_rank :], value_expand)
    query_heads = query_lin.reshape(tok_rows, q_heads, HEAD_SIZE)
    key_heads = key_lin.reshape(tok_rows, kv_heads, HEAD_SIZE)
    query_rot = (query_heads * cos_table + rotate(query_heads) * sin_table).astype(jnp.bfloat16)
    key_rot = (key_heads * cos_table + rotate(key_heads) * sin_table).astype(jnp.bfloat16)
    value_cast = value_lin.reshape(tok_rows, kv_heads, HEAD_SIZE).astype(jnp.bfloat16)
    query_att, key_att, value_att = (
        lax.all_to_all(query_rot, "head", split_axis=1, concat_axis=0, tiled=True),
        lax.all_to_all(key_rot, "head", split_axis=1, concat_axis=0, tiled=True),
        lax.all_to_all(value_cast, "head", split_axis=1, concat_axis=0, tiled=True),
    )
    query_spans = query_att.reshape(spans, att_rows, local_kv, query_group_ratio, HEAD_SIZE)
    key_spans = key_att.reshape(spans, att_rows, local_kv, HEAD_SIZE)
    value_spans = value_att.reshape(spans, att_rows, local_kv, HEAD_SIZE)
    start_state = (
        jnp.full((spans, local_kv, query_group_ratio, att_rows), neg_big, jnp.float32),
        jnp.zeros((spans, local_kv, query_group_ratio, att_rows), jnp.float32),
        jnp.zeros((spans, local_kv, query_group_ratio, att_rows, HEAD_SIZE), jnp.float32),
    )
    key_piece = lax.all_gather(key_att, "blk", axis=0, tiled=True)
    value_piece = lax.all_gather(value_att, "blk", axis=0, tiled=True)
    length = key_piece.shape[0]
    stride = math.gcd(length, 512)

    def attend_over_blocks(k_index, loop_state):
        top_all, total_all, accum_all = loop_state
        offset = k_index * stride
        key_blk = lax.dynamic_slice_in_dim(key_piece, offset, stride, 0)
        value_blk = lax.dynamic_slice_in_dim(value_piece, offset, stride, 0)
        seq_blk = lax.dynamic_slice_in_dim(cycle_seq, offset, stride)
        pos_blk = lax.dynamic_slice_in_dim(cycle_pos, offset, stride)
        allowed = block_allowed(seq_spans[0], pos_spans[0], seq_blk, pos_blk)
        updated = lax.cond(
            jnp.any(allowed),
            partial(
                attend_block,
                query_block_slice=query_spans[0],
                key_blk=key_blk,
                value_blk=value_blk,
                allowed=allowed,
                factor=factor,
            ),
            unchanged,
            (top_all[0], total_all[0], accum_all[0]),
        )
        top_all = top_all.at[0].set(updated[0])
        total_all = total_all.at[0].set(updated[1])
        accum_all = accum_all.at[0].set(updated[2])
        return (top_all, total_all, accum_all)

    top_all, total_all, accum_all = lax.fori_loop(
        0, length // stride, attend_over_blocks, start_state
    )
    mixed_f = jnp.transpose(accum_all / total_all[..., None], (0, 3, 1, 2, 4))
    lse_spans = top_all + jnp.log(total_all)
    mixed_att = mixed_f.reshape(att_rows, local_q, HEAD_SIZE).astype(jnp.bfloat16)
    mixed_tok = lax.all_to_all(mixed_att, "head", split_axis=0, concat_axis=1, tiled=True).reshape(
        tok_rows, q_width
    )
    low_out = (product(mixed_tok, out_shrink) * select).astype(jnp.bfloat16)
    middle = inputs + product(mixed_tok, out_weight) + product(low_out, out_expand)
    scale_mid = row_scale(middle)
    normed_mid = (middle * scale_mid * gain_ffn).astype(jnp.bfloat16)
    low_gu = (product(normed_mid, gateup_shrink) * select_two).astype(jnp.bfloat16)
    pieces = (
        lax.all_gather(w_gate, ("head", "blk"), axis=0, tiled=True),
        lax.all_gather(w_up, ("head", "blk"), axis=0, tiled=True),
    )
    columns_in = normed_mid
    gate_pre = product(low_gu[:, :low_rank], gate_expand) + product(columns_in, pieces[0])
    up_pre = product(low_gu[:, low_rank:], up_expand) + product(columns_in, pieces[1])
    sigmoid_g = jax.nn.sigmoid(gate_pre)
    silu_gate = gate_pre * sigmoid_g
    active = (silu_gate * up_pre).astype(jnp.bfloat16)
    low_down = (product(active, down_shrink) * select).astype(jnp.bfloat16)
    columns_in = active
    ffn_result = product(low_down, down_expand) + product(
        columns_in, lax.all_gather(w_down, ("head", "blk"), axis=0, tiled=True)
    )
    output = (middle + ffn_result).astype(jnp.bfloat16)
    grad_low_down = (times_transposed(cotangent, down_expand) * select).astype(jnp.bfloat16)
    grad_down_expand = inner_rows(low_down, cotangent)
    grad_down_shrink = inner_rows(active, grad_low_down)
    grad_active = times_transposed(
        cotangent, lax.all_gather(w_down, ("head", "blk"), axis=0, tiled=True)
    ) + times_transposed(grad_low_down, down_shrink)
    grad_gate = (grad_active * up_pre * sigmoid_g * (1.0 + gate_pre * (1.0 - sigmoid_g))).astype(
        jnp.bfloat16
    )
    grad_up = (grad_active * silu_gate).astype(jnp.bfloat16)
    grad_low_gu = (
        jnp.concatenate(
            [times_transposed(grad_gate, gate_expand), times_transposed(grad_up, up_expand)], axis=1
        )
        * select_two
    ).astype(jnp.bfloat16)
    grad_gate_expand = inner_rows(low_gu[:, :low_rank], grad_gate)
    grad_up_expand = inner_rows(low_gu[:, low_rank:], grad_up)
    grad_gateup_shrink = inner_rows(normed_mid, grad_low_gu)
    pieces = lax.all_gather((w_gate, w_up), ("head", "blk"), axis=0, tiled=True)
    grad_normed_mid = (
        times_transposed(grad_gate, pieces[0])
        + times_transposed(grad_up, pieces[1])
        + times_transposed(grad_low_gu, gateup_shrink)
    )
    grad_middle = cotangent.astype(jnp.float32) + norm_back(
        middle, scale_mid, gain_ffn, grad_normed_mid
    )
    grad_attn_out = grad_middle.astype(jnp.bfloat16)
    grad_low_out = (times_transposed(grad_attn_out, out_expand) * select).astype(jnp.bfloat16)
    grad_out_expand = inner_rows(low_out, grad_attn_out)
    grad_out_shrink = inner_rows(mixed_tok, grad_low_out)
    grad_mixed = (
        times_transposed(grad_attn_out, out_weight) + times_transposed(grad_low_out, out_shrink)
    ).astype(jnp.bfloat16)
    grad_mixed_att = lax.all_to_all(
        grad_mixed.reshape(tok_rows, q_heads, HEAD_SIZE),
        "head",
        split_axis=1,
        concat_axis=0,
        tiled=True,
    )
    dout_spans = grad_mixed_att.reshape(spans, att_rows, local_kv, query_group_ratio, HEAD_SIZE)
    delta_spans = jnp.einsum("cqkgd,cqkgd->ckgq", dout_spans.astype(jnp.float32), mixed_f)
    zero_queries = jnp.zeros((spans, att_rows, local_kv, query_group_ratio, HEAD_SIZE), jnp.float32)
    zero_keys = jnp.zeros((spans, att_rows, local_kv, HEAD_SIZE), jnp.float32)
    lse_rows = jnp.transpose(lse_spans, (0, 3, 1, 2)).reshape(att_rows, local_q)
    delta_rows = jnp.transpose(delta_spans, (0, 3, 1, 2)).reshape(att_rows, local_q)
    lse_cycle, delta_cycle = (
        lax.all_gather(lse_rows, "blk", axis=0, tiled=True),
        lax.all_gather(delta_rows, "blk", axis=0, tiled=True),
    )
    pieces = (
        lax.all_gather(key_att, "blk", axis=0, tiled=True),
        lax.all_gather(value_att, "blk", axis=0, tiled=True),
        lax.all_gather(query_att, "blk", axis=0, tiled=True),
        lax.all_gather(grad_mixed_att, "blk", axis=0, tiled=True),
    )
    length = pieces[0].shape[0]
    grad_stride = math.gcd(length, 512)
    grad_key_piece = pieces[0]
    grad_value_piece = pieces[1]
    query_piece = pieces[2].reshape(length, local_kv, query_group_ratio, HEAD_SIZE)
    dout_piece = pieces[3].reshape(length, local_kv, query_group_ratio, HEAD_SIZE)

    def grad_over_blocks(k_index, loop_state):
        dq_all, dk_all, dv_all = loop_state
        offset = k_index * grad_stride
        key_blk = lax.dynamic_slice_in_dim(grad_key_piece, offset, grad_stride, 0)
        value_blk = lax.dynamic_slice_in_dim(grad_value_piece, offset, grad_stride, 0)
        query_block_slice = lax.dynamic_slice_in_dim(query_piece, offset, grad_stride, 0)
        dout_blk = lax.dynamic_slice_in_dim(dout_piece, offset, grad_stride, 0)
        lse_blk = jnp.transpose(
            lax.dynamic_slice_in_dim(lse_cycle, offset, grad_stride, 0).reshape(
                grad_stride, local_kv, query_group_ratio
            ),
            (1, 2, 0),
        )
        delta_blk = jnp.transpose(
            lax.dynamic_slice_in_dim(delta_cycle, offset, grad_stride, 0).reshape(
                grad_stride, local_kv, query_group_ratio
            ),
            (1, 2, 0),
        )
        seq_blk = lax.dynamic_slice_in_dim(cycle_seq, offset, grad_stride)
        pos_blk = lax.dynamic_slice_in_dim(cycle_pos, offset, grad_stride)
        allowed_here = block_allowed(seq_spans[0], pos_spans[0], seq_blk, pos_blk)
        renewed = lax.cond(
            jnp.any(allowed_here),
            partial(
                query_block_grad,
                query_block_slice=query_spans[0],
                dout_blk=dout_spans[0],
                lse_blk=lse_spans[0],
                delta_blk=delta_spans[0],
                key_blk=key_blk,
                value_blk=value_blk,
                allowed=allowed_here,
                factor=factor,
            ),
            unchanged,
            dq_all[0],
        )
        dq_all = dq_all.at[0].set(renewed)
        allowed_there = block_allowed(seq_blk, pos_blk, seq_spans[0], pos_spans[0])
        key_pair = lax.cond(
            jnp.any(allowed_there),
            partial(
                key_block_grad,
                query_block_slice=query_block_slice,
                dout_blk=dout_blk,
                lse_blk=lse_blk,
                delta_blk=delta_blk,
                key_blk=key_spans[0],
                value_blk=value_spans[0],
                allowed=allowed_there,
                factor=factor,
            ),
            unchanged,
            (dk_all[0], dv_all[0]),
        )
        dk_all = dk_all.at[0].set(key_pair[0])
        dv_all = dv_all.at[0].set(key_pair[1])
        return (dq_all, dk_all, dv_all)

    dq_spans, dk_spans, dv_spans = lax.fori_loop(
        0, length // grad_stride, grad_over_blocks, (zero_queries, zero_keys, zero_keys)
    )
    dk_rows = dk_spans.reshape(att_rows, local_kv, HEAD_SIZE)
    dv_rows = dv_spans.reshape(att_rows, local_kv, HEAD_SIZE)
    dq_att = dq_spans.reshape(att_rows, local_q, HEAD_SIZE).astype(jnp.bfloat16)
    query_back, key_back, value_back = (
        lax.all_to_all(dq_att, "head", split_axis=0, concat_axis=1, tiled=True),
        lax.all_to_all(
            dk_rows.astype(jnp.bfloat16), "head", split_axis=0, concat_axis=1, tiled=True
        ),
        lax.all_to_all(
            dv_rows.astype(jnp.bfloat16), "head", split_axis=0, concat_axis=1, tiled=True
        ),
    )
    query_back = query_back.astype(jnp.float32)
    key_back = key_back.astype(jnp.float32)
    grad_query = (
        (query_back * cos_table - rotate(query_back * sin_table))
        .astype(jnp.bfloat16)
        .reshape(tok_rows, q_width)
    )
    grad_key = (
        (key_back * cos_table - rotate(key_back * sin_table))
        .astype(jnp.bfloat16)
        .reshape(tok_rows, kv_width)
    )
    grad_value = value_back.reshape(tok_rows, kv_width)
    grad_low_qkv = (
        jnp.concatenate(
            [
                times_transposed(grad_query, query_expand),
                times_transposed(grad_key, key_expand),
                times_transposed(grad_value, value_expand),
            ],
            axis=1,
        )
        * select_three
    ).astype(jnp.bfloat16)
    grad_query_expand = inner_rows(low_qkv[:, :low_rank], grad_query)
    grad_key_expand = inner_rows(low_qkv[:, low_rank : 2 * low_rank], grad_key)
    grad_value_expand = inner_rows(low_qkv[:, 2 * low_rank :], grad_value)
    grad_qkv_shrink = inner_rows(normed, grad_low_qkv)
    grad_normed = (
        times_transposed(grad_query, query_weight)
        + times_transposed(grad_key, key_weight)
        + times_transposed(grad_value, value_weight)
        + times_transposed(grad_low_qkv, qkv_shrink)
    )
    grad_input = (grad_middle + norm_back(inputs, scale_in, gain_attn, grad_normed)).astype(
        jnp.bfloat16
    )
    summed = lax.psum(
        (
            grad_qkv_shrink,
            grad_query_expand,
            grad_key_expand,
            grad_value_expand,
            grad_out_shrink,
            grad_out_expand,
            grad_gateup_shrink,
            grad_gate_expand,
            grad_up_expand,
            grad_down_shrink,
            grad_down_expand,
        ),
        ("head", "blk"),
    )
    return (output, grad_input) + tuple(summed)


def solution(mesh):
    placed = (
        P(("head", "blk"), None),
        P(),
        P(),
        P(("head", "blk"), None),
        P(("head", "blk"), None),
        P(("head", "blk"), None),
        P(("head", "blk"), None),
        P(("head", "blk"), None),
        P(("head", "blk"), None),
        P(("head", "blk"), None),
        P(),
        P(),
        P(),
        P(),
        P(),
        P(),
        P(),
        P(),
        P(),
        P(),
        P(),
        P(),
        P(),
        P(),
        P(("head", "blk"), None),
    )
    return jax.shard_map(
        local,
        mesh=mesh,
        in_specs=placed,
        out_specs=(
            P(("head", "blk"), None),
            P(("head", "blk"), None),
            P(),
            P(),
            P(),
            P(),
            P(),
            P(),
            P(),
            P(),
            P(),
            P(),
            P(),
        ),
        check_vma=False,
    )
```

profile of v0, /device:TPU:1, one launch (start us, length us, event | category | flops | bytes accessed | tf_op | source)
XLA Modules:
  0.0 2189.8 jit_solution(7732887335191214580)
XLA Ops:
  21.8 59.9 %all-gather.12.cloned.1.call-done = bf16[2048,1024]{1,0:T(8,128)(2,1)} async-done(((bf16[16,1024]{1,0:T(8,128)(2,1)}), bf16[2048,1024]{1,0:T(8,128)(2,1)}) %all-gather.12.cloned.1.call-update) | async-done | bytes 4194320 | tf_op jit(solution)/shard_map/all_gather | solution.py:210
  85.6 8.9 all_to_all.120
  96.5 52.6 %all-gather.18.cloned.1.call-done = bf16[2048,1024]{1,0:T(8,128)(2,1)} async-done(((bf16[16,1024]{1,0:T(8,128)(2,1)}), bf16[2048,1024]{1,0:T(8,128)(2,1)}) %all-gather.18.cloned.1.call-update) | async-done | bytes 4194320 | tf_op jit(solution)/shard_map/all_gather | solution.py:211
  152.1 8.9 all_to_all.121
  164.7 55.1 %all-gather.16.cloned.1.call-done = bf16[2048,2048]{1,0:T(8,128)(2,1)} async-done(((bf16[16,2048]{1,0:T(8,128)(2,1)}), bf16[2048,2048]{1,0:T(8,128)(2,1)}) %all-gather.16.cloned.1.call-update) | async-done | bytes 8388624 | tf_op jit(solution)/shard_map/all_gather | solution.py:209
  232.8 17.6 all_to_all.122
  254.2 90.9 %all-gather.14.cloned.1.call-done = bf16[16384,2,256]{2,0,1:T(8,128)(2,1)} async-done(((bf16[256,2,256]{2,0,1:T(8,128)(2,1)}), bf16[16384,2,256]{2,0,1:T(8,128)(2,1)}) %all-gather.14.cloned.1.call-update) | async-done | bytes 16777232 | tf_op jit(solution)/shard_map/all_gather | solution.py:236
  345.1 124.8 %all-gather.20.cloned.1.call-done = bf16[16384,2,256]{2,0,1:T(8,128)(2,1)} async-done(((bf16[256,2,256]{2,0,1:T(8,128)(2,1)}), bf16[16384,2,256]{2,0,1:T(8,128)(2,1)}) %all-gather.20.cloned.1.call-update) | async-done | bytes 16777232 | tf_op jit(solution)/shard_map/all_gather | solution.py:237
  471.5 187.6 %while.46 = (s32[]{:T(128)}, f32[1,2,2,256]{3,2,1,0:T(2,128)}, f32[1,2,2,256]{3,2,1,0:T(2,128)S(1)}, f32[1,2,2,256,256]{4,3,2,1,0:T(8,128)}, s32[16384]{0:T(1024...) while((s32[]{:T(128)}, f32[1,2,2,256]{3,2,1,0:T(2,128)}, ...), condition=%wide.region_11.12_spmd, body=%wide.region_5.11_spmd.sunk | while | flops 544737280 | bytes 18955632 | solution.py:267
  475.2 7.6 conditional.6
  572.2 7.6 conditional.6
  583.5 7.6 conditional.6
  594.7 7.8 conditional.6
  606.2 7.7 conditional.6
  617.5 7.7 conditional.6
  628.9 7.7 conditional.6
  640.3 7.6 conditional.6
  651.5 7.6 conditional.6
  667.8 9.4 all-to-all-done.3
  689.1 13.6 fusion.130
  705.4 57.7 %all-gather.24.cloned.1.call-done = bf16[2048,8192]{1,0:T(8,128)(2,1)} async-done(((bf16[16,8192]{1,0:T(8,128)(2,1)}), bf16[2048,8192]{1,0:T(8,128)(2,1)}) %all-gather.24.cloned.1.call-update) | async-done | bytes 33554448 | tf_op jit(solution)/shard_map/all_gather | solution.py:282
  763.1 13.1 fusion.129
  778.9 99.4 %all-gather.28.cloned.1.call-done = bf16[8192,2048]{1,0:T(8,128)(2,1)} async-done(((bf16[64,2048]{1,0:T(8,128)(2,1)}), bf16[8192,2048]{1,0:T(8,128)(2,1)}) %all-gather.28.cloned.1.call-update) | async-done | bytes 33554448 | tf_op jit(solution)/shard_map/all_gather | solution.py:294
  878.3 17.7 fusion.132
  896.0 7.2 multiply_convert_fusion
  907.2 25.7 %fusion.133 = f32[128,2048]{1,0:T(8,128)} fusion(bf16[128,8192]{1,0:T(8,128)(2,1)S(1)} %get-tuple-element.1422, bf16[2048,8192]{1,0:T(8,128)(2,1)} %all-gather.24.cloned.1.call-done), kind=kOutput, calls=%fused_computation.218 | convolution fusion | flops 4294967296 | bytes 36700160 | tf_op jit(solution)/shard_map/dot_general | solution.py:23
  932.9 17.7 convolution_add_fusion.12
  961.1 18.0 all_to_all.123
  981.9 100.3 %all_gather.53 = f32[16384,4]{0,1:T(4,128)} all-gather(f32[256,4]{0,1:T(4,128)S(1)} %reshape.744), channel_id=1, replica_groups=mesh['head'=2,'blk'=64] {'blk'}, dimensions={0}, use_global_device_ids=true | all-gather | bytes 266240 | tf_op jit(solution)/shard_map/all_gather | solution.py:346
  1099.1 83.3 %all_gather.54 = f32[16384,4]{0,1:T(4,128)} all-gather(f32[256,4]{0,1:T(4,128)S(1)} %reshape.745), channel_id=1, replica_groups=mesh['head'=2,'blk'=64] {'blk'}, dimensions={0}, use_global_device_ids=true | all-gather | bytes 266240 | tf_op jit(solution)/shard_map/all_gather | solution.py:347
  1182.4 84.1 %all-gather.32.cloned.1.call-done = bf16[16384,4,256]{2,0,1:T(8,128)(2,1)} async-done(((bf16[256,4,256]{2,0,1:T(8,128)(2,1)}), bf16[16384,4,256]{2,0,1:T(8,128)(2,1)}) %all-gather.32.cloned.1.call-update) | async-done | bytes 33554448 | tf_op jit(solution)/shard_map/all_gather | solution.py:353
  1268.5 487.8 %while.47 = (s32[]{:T(128)}, f32[1,256,2,2,256]{4,1,3,2,0:T(8,128)}, f32[1,256,2,256]{3,1,2,0:T(8,128)S(1)}, f32[1,256,2,256]{3,1,2,0:T(8,128)}, s32[16384]{0:T(...) while((s32[]{:T(128)}, ...), condition=%wide.region_21.22_spmd, body=%wide.region_14.21_spmd.sunk | while | flops 1887830016 | bytes 22675548 | solution.py:422
  1272.9 7.2 conditional.8
  1292.0 7.2 conditional.8
  1306.4 7.2 conditional.8
  1320.7 7.2 conditional.8
  1335.0 7.2 conditional.8
  1349.3 7.2 conditional.8
  1363.7 7.2 conditional.8
  1378.0 7.2 conditional.8
  1392.3 7.2 conditional.8
  1406.7 7.2 conditional.8
  1421.0 7.2 conditional.8
  1435.3 7.2 conditional.8
  1449.7 7.2 conditional.8
  1464.0 7.2 conditional.8
  1478.3 7.2 conditional.8
  1492.6 7.2 conditional.8
  1507.0 7.2 conditional.8
  1521.3 7.2 conditional.8
  1535.6 7.2 conditional.8
  1550.0 7.2 conditional.8
  1564.3 7.2 conditional.8
  1578.6 7.2 conditional.8
  1593.0 7.2 conditional.8
  1607.3 7.2 conditional.8
  1621.6 7.2 conditional.8
  1640.8 7.2 conditional.8
  1659.9 7.2 conditional.8
  1679.1 7.2 conditional.8
  1698.3 7.2 conditional.8
  1717.4 7.2 conditional.8
  1800.5 13.0 fusion.131
  1827.4 332.1 %all-reduce.3.cloned.1.call-done = (f32[2048,384]{1,0:T(8,128)}, f32[128,2048]{1,0:T(8,128)}, f32[128,1024]{1,0:T(8,128)}, f32[128,1024]{1,0:T(8,128)}, f32[2048...) async-done(((f32[2048,384]{1,0:T(8,128)}, ...) | async-done | bytes 23068688 | tf_op jit(solution)/shard_map/psum | solution.py:474
  (1188 shorter events, 847.2 us)
Async XLA Ops:
  7.2 888.8 %copy-start = (bf16[8192,128]{1,0:T(8,128)(2,1)S(1)}, bf16[8192,128]{1,0:T(8,128)(2,1)}, u32[]{:S(2)}) copy-start(bf16[8192,128]{1,0:T(8,128)(2,1)} %param.66) | copy-start | bytes 6291460
  7.2 10.1 copy-start.2
  7.2 10.9 copy-start.64
  7.2 74.5 %all-gather.12.cloned.1.call-start = ((), (), s32[]{:S(2)}) async-start(), calls=%async_computation.8 | async-start | bytes 4227072 | tf_op jit(solution)/shard_map/all_gather | solution.py:210
  8.0 141.2 %all-gather.18.cloned.1.call-start = ((), (), s32[]{:S(2)}) async-start(), calls=%async_computation.11 | async-start | bytes 4227072 | tf_op jit(solution)/shard_map/all_gather | solution.py:211
  8.7 211.1 %all-gather.16.cloned.1.call-start = ((), (), s32[]{:S(2)}) async-start(), calls=%async_computation.10 | async-start | bytes 8454144 | tf_op jit(solution)/shard_map/all_gather | solution.py:209
  9.4 335.6 %all-gather.14.cloned.1.call-start = ((), (), s32[]{:S(2)}) async-start(), calls=%async_computation.9 | async-start | bytes 17039360 | tf_op jit(solution)/shard_map/all_gather | solution.py:236
  16.4 214.0 %copy-start.39 = (f32[128,256]{0,1:T(8,128)}, f32[128,256]{0,1:T(8,128)S(1)}, u32[]{:S(2)}) copy-start(f32[128,256]{0,1:T(8,128)S(1)} %pad_maximum_fusion.2) | copy-start | bytes 393220
  17.1 213.3 %copy-start.42 = (f32[128,256]{0,1:T(8,128)}, f32[128,256]{0,1:T(8,128)S(1)}, u32[]{:S(2)}) copy-start(f32[128,256]{0,1:T(8,128)S(1)} %pad_maximum_fusion.3) | copy-start | bytes 393220
  17.3 67.5 %copy-start.50 = (f32[128,256]{1,0:T(8,128)}, f32[128,256]{1,0:T(8,128)S(1)}, u32[]{:S(2)}) copy-start(f32[128,256]{1,0:T(8,128)S(1)} %copy.296) | copy-start | bytes 393220
  18.1 201.7 %copy-start.82 = (f32[128]{0:T(128)}, f32[128]{0:T(128)S(1)}, u32[]{:S(2)}) copy-start(f32[128]{0:T(128)S(1)} %get-tuple-element.1435) | copy-start | bytes 1540
  95.3 374.6 %all-gather.20.cloned.1.call-start = ((), (), s32[]{:S(2)}) async-start(), calls=%async_computation.12 | async-start | bytes 17039360 | tf_op jit(solution)/shard_map/all_gather | solution.py:237
  161.8 520.2 %all-gather.22.cloned.1.call-start = ((), (), s32[]{:S(2)}) async-start(), calls=%async_computation.13 | async-start | bytes 8454144 | tf_op jit(solution)/shard_map/all_gather | solution.py:212
  162.4 526.7 %all-gather.26.cloned.1.call-start = ((), (), s32[]{:S(2)}) async-start(), calls=%async_computation.15 | async-start | bytes 33816576 | tf_op jit(solution)/shard_map/all_gather | solution.py:283
  163.1 599.9 %all-gather.24.cloned.1.call-start = ((), (), s32[]{:S(2)}) async-start(), calls=%async_computation.14 | async-start | bytes 33816576 | tf_op jit(solution)/shard_map/all_gather | solution.py:282
  163.9 714.4 %all-gather.28.cloned.1.call-start = ((), (), s32[]{:S(2)}) async-start(), calls=%async_computation.16 | async-start | bytes 33816576 | tf_op jit(solution)/shard_map/all_gather | solution.py:294
  164.6 59.9 %copy-start.46 = (bf16[128,2048]{1,0:T(8,128)(2,1)S(1)}, bf16[128,2048]{1,0:T(8,128)(2,1)}, u32[]{:S(2)}) copy-start(bf16[128,2048]{1,0:T(8,128)(2,1)} %param.58) | copy-start | bytes 1572868
  164.6 1017.8 %all-gather.30.cloned.1.call-start = ((), (), s32[]{:S(2)}) async-start(), calls=%async_computation.17 | async-start | bytes 34078720 | tf_op jit(solution)/shard_map/all_gather | solution.py:352
  231.5 19.8 copy-start.75
  231.5 20.5 copy-start.78
  659.1 7.2 copy-start.23
  659.1 7.2 copy-start.85
  661.8 15.3 all-to-all-start.3
  666.1 600.5 %all-gather.32.cloned.1.call-start = ((), (), s32[]{:S(2)}) async-start(), calls=%async_computation.18 | async-start | bytes 34078720 | tf_op jit(solution)/shard_map/all_gather | solution.py:353
  667.7 228.3 %copy-start.79 = (bf16[128,128]{1,0:T(8,128)(2,1)}, bf16[128,128]{1,0:T(8,128)(2,1)S(1)}, u32[]{:S(2)}) copy-start(bf16[128,128]{1,0:T(8,128)(2,1)S(1)} %fusion.78) | copy-start | bytes 98308
  680.3 6.7 copy-start.18
  689.0 13.6 copy-start.28
  763.1 13.1 copy-start.26
  896.0 7.3 copy-start.27
  903.3 29.6 %copy-start.13 = (bf16[128,8192]{1,0:T(8,128)(2,1)}, bf16[128,8192]{1,0:T(8,128)(2,1)S(1)}, u32[]{:S(2)}) copy-start(bf16[128,8192]{1,0:T(8,128)(2,1)S(1)} %get-tuple-element.1421) | copy-start | bytes 6291460
  932.9 17.7 copy-start.6
  953.9 6.9 copy-start.8
  954.2 6.6 copy-start.45
  981.9 102.6 %copy-start.9 = (f32[128,2048]{1,0:T(8,128)S(1)}, f32[128,2048]{1,0:T(8,128)}, u32[]{:S(2)}) copy-start(f32[128,2048]{1,0:T(8,128)} %copy-done.8) | copy-start | bytes 3145732
  1097.4 171.1 %copy-start.17 = (bf16[2,128,2,256]{3,1,0,2:T(8,128)(2,1)S(1)}, bf16[2,128,2,256]{3,1,0,2:T(8,128)(2,1)}, u32[]{:S(2)}) copy-start(bf16[2,128,2,256]{3,1,0,2:T(8,128)(2,1)} %copy.304) | copy-start | bytes 786436
  1282.2 5.5 copy-start.71
  1282.2 5.5 copy-start.73
  1630.9 5.5 copy-start.71
  1630.9 5.5 copy-start.73
  1650.1 5.5 copy-start.71
  1650.1 5.5 copy-start.73
  1669.2 5.5 copy-start.71
  1669.3 5.5 copy-start.73
  1688.4 5.5 copy-start.71
  1688.4 5.5 copy-start.73
  1707.6 5.5 copy-start.71
  1707.6 5.5 copy-start.73
  1726.8 5.5 copy-start.71
  1726.8 5.5 copy-start.73
  1738.8 5.5 copy-start.71
  1738.8 5.5 copy-start.73
  1750.8 5.5 copy-start.71
  1756.3 7.0 copy-start.38
  1757.4 10.1 all-to-all-start.6
  1767.5 9.7 all-to-all-start.7
  1772.9 11.2 copy-start.33
  1772.9 9.2 copy-start.53
  1777.2 10.4 all-to-all-start.5
  1780.7 378.8 %all-reduce.3.cloned.1.call-start = ((), (), s32[]{:S(2)}) async-start(), calls=%async_computation.19 | async-start | bytes 46137344 | tf_op jit(solution)/shard_map/psum | solution.py:474
  1800.5 13.0 copy-start.7
  1800.5 13.0 copy-start.41
  1800.5 13.0 copy-start.69
  1814.7 6.5 copy-start.15
  1814.7 6.5 copy-start.34
  (179 other events, 437.3 us)
Sparse Core Ops, SparseCore 0:
  11.2 70.4 all-gather.11
  84.8 64.3 all-gather.17
  152.1 67.5 all-gather.15
  221.9 123.0 all-gather.13
  347.2 122.6 all-gather.19
  472.7 69.5 all-gather.21
  545.3 104.2 all-gather.25
  652.6 110.3 all-gather.23
  766.1 112.1 all-gather.27
  880.4 198.8 all-gather.29
  1081.7 184.8 all-gather.31
  1799.1 360.3 all-reduce.2
where the time goes:
time: 2220 us; the launch traced here: 2190 us
  waiting for transfers between devices  978 us (44%)
  matrix products  486 us (22%)
  local copies, waits for them, and re-layouts  249 us (11%)
  blocking collectives  237 us (11%)
  other arithmetic  142 us (6%)
  loops' own time  65.6 us (3%)
    psum x1, waiting for transfers between devices, local(): lax.psum((grad_qkv_shrink, grad_query_expand, grad_key_expand, grad_value...  332 us
    all_gather x1, waiting for transfers between devices, local(): value_piece = lax.all_gather(value_att, 'blk', axis=0, tiled=True)  125 us
    all_gather x1, blocking collectives, local(): lax.all_gather(lse_rows, 'blk', axis=0, tiled=True)  100 us
    all_gather x1, waiting for transfers between devices, local(): lax.all_gather(w_down, ('head', 'blk'), axis=0, tiled=True)  99.4 us
    dot_general x18, matrix products, times_transposed(): lax.dot_general(left, right, (((1,), (1,)), ((), ())), preferred_element_...  92.8 us
    all_gather x1, waiting for transfers between devices, local(): key_piece = lax.all_gather(key_att, 'blk', axis=0, tiled=True)  90.9 us
    all_gather x1, waiting for transfers between devices, local(): lax.all_gather(grad_mixed_att, 'blk', axis=0, tiled=True)  84.1 us
    all_gather x1, blocking collectives, local(): lax.all_gather(delta_rows, 'blk', axis=0, tiled=True)  83.3 us
  transfers between devices with their start and end apart: 16, of which 13 were waited for; matrix products, arithmetic and copies ran while one was open for 17% of the time, Pallas kernels for 0%

commit v1 on v0

v1 whole, which is shorter than its diff:
```python
from functools import partial

import jax
import jax.numpy as jnp
from jax import lax
from jax.experimental import pallas as pl
from jax.experimental.pallas import tpu as pltpu
from jax.sharding import Mesh, PartitionSpec as P

HEAD_SIZE = 256
RANK = 16
HALF = 64
GROUP = 512

ALL = ("zh", "zl", "x", "y", "c")
PLANE = ("zh", "zl", "x")

norm_eps = 1e-06
rope_theta = 1000042.0
neg_big = -1e30
far = 1 << 30

f32 = jnp.float32
bf16 = jnp.bfloat16


def product(left, right):
    return jnp.dot(left, right, preferred_element_type=f32)


def times_transposed(left, right):
    return lax.dot_general(left, right, (((1,), (1,)), ((), ())), preferred_element_type=f32)


def inner_rows(left, right):
    return lax.dot_general(left, right, (((0,), (0,)), ((), ())), preferred_element_type=f32)


def row_scale(value_matrix):
    return lax.rsqrt(jnp.mean(value_matrix * value_matrix, axis=-1, keepdims=True) + norm_eps)


def norm_back(value_matrix, scale, gain, grad):
    scaled = gain * grad
    return scale * scaled - value_matrix * (scale * scale * scale) * jnp.mean(
        value_matrix * scaled, axis=-1, keepdims=True
    )


def rotate(value_matrix):
    middle = value_matrix.shape[-1] // 2
    return jnp.concatenate([-value_matrix[..., middle:], value_matrix[..., :middle]], axis=-1)


def rope_tables(positions, width):
    middle = width // 2
    inverse = rope_theta ** (-(jnp.arange(middle, dtype=f32) * 2.0) / width)
    angles = positions.astype(f32)[:, None] * inverse[None, :]
    cos_half, sin_half = jnp.cos(angles), jnp.sin(angles)
    cos_table = jnp.concatenate([cos_half, cos_half], axis=-1)[:, None, :]
    sin_table = jnp.concatenate([sin_half, sin_half], axis=-1)[:, None, :]
    return (cos_table, sin_table)


def swap_cores(value):
    return lax.ppermute(value, "c", [(0, 1), (1, 0)])


def shift_y(value, step):
    return lax.ppermute(value, "y", [(i, (i + step) % 4) for i in range(4)])


def gather_y(value):
    return lax.all_gather(value, "y", axis=0, tiled=True)


def sum_y(blocks_of, y):
    total = blocks_of(y).astype(f32)
    for step in (2, 1, 3):
        total = total + shift_y(blocks_of((y + step) % 4), step).astype(f32)
    return total


def allowed_mask(own_pos, own_start, key_pos):
    return (key_pos <= own_pos) & (key_pos >= own_start)


def attend_kernel(
    active, place, q_ref, pos_ref, start_ref, kpos_ref, prev_ref, own_ref, mixed_ref, lse_ref, top, total, accum
):
    step = pl.program_id(0)

    @pl.when(step == 0)
    def _():
        top[...] = jnp.full(top.shape, neg_big, f32)
        total[...] = jnp.zeros(total.shape, f32)
        accum[...] = jnp.zeros(accum.shape, f32)

    for side, kv_ref in ((0, prev_ref), (1, own_ref)):

        @pl.when(active[side * 8 + step] != 0)
        def _():
            key = kv_ref[0, 0, :, :HEAD_SIZE]
            value = kv_ref[0, 0, :, HEAD_SIZE:]
            allowed = allowed_mask(pos_ref[...], start_ref[...], kpos_ref[0, side])
            for head in range(2):
                scores = times_transposed(q_ref[:, head * HEAD_SIZE : (head + 1) * HEAD_SIZE], key)
                scores = jnp.where(allowed, scores, neg_big)
                top_old = top[head]
                top_new = jnp.maximum(top_old, jnp.max(scores, axis=-1, keepdims=True))
                weights_p = jnp.where(allowed, jnp.exp(scores - top_new), 0.0)
                damping = jnp.exp(top_old - top_new)
                total[head] = total[head] * damping + jnp.sum(weights_p, axis=-1, keepdims=True)
                accum[head] = accum[head] * damping + product(weights_p.astype(bf16), value)
                top[head] = top_new

    @pl.when(step == 7)
    def _():
        for head in range(2):
            mixed_ref[:, head * HEAD_SIZE : (head + 1) * HEAD_SIZE] = accum[head] / total[head]
            lse_ref[head] = top[head] + jnp.log(total[head])


def attend_back_kernel(
    active,
    place,
    q_ref,
    pos_ref,
    start_ref,
    kpos_ref,
    prev_ref,
    own_ref,
    mixed_ref,
    lse_ref,
    dout_ref,
    dq_ref,
    dprev_ref,
    down_ref,
    delta,
):
    step = pl.program_id(0)

    @pl.when(step == 0)
    def _():
        dq_ref[...] = jnp.zeros(dq_ref.shape, f32)
        for head in range(2):
            cols = slice(head * HEAD_SIZE, (head + 1) * HEAD_SIZE)
            delta[head] = jnp.sum(dout_ref[:, cols].astype(f32) * mixed_ref[:, cols], axis=-1, keepdims=True)

    for side, kv_ref, dkv_ref in ((0, prev_ref, dprev_ref), (1, own_ref, down_ref)):

        @pl.when(active[side * 8 + step] == 0)
        def _():
            dkv_ref[...] = jnp.zeros(dkv_ref.shape, bf16)

        @pl.when(active[side * 8 + step] != 0)
        def _():
            key = kv_ref[0, 0, :, :HEAD_SIZE]
            value = kv_ref[0, 0, :, HEAD_SIZE:]
            allowed = allowed_mask(pos_ref[...], start_ref[...], kpos_ref[0, side])
            dk = jnp.zeros((GROUP, HEAD_SIZE), f32)
            dv = jnp.zeros((GROUP, HEAD_SIZE), f32)
            for head in range(2):
                cols = slice(head * HEAD_SIZE, (head + 1) * HEAD_SIZE)
                query, dout = q_ref[:, cols], dout_ref[:, cols]
                scores = times_transposed(query, key)
                weights_p = jnp.where(allowed, jnp.exp(scores - lse_ref[head]), 0.0)
                dprobs = times_transposed(dout, value)
                dscores = (weights_p * (dprobs - delta[head])).astype(bf16)
                dq_ref[:, cols] += product(dscores, key)
                dk = dk + inner_rows(dscores, query)
                dv = dv + inner_rows(weights_p.astype(bf16), dout)
            dkv_ref[0, :, :HEAD_SIZE] = dk.astype(bf16)
            dkv_ref[0, :, HEAD_SIZE:] = dv.astype(bf16)


def whole(shape):
    return pl.BlockSpec(shape, lambda i, *refs: (0,) * len(shape))


def key_specs():
    return [
        pl.BlockSpec((1, 2, 1, GROUP), lambda i, active, place: (i, 0, 0, 0)),
        pl.BlockSpec((1, 1, GROUP, GROUP), lambda i, active, place: (0, i, 0, 0)),
        pl.BlockSpec((1, 1, GROUP, GROUP), lambda i, active, place: (place[0], i, 0, 0)),
    ]


def attend(active, place, query, pos_col, start_col, key_pos, prev, family):
    return pl.pallas_call(
        attend_kernel,
        grid_spec=pltpu.PrefetchScalarGridSpec(
            num_scalar_prefetch=2,
            grid=(8,),
            in_specs=[whole((GROUP, GROUP)), whole((GROUP, 1)), whole((GROUP, 1))] + key_specs(),
            out_specs=[whole((GROUP, GROUP)), whole((2, GROUP, 1))],
            scratch_shapes=[
                pltpu.VMEM((2, GROUP, 1), f32),
                pltpu.VMEM((2, GROUP, 1), f32),
                pltpu.VMEM((2, GROUP, HEAD_SIZE), f32),
            ],
        ),
        out_shape=[
            jax.ShapeDtypeStruct((GROUP, GROUP), f32),
            jax.ShapeDtypeStruct((2, GROUP, 1), f32),
        ],
        compiler_params=pltpu.CompilerParams(vmem_limit_bytes=40 << 20),
        name="attend",
    )(active, place, query, pos_col, start_col, key_pos, prev, family)


def attend_back(active, place, query, pos_col, start_col, key_pos, prev, family, mixed, lse, dout):
    return pl.pallas_call(
        attend_back_kernel,
        grid_spec=pltpu.PrefetchScalarGridSpec(
            num_scalar_prefetch=2,
            grid=(8,),
            in_specs=[whole((GROUP, GROUP)), whole((GROUP, 1)), whole((GROUP, 1))]
            + key_specs()
            + [whole((GROUP, GROUP)), whole((2, GROUP, 1)), whole((GROUP, GROUP))],
            out_specs=[
                whole((GROUP, GROUP)),
                pl.BlockSpec((1, GROUP, GROUP), lambda i, active, place: (i, 0, 0)),
                pl.BlockSpec((1, GROUP, GROUP), lambda i, active, place: (i, 0, 0)),
            ],
            scratch_shapes=[pltpu.VMEM((2, GROUP, 1), f32)],
        ),
        out_shape=[
            jax.ShapeDtypeStruct((GROUP, GROUP), f32),
            jax.ShapeDtypeStruct((8, GROUP, GROUP), bf16),
            jax.ShapeDtypeStruct((8, GROUP, GROUP), bf16),
        ],
        compiler_params=pltpu.CompilerParams(vmem_limit_bytes=40 << 20),
        name="attend_back",
    )(active, place, query, pos_col, start_col, key_pos, prev, family, mixed, lse, dout)


def local(
    hidden_in,
    gain_attn,
    gain_ffn,
    w_query,
    w_key,
    w_value,
    w_out,
    w_gate,
    w_up,
    w_down,
    qkv_shrink,
    query_expand,
    key_expand,
    value_expand,
    out_shrink,
    out_expand,
    gateup_shrink,
    gate_expand,
    up_expand,
    down_shrink,
    down_expand,
    lengths,
    adapter,
    packed_pos,
    cotangent,
):
    zh, zl, x, y, c = (lax.axis_index(name) for name in ALL)
    row = 2 * zh + c
    block = 4 * zl + x
    mine, other = 2 * y + c, 2 * y + 1 - c
    factor = HEAD_SIZE ** (-0.5)
    rank = out_shrink.shape[1]

    def to_rows(value):
        own = lax.dynamic_slice_in_dim(value, c * HALF, HALF, 0)
        sent = lax.dynamic_slice_in_dim(value, (1 - c) * HALF, HALF, 0)
        return jnp.concatenate([own, swap_cores(sent)], axis=0)

    def from_rows(value):
        own, got = value[:HALF], swap_cores(value[HALF:])
        return jnp.where(c == 0, jnp.concatenate([own, got], 0), jnp.concatenate([got, own], 0))

    hidden = to_rows(hidden_in)
    cot = to_rows(cotangent)

    spread = packed_pos.reshape(2, 8, 4, 2, 2, HALF)
    spread = jnp.transpose(spread, (0, 4, 1, 2, 3, 5))
    rows_pos = jnp.stack([spread[:, 0], spread[:, 1, :, :, ::-1]], axis=1).reshape(4, 8, GROUP)
    own_row = lax.dynamic_index_in_dim(rows_pos, row, 0, keepdims=False)
    prev_row = lax.dynamic_index_in_dim(rows_pos, jnp.maximum(row - 1, 0), 0, keepdims=False)
    prev_row = jnp.where(row == 0, far, prev_row)
    key_pos = jnp.stack([prev_row, own_row], axis=1)
    group_pos = lax.dynamic_index_in_dim(own_row, block, 0, keepdims=False)
    seq_ends = jnp.cumsum(lengths)
    starts = seq_ends - lengths
    member = (group_pos[:, None] >= starts[None, :]) & (group_pos[:, None] < seq_ends[None, :])
    member_int = member.astype(jnp.int32)
    group_start = jnp.sum(member_int * starts[None, :], axis=1)
    group_owner = jnp.sum(member_int * adapter[None, :], axis=1)
    low, high = jnp.min(group_start), jnp.max(group_pos)
    active = (jnp.min(key_pos, axis=2) <= high) & (jnp.max(key_pos, axis=2) >= low)
    active = jnp.transpose(active).reshape(16).astype(jnp.int32)
    place = zh.reshape(1).astype(jnp.int32)
    columns = jnp.arange(rank, dtype=jnp.int32) // RANK
    select_g = (group_owner[:, None] == columns[None, :]).astype(f32)
    select = lax.dynamic_slice_in_dim(select_g, y * 128, 128, 0)
    cos_table, sin_table = rope_tables(group_pos - group_start, HEAD_SIZE)

    def column_slices(weight):
        rows_here, width = weight.shape
        parts = jnp.transpose(weight.reshape(rows_here, 16, 8, width // 128), (2, 0, 1, 3))
        return parts.reshape(8, rows_here, width // 8)

    heads_q = w_query.reshape(16, 4, 512)
    heads_kv = jnp.concatenate([w_key.reshape(16, 4, 256), w_value.reshape(16, 4, 256)], axis=2)
    qkv_parts = jnp.transpose(jnp.stack([heads_q, heads_kv], axis=2), (1, 2, 0, 3)).reshape(8, 16, 512)
    qkv_mine = lax.all_to_all(qkv_parts, ("y", "c"), split_axis=0, concat_axis=0, tiled=True).reshape(128, 512)
    qkv_mine = lax.all_gather(qkv_mine, PLANE, axis=0, tiled=True)
    qkv_other = swap_cores(qkv_mine)
    wq = jnp.where(c == 0, qkv_mine, qkv_other)
    wkv = jnp.where(c == 0, qkv_other, qkv_mine)
    wo = lax.all_gather(w_out, ALL, axis=0, tiled=True)
    gate_up_parts = jnp.concatenate([column_slices(w_gate), column_slices(w_up)], axis=2)
    gate_up = lax.all_to_all(gate_up_parts, ("y", "c"), split_axis=0, concat_axis=0, tiled=True).reshape(128, 2048)
    wgu_mine = lax.all_gather(gate_up, PLANE, axis=0, tiled=True)
    wd_mine = lax.all_gather(w_down, PLANE, axis=0, tiled=True)
    wgu_other, wd_other = swap_cores(wgu_mine), swap_cores(wd_mine)

    def columns_of(array, width):
        return lax.dynamic_slice_in_dim(array, y * width, width, 1)

    inputs = hidden.astype(f32)
    scale_in = row_scale(inputs)
    normed = (inputs * scale_in * gain_attn).astype(bf16)
    normed_g = gather_y(normed)
    cot_g = gather_y(cot)
    q_expand = columns_of(query_expand, 512)
    k_expand = columns_of(key_expand, 256)
    v_expand = columns_of(value_expand, 256)
    low_qkv = (product(normed_g, qkv_shrink) * jnp.tile(select_g, (1, 3))).astype(bf16)
    query_lin = product(normed_g, wq) + product(low_qkv[:, :rank], q_expand)
    kv_lin = product(normed_g, wkv)
    key_lin = kv_lin[:, :256] + product(low_qkv[:, rank : 2 * rank], k_expand)
    value_lin = kv_lin[:, 256:] + product(low_qkv[:, 2 * rank :], v_expand)
    query_heads = query_lin.reshape(GROUP, 2, HEAD_SIZE)
    key_heads = key_lin.reshape(GROUP, 1, HEAD_SIZE)
    query = (query_heads * cos_table + rotate(query_heads) * sin_table).astype(bf16)
    query = (query * bf16(factor)).reshape(GROUP, 512)
    key = (key_heads * cos_table + rotate(key_heads) * sin_table).astype(bf16).reshape(GROUP, 256)
    key_value = jnp.concatenate([key, value_lin.astype(bf16)], axis=1)

    family = lax.all_gather(key_value, PLANE, axis=0, tiled=True).reshape(2, 8, GROUP, GROUP)
    wanted = jnp.where(c == 0, zh, 0)
    prev = swap_cores(lax.dynamic_slice_in_dim(family, wanted, 1, 0))

    pos_col, start_col = group_pos[:, None], group_start[:, None]
    key_pos4 = key_pos.reshape(8, 2, 1, GROUP)
    mixed_f, lse = attend(active, place, query, pos_col, start_col, key_pos4, prev, family)
    mixed = mixed_f.astype(bf16)

    mixed_tok = lax.all_to_all(mixed, "y", split_axis=0, concat_axis=1, tiled=True)
    low_out = (product(mixed_tok, out_shrink) * select).astype(bf16)
    middle = inputs + product(mixed_tok, wo) + product(low_out, out_expand)
    scale_mid = row_scale(middle)
    normed_mid = (middle * scale_mid * gain_ffn).astype(bf16)
    normed_mid_g = gather_y(normed_mid)

    select_two = jnp.tile(select_g, (1, 2))
    low_gu = (product(normed_mid_g, gateup_shrink) * select_two).astype(bf16)
    grad_low_down = (times_transposed(cot_g, down_expand) * select_g).astype(bf16)
    result = jnp.zeros((GROUP, 2048), f32)
    low_down_part = jnp.zeros((GROUP, rank), f32)
    grad_mid_part = jnp.zeros((GROUP, 2048), f32)
    grad_low_part = jnp.zeros((GROUP, 2 * rank), f32)
    unit_grads = []
    units = 1024
    for wgu, wd, at in ((wgu_mine, wd_mine, mine), (wgu_other, wd_other, other)):
        wg, wu = wgu[:, :units], wgu[:, units:]
        g_expand = lax.dynamic_slice_in_dim(gate_expand.reshape(rank, 16, 8, 64), at, 1, 2).reshape(rank, units)
        u_expand = lax.dynamic_slice_in_dim(up_expand.reshape(rank, 16, 8, 64), at, 1, 2).reshape(rank, units)
        d_shrink = lax.dynamic_slice_in_dim(down_shrink.reshape(16, 8, 64, rank), at, 1, 1).reshape(units, rank)
        gate_pre = product(normed_mid_g, wg) + product(low_gu[:, :rank], g_expand)
        up_pre = product(normed_mid_g, wu) + product(low_gu[:, rank:], u_expand)
        sigmoid_g = jax.nn.sigmoid(gate_pre)
        silu_gate = gate_pre * sigmoid_g
        active_units = (silu_gate * up_pre).astype(bf16)
        result = result + product(active_units, wd)
        low_down_part = low_down_part + product(active_units, d_shrink)
        grad_active = times_transposed(cot_g, wd) + times_transposed(grad_low_down, d_shrink)
        grad_gate = (grad_active * up_pre * sigmoid_g * (1.0 + gate_pre * (1.0 - sigmoid_g))).astype(bf16)
        grad_up = (grad_active * silu_gate).astype(bf16)
        grad_mid_part = grad_mid_part + times_transposed(grad_gate, wg) + times_transposed(grad_up, wu)
        grad_low_part = grad_low_part + jnp.concatenate(
            [times_transposed(grad_gate, g_expand), times_transposed(grad_up, u_expand)], axis=1
        )
        unit_grads.append(
            (
                inner_rows(grad_gate, low_gu[:, :rank]),
                inner_rows(grad_up, low_gu[:, rank:]),
                inner_rows(active_units, grad_low_down),
            )
        )

    def sum_tokens(*parts):
        packed = jnp.concatenate([part.astype(bf16) for part in parts], axis=1)
        return sum_y(lambda i: lax.dynamic_slice_in_dim(packed, i * 128, 128, 0), y)

    back = sum_tokens(grad_mid_part, grad_low_part)
    ahead = sum_tokens(result, low_down_part)

    low_down = (ahead[:, 2048:] * select).astype(bf16)
    output = (middle + ahead[:, :2048] + product(low_down, down_expand)).astype(bf16)
    grad_low_gu = (back[:, 2048:] * jnp.tile(select, (1, 2))).astype(bf16)
    grad_normed_mid = back[:, :2048] + times_transposed(grad_low_gu, gateup_shrink)
    cot_f = cot.astype(f32)
    grad_middle = cot_f + norm_back(middle, scale_mid, gain_ffn, grad_normed_mid)
    grad_attn_out = grad_middle.astype(bf16)
    grad_low_out = (times_transposed(grad_attn_out, out_expand) * select).astype(bf16)
    grad_mixed = (times_transposed(grad_attn_out, wo) + times_transposed(grad_low_out, out_shrink)).astype(bf16)

    dout = lax.all_to_all(grad_mixed, "y", split_axis=1, concat_axis=0, tiled=True)
    dq, dprev, downed = attend_back(
        active, place, query, pos_col, start_col, key_pos4, prev, family, mixed_f, lse, dout
    )
    other_row = swap_cores(dprev)
    place_own = jnp.arange(2, dtype=jnp.int32) == zh
    place_got = jnp.where(c == 0, place_own, (jnp.arange(2, dtype=jnp.int32) == 0) & (zh == 1))
    terms = jnp.where(place_own[:, None, None, None], downed[None], bf16(0)) + jnp.where(
        place_got[:, None, None, None], other_row[None], bf16(0)
    )
    dkv = lax.psum_scatter(terms.reshape(16 * GROUP, GROUP), PLANE, scatter_dimension=0, tiled=True)
    dkv = dkv.astype(f32)
    query_back = (dq * factor).astype(bf16).astype(f32).reshape(GROUP, 2, HEAD_SIZE)
    key_back = dkv[:, :256].astype(bf16).astype(f32).reshape(GROUP, 1, HEAD_SIZE)
    grad_value = dkv[:, 256:].astype(bf16)
    grad_query = (query_back * cos_table - rotate(query_back * sin_table)).astype(bf16).reshape(GROUP, 512)
    grad_key = (key_back * cos_table - rotate(key_back * sin_table)).astype(bf16).reshape(GROUP, 256)
    grad_kv = jnp.concatenate([grad_key, grad_value], axis=1)

    grad_low_part = jnp.concatenate(
        [
            times_transposed(grad_query, q_expand),
            times_transposed(grad_key, k_expand),
            times_transposed(grad_value, v_expand),
        ],
        axis=1,
    )
    grad_normed_part = times_transposed(grad_query, wq) + times_transposed(grad_kv, wkv)
    last = sum_tokens(grad_normed_part, grad_low_part)
    grad_low_qkv = (last[:, 2048:] * jnp.tile(select, (1, 3))).astype(bf16)
    grad_normed = last[:, :2048] + times_transposed(grad_low_qkv, qkv_shrink)
    grad_input = (grad_middle + norm_back(inputs, scale_in, gain_attn, grad_normed)).astype(bf16)

    def features(array):
        return lax.dynamic_slice_in_dim(array, y * 512, 512, 1)

    def by_halves(pair_at):
        own, others = unit_grads[0][pair_at], unit_grads[1][pair_at]
        own, others = own.reshape(16, 1, 64, rank), others.reshape(16, 1, 64, rank)
        ordered = jnp.where(c == 0, jnp.concatenate([own, others], 1), jnp.concatenate([others, own], 1))
        return ordered.reshape(32, 64, rank)

    def by_rows(array):
        return array.reshape(32, array.shape[0] // 32, rank)

    low_down_g = gather_y(low_down)
    grad_low_gu_g = gather_y(grad_low_gu)
    grad_low_out_g = gather_y(grad_low_out)
    grad_low_qkv_g = gather_y(grad_low_qkv)
    low_out_g = gather_y(low_out)
    grad_attn_out_g = lax.all_to_all(grad_attn_out, "y", split_axis=1, concat_axis=0, tiled=True)
    grad_gateup = inner_rows(features(normed_mid_g), grad_low_gu_g)
    grad_qkv = inner_rows(features(normed_g), grad_low_qkv_g)
    pieces = [
        by_halves(0),
        by_halves(1),
        by_halves(2),
        by_rows(inner_rows(grad_query, low_qkv[:, :rank])),
        by_rows(inner_rows(grad_key, low_qkv[:, rank : 2 * rank])),
        by_rows(inner_rows(grad_value, low_qkv[:, 2 * rank :])),
        by_rows(inner_rows(mixed, grad_low_out_g)),
        by_rows(inner_rows(grad_attn_out_g, low_out_g)),
        by_rows(inner_rows(features(cot_g), low_down_g)),
        by_rows(grad_gateup[:, :rank]),
        by_rows(grad_gateup[:, rank:]),
        by_rows(grad_qkv[:, :rank]),
        by_rows(grad_qkv[:, rank : 2 * rank]),
        by_rows(grad_qkv[:, 2 * rank :]),
    ]
    sizes = [piece.shape[1] for piece in pieces]
    packed = jnp.concatenate(pieces, axis=1)
    summed = lax.psum_scatter(packed, PLANE + ("c",), scatter_dimension=0, tiled=False)
    everyone = lax.all_gather(summed.astype(bf16), ALL, axis=0, tiled=False)
    found, at = [], 0
    for size in sizes:
        found.append(everyone[:, at : at + size].astype(f32))
        at += size

    def units_order(array):
        return array.reshape(-1, rank)

    def rows_order(array):
        rows_each = array.shape[1]
        ordered = jnp.transpose(array.reshape(16, 4, 2, rows_each, rank), (1, 0, 2, 3, 4))
        return ordered.reshape(-1, rank)

    g_gate, g_up, g_down_shrink = (units_order(array) for array in found[:3])
    rest = [rows_order(array) for array in found[3:]]
    g_q, g_k, g_v, g_out_shrink, g_out_expand, g_down_expand = rest[:6]
    return (
        from_rows(output),
        from_rows(grad_input),
        jnp.concatenate(rest[8:11], axis=1),
        g_q.T,
        g_k.T,
        g_v.T,
        g_out_shrink,
        g_out_expand.T,
        jnp.concatenate(rest[6:8], axis=1),
        g_gate.T,
        g_up.T,
        g_down_shrink,
        g_down_expand.T,
    )


def solution(mesh):
    fine = Mesh(mesh.devices.reshape(2, 2, 4, 4, 2), ALL)
    split = P(ALL, None)
    placed = (split, P(), P()) + (split,) * 7 + (P(),) * 14 + (split,)
    return jax.shard_map(
        local,
        mesh=fine,
        in_specs=placed,
        out_specs=(split, split) + (P(),) * 11,
        check_vma=False,
    )
```

time: 2220 us -> 1050 us (0.47)
  waiting for transfers between devices: 978 us -> 509 us
  matrix products: 486 us -> 121 us
  blocking collectives: 237 us -> 89.5 us
  other arithmetic: 142 us -> 51.6 us
  local copies, waits for them, and re-layouts: 249 us -> 177 us
  loops' own time: 65.6 us -> 0 us
  Pallas kernels: 0 us -> 37.4 us
  starting transfers between devices: 16.7 us -> 39.4 us
    psum x1 -> x0, waiting for transfers between devices: 332 us -> none  [local(): lax.psum((grad_qkv_shrink, grad_query_expand, grad_key_expand, grad_value...]
    dot_general x144 -> x23, matrix products: 372 us -> 57.1 us  [product(): return jnp.dot(left, right, preferred_element_type=f32)]
    all_gather x11 -> x9, waiting for transfers between devices: 625 us -> 348 us  [the longest x1 68.6 us: local(): everyone = lax.all_gather(summed.astype(bf16), ALL, axis=0, tiled=False)]
    all_gather x2 -> x5, blocking collectives: 184 us -> 52.5 us  [gather_y(): return lax.all_gather(value, 'y', axis=0, tiled=True)]
    dynamic_slice x163 -> x9, local copies, waits for them, and re-layouts: 121 us -> 12.6 us  [the longest x1 4.76 us: local(): prev = swap_cores(lax.dynamic_slice_in_dim(family, wanted, 1, 0))]
    reduce_scatter x0 -> x2, waiting for transfers between devices: none -> 108 us  [the longest x1 85 us: local(): lax.psum_scatter(packed, PLANE + ('c',), scatter_dimension=0, tiled=False)]
    reduce_or x96 -> x0, other arithmetic: 103 us -> none  [the longest x32 48.1 us: grad_over_blocks(): jnp.any(allowed_here)]
    another operation x98 -> x0, loops' own time: 65.6 us -> none  [the longest x1 41.6 us: local(): lax.fori_loop(0, length // grad_stride, grad_over_blocks, (zero_queries,...]
  transfers between devices with their start and end apart: 16 -> 31, of which waited for: 13 -> 20; matrix products, arithmetic and copies ran while one was open for 17% -> 19% of each run, Pallas kernels for 0% -> 2%
where the time goes in v1:
time: 1050 us; the launch traced here: 1040 us
  waiting for transfers between devices  509 us (48%)
  local copies, waits for them, and re-layouts  177 us (17%)
  matrix products  121 us (12%)
  blocking collectives  89.5 us (9%)
  other arithmetic  51.6 us (5%)
  starting transfers between devices  39.4 us (4%)
  Pallas kernels  37.4 us (4%)
  between operations  16.2 us (2%)
    reduce_scatter x1, waiting for transfers between devices, local(): lax.psum_scatter(packed, PLANE + ('c',), scatter_dimension=0, tiled=False)  85 us
    unnamed x257, local copies, waits for them, and re-layouts  80.8 us
    all_gather x1, waiting for transfers between devices, local(): everyone = lax.all_gather(summed.astype(bf16), ALL, axis=0, tiled=False)  68.6 us
    all_gather x1, waiting for transfers between devices, local(): wo = lax.all_gather(w_out, ALL, axis=0, tiled=True)  67.9 us
    all_gather x3, waiting for transfers between devices, gather_y(): return lax.all_gather(value, 'y', axis=0, tiled=True)  60.5 us
    dot_general x23, matrix products, product(): return jnp.dot(left, right, preferred_element_type=f32)  57.1 us
    all_gather x1, waiting for transfers between devices, local(): lax.all_gather(key_value, PLANE, axis=0, tiled=True)  56.2 us
    all_gather x5, blocking collectives, gather_y(): return lax.all_gather(value, 'y', axis=0, tiled=True)  52.5 us
  transfers between devices with their start and end apart: 31, of which 20 were waited for; matrix products, arithmetic and copies ran while one was open for 19% of the time, Pallas kernels for 2%

profile of v1, /device:TPU:1, one launch (start us, length us, event | category | flops | bytes accessed | tf_op | source)
XLA Modules:
  0.0 1041.1 jit_solution(9280227837673463651)
XLA Ops:
  10.0 11.1 %all_to_all.67 = bf16[8,16,512]{2,1,0:T(8,128)(2,1)} all-to-all(bf16[8,16,512]{2,1,0:T(8,128)(2,1)S(1)} %bitcast.397), channel_id=1, replica_groups=mesh['zh'=2,'zl'=2,'x'=4,'y'=4,'c'=2] {'y','c'}, dimensions={0} | all-to-all | bytes 262144 | tf_op jit(solution)/shard_map/all_to_all | solution.py:315
  27.2 38.9 %all-gather.12.cloned.1.call-done = bf16[2048,512]{1,0:T(8,128)(2,1)} async-done(((bf16[128,512]{1,0:T(8,128)(2,1)}), bf16[2048,512]{1,0:T(8,128)(2,1)}) %all-gather.12.cloned.1.call-update) | async-done | bytes 2097168 | tf_op jit(solution)/shard_map/all_gather | solution.py:316
  71.4 28.1 %all-gather.10.cloned.1.call-done = bf16[512,2048]{1,0:T(8,128)(2,1)} async-done(((bf16[128,2048]{1,0:T(8,128)(2,1)}), bf16[512,2048]{1,0:T(8,128)(2,1)}) %all-gather.10.cloned.1.call-update) | async-done | bytes 2097168 | tf_op jit(solution)/shard_map/all_gather | solution.py:74
  99.5 3.0 fusion.28
  111.3 14.8 %all_to_all.68 = bf16[8,16,2048]{2,1,0:T(8,128)(2,1)} all-to-all(bf16[8,16,2048]{2,1,0:T(8,128)(2,1)S(1)} %pad_maximum_fusion.6), channel_id=1, replica_groups=mesh['zh'=2,'zl'=2,'x'=4,'y'=4,'c'=2] {'y','c'}, dimensions={0} | all-to-all | bytes 1048576 | tf_op jit(solution)/shard_map/all_to_all | solution.py:322
  131.4 56.2 %all-gather.14.cloned.1.call-done = bf16[8192,512]{0,1:T(8,128)(2,1)} async-done(((bf16[512,512]{0,1:T(8,128)(2,1)}), bf16[8192,512]{0,1:T(8,128)(2,1)}) %all-gather.14.cloned.1.call-update) | async-done | bytes 8388624 | tf_op jit(solution)/shard_map/all_gather | solution.py:350
  187.7 11.9 %copy.340 = bf16[8192,512]{1,0:T(8,128)(2,1)} copy(bf16[8192,512]{0,1:T(8,128)(2,1)} %all-gather.14.cloned.1.call-done) | data formatting | bytes 16777216 | tf_op jit(solution)/shard_map/all_gather | solution.py:350
  199.6 4.8 constant_dynamic-slice_fusion.12
  213.4 4.9 convolution_add_fusion.6
  218.3 2.8 reshape.490
  224.5 18.9 %attend.1 = (f32[512,512]{1,0:T(8,128)S(1)}, f32[2,512,1]{2,1,0:T(8,128)S(1)}) custom-call(s32[16]{0:T(128)S(1)} %reshape.550.active, s32[1]{0:T(128)} %bitcast.6.place, bf16[512,512]{1,0:T(8,128)(2,1)S(1)} %fusion.60.q_ref, s32[512,1]{1,0:T(8,128)S(1)} %copy-done.4, s32[512,1]{1,0:T(8,128)S(1)} %copy.342.start_ref, s32[8,2,1,512]{3,2,1,0:T(1,128)S(1)} %reshape.491.kpos_ref, ...), custom_call_target="tpu_custom_call" | custom-call | tf_op jit(solution)/shard_map/attend/pallas_call | solution.py:190
  247.1 4.1 all-to-all-start.1
  252.2 8.5 all-gather.20.cloned.1.call-done
  265.8 67.9 %all-gather.16.cloned.1.call-done = bf16[2048,2048]{1,0:T(8,128)(2,1)} async-done(((bf16[16,2048]{1,0:T(8,128)(2,1)}), bf16[2048,2048]{1,0:T(8,128)(2,1)}) %all-gather.16.cloned.1.call-update) | async-done | bytes 8388624 | tf_op jit(solution)/shard_map/all_gather | solution.py:320
  333.7 5.4 multiply_reduce_fusion.1
  341.1 4.1 copy.346
  345.2 4.1 copy.347
  354.9 8.9 all-gather.24.cloned.1.call-done
  369.8 47.8 %all-gather.22.cloned.1.call-done = bf16[1024,2048]{1,0:T(8,128)(2,1)} async-done(((bf16[64,2048]{1,0:T(8,128)(2,1)}), bf16[1024,2048]{1,0:T(8,128)(2,1)}) %all-gather.22.cloned.1.call-update) | async-done | bytes 4194320 | tf_op jit(solution)/shard_map/all_gather | solution.py:324
  417.6 9.2 collective-permute-start.4
  426.8 23.5 %all-gather.18.cloned.1.call-done = bf16[512,2048]{1,0:T(8,128)(2,1)} async-done(((bf16[128,2048]{1,0:T(8,128)(2,1)}), bf16[512,2048]{1,0:T(8,128)(2,1)}) %all-gather.18.cloned.1.call-update) | async-done | bytes 2097168 | tf_op jit(solution)/shard_map/all_gather | solution.py:74
  451.5 2.7 fusion.29
  454.2 4.7 fusion.10
  464.1 5.5 multiply_convert_fusion.2
  473.3 4.6 fusion.25
  477.9 6.3 fusion.22
  484.2 6.2 multiply_convert_fusion
  492.4 4.5 fusion.141
  496.9 4.6 add_convert_fusion.2
  504.2 3.1 collective-permute-start.7
  512.1 4.6 fusion.4
  516.7 4.8 add_convert_fusion.1
  525.5 6.6 collective-permute-done.6
  534.6 8.0 collective-permute-done.10
  542.6 13.6 %collective-permute-done.11 = bf16[128,2304]{1,0:T(8,128)(2,1)S(1)} collective-permute-done((bf16[128,2304]{1,0:T(8,128)(2,1)S(1)}, bf16[128,2304]{1,0:T(8,128)(2,1)S(1)}, u32[]{:S(2)}, u32[]{:S(2)}) %collective-permute-start.11) | collective-permute-done | bytes 589856 | tf_op jit(solution)/shard_map/ppermute | solution.py:70
  561.1 2.9 fusion.149
  564.4 11.0 %all_to_all.69 = bf16[128,4,512]{2,0,1:T(8,128)(2,1)S(1)} all-to-all(bf16[128,4,512]{2,0,1:T(8,128)(2,1)S(1)} %bitcast.377), channel_id=1, replica_groups=mesh['zh'=2,'zl'=2,'x'=4,'y'=4,'c'=2] {'y'}, dimensions={1} | all-to-all | bytes 1048576 | tf_op jit(solution)/shard_map/all_to_all | solution.py:419
  575.4 18.5 %attend_back.1 = (f32[512,512]{1,0:T(8,128)S(1)}, bf16[8,512,512]{2,1,0:T(8,128)(2,1)}, bf16[8,512,512]{2,1,0:T(8,128)(2,1)S(1)}) custom-call(s32[16]{0:T(128)S(1)} %reshape.550.active, s32[1]{0:T(128)} %bitcast.6.place, bf16[512,512]{1,0:T(8,128)(2,1)S(1)} %fusion.60.q_ref, s32[512,1]{1,0:T(8,128)S(1)} %copy-done.5, s32[512,1]{1,0:T(8,128)S(1)} %copy.342.start_ref, ...), custom_call_target="tpu_custom_call" | custom-call | tf_op jit(solution)/shard_map/attend_back/pallas_call | solution.py:213
  597.3 8.0 copy.357
  605.3 6.3 broadcast_in_dim.77
  611.6 16.5 %copy.416 = bf16[64,8,16,512]{3,1,2,0:T(8,128)(2,1)} copy(bf16[64,8,16,512]{3,2,1,0:T(8,128)(2,1)} %bitcast.319) | data formatting | bytes 16777216
  628.1 8.3 copy.358
  636.5 6.3 broadcast_in_dim.83
  642.8 16.6 %copy.418 = bf16[64,8,16,512]{3,1,2,0:T(8,128)(2,1)} copy(bf16[64,8,16,512]{3,2,1,0:T(8,128)(2,1)} %bitcast.320) | data formatting | bytes 16777216
  659.4 9.1 select_add_fusion
  669.5 10.1 all_gather.52
  688.3 9.6 all_gather.53
  700.9 4.3 all-to-all-start.4
  705.2 11.9 %all_gather.54 = bf16[512,256]{1,0:T(8,128)(2,1)S(1)} all-gather(bf16[128,256]{1,0:T(8,128)(2,1)S(1)} %copy-done.86), channel_id=1, replica_groups=mesh['zh'=2,'zl'=2,'x'=4,'y'=4,'c'=2] {'y'}, dimensions={0}, use_global_device_ids=true | all-gather | bytes 327680 | tf_op jit(solution)/shard_map/all_gather | solution.py:74
  719.5 10.2 all_gather.51
  733.8 2.9 reshape.508
  743.8 23.0 %reduce-scatter.3.cloned.1.call-done = bf16[512,512]{0,1:T(8,128)(2,1)} async-done(((bf16[8192,512]{0,1:T(8,128)(2,1)}), bf16[512,512]{0,1:T(8,128)(2,1)}) %reduce-scatter.3.cloned.1.call-update) | async-done | bytes 524304 | tf_op jit(solution)/shard_map/reduce_scatter | solution.py:429
  771.8 3.0 add_convert_fusion
  775.2 2.8 collective-permute-start.14
  785.6 4.9 collective-permute-done.14
  790.5 14.7 %collective-permute-done.16 = bf16[128,2432]{1,0:T(8,128)(2,1)S(1)} collective-permute-done((bf16[128,2432]{1,0:T(8,128)(2,1)S(1)}, bf16[128,2432]{1,0:T(8,128)(2,1)S(1)}, u32[]{:S(2)}, u32[]{:S(2)}) %collective-permute-start.16) | collective-permute-done | bytes 622624 | tf_op jit(solution)/shard_map/ppermute | solution.py:70
  806.5 10.6 %all_gather.55 = bf16[512,384]{1,0:T(8,128)(2,1)S(1)} all-gather(bf16[128,384]{1,0:T(8,128)(2,1)S(1)} %fusion.79), channel_id=1, replica_groups=mesh['zh'=2,'zl'=2,'x'=4,'y'=4,'c'=2] {'y'}, dimensions={0}, use_global_device_ids=true | all-gather | bytes 491520 | tf_op jit(solution)/shard_map/all_gather | solution.py:74
  821.1 85.0 %reduce-scatter.5.cloned.1.call-done = f32[1,352,128]{2,1,0:T(8,128)} async-done(((f32[32,352,128]{2,1,0:T(8,128)}), f32[1,352,128]{2,1,0:T(8,128)}) %reduce-scatter.5.cloned.1.call-update) | async-done | bytes 180240 | tf_op jit(solution)/shard_map/reduce_scatter | solution.py:490
  915.1 68.6 %all-gather.26.cloned.1.call-done = bf16[128,352,128]{2,1,0:T(8,128)(2,1)} async-done(((bf16[1,352,128]{2,1,0:T(8,128)(2,1)}), bf16[128,352,128]{2,1,0:T(8,128)(2,1)}) %all-gather.26.cloned.1.call-update) | async-done | bytes 11534352 | tf_op jit(solution)/shard_map/all_gather | solution.py:491
  986.9 4.4 fusion.132
  1004.6 5.7 fusion.133
  1015.2 5.6 copy.395
  1020.8 3.9 convert_bitcast_fusion.1
  1024.7 5.7 copy.394
  (483 shorter events, 175.6 us)
Async XLA Ops:
  7.2 92.3 %copy-start = (bf16[2048,384]{1,0:T(8,128)(2,1)S(1)}, bf16[2048,384]{1,0:T(8,128)(2,1)}, u32[]{:S(2)}) copy-start(bf16[2048,384]{1,0:T(8,128)(2,1)} %param.35) | copy-start | bytes 4718596
  7.2 18.5 %copy-start.100 = (f32[2048]{0:T(1024)S(1)}, f32[2048]{0:T(1024)}, u32[]{:S(2)}) copy-start(f32[2048]{0:T(1024)} %param.26) | copy-start | bytes 24580
  7.2 58.9 %all-gather.12.cloned.1.call-start = ((), (), s32[]{:S(2)}) async-start(), calls=%async_computation.8 | async-start | bytes 2228224 | tf_op jit(solution)/shard_map/all_gather | solution.py:316
  9.8 17.0 %copy-start.107 = (s32[16]{0:T(128)S(1)}, s32[16]{0:T(128)}, u32[]{:S(2)}) copy-start(s32[16]{0:T(128)} %param.46) | copy-start | bytes 196
  9.8 17.2 %copy-start.102 = (s32[16384]{0:T(1024)S(1)}, s32[16384]{0:T(1024)}, u32[]{:S(2)}) copy-start(s32[16384]{0:T(1024)} %param.48) | copy-start | bytes 196612
  21.2 78.4 %all-gather.10.cloned.1.call-start = ((), (), s32[]{:S(2)}) async-start(), calls=%async_computation.7 | async-start | bytes 2621440 | tf_op jit(solution)/shard_map/all_gather | solution.py:74
  21.2 47.8 %copy-start.108 = (s32[16]{0:T(128)S(1)}, s32[16]{0:T(128)}, u32[]{:S(2)}) copy-start(s32[16]{0:T(128)} %param.47) | copy-start | bytes 196
  22.3 2.1 collective-permute-start
  26.7 160.9 %all-gather.14.cloned.1.call-start = ((), (), s32[]{:S(2)}) async-start(), calls=%async_computation.9 | async-start | bytes 8912896 | tf_op jit(solution)/shard_map/all_gather | solution.py:350
  66.1 37.7 %collective-permute-start.1 = (bf16[2048,512]{1,0:T(8,128)(2,1)}, bf16[2048,512]{1,0:T(8,128)(2,1)}, u32[]{:S(2)}, u32[]{:S(2)}) collective-permute-start(bf16[2048,512]{1,0:T(8,128)(2,1)} %all-gather.12.cloned.1.call-done), channel_id=1, source_target_pairs={{0,1},{1,0},{2,3},{3,2},{4,5},{5,4},{6,7},{7,6},{8,9},{9,8},{10,11... | collective-permute-start | bytes 6291464 | tf_op jit(solution)/shard_map/ppermute | solution.py:66
  69.2 33.3 %copy-start.39 = (f32[512,128]{1,0:T(8,128)}, f32[512,128]{1,0:T(8,128)S(1)}, u32[]{:S(2)}) copy-start(f32[512,128]{1,0:T(8,128)S(1)} %compare_convert_fusion) | copy-start | bytes 786436
  71.4 35.0 %copy-start.50 = (f32[512,128]{0,1:T(8,128)}, f32[512,128]{0,1:T(8,128)S(1)}, u32[]{:S(2)}) copy-start(f32[512,128]{0,1:T(8,128)S(1)} %get-tuple-element.161) | copy-start | bytes 786436
  71.4 35.0 %copy-start.52 = (f32[512,128]{0,1:T(8,128)}, f32[512,128]{0,1:T(8,128)S(1)}, u32[]{:S(2)}) copy-start(f32[512,128]{0,1:T(8,128)S(1)} %get-tuple-element.162) | copy-start | bytes 786436
  108.3 152.4 %all-gather.20.cloned.1.call-start = ((), (), s32[]{:S(2)}) async-start(), calls=%async_computation.12 | async-start | bytes 8912896 | tf_op jit(solution)/shard_map/all_gather | solution.py:323
  111.2 15.6 %copy-start.89 = (bf16[128,2048]{1,0:T(8,128)(2,1)S(1)}, bf16[128,2048]{1,0:T(8,128)(2,1)}, u32[]{:S(2)}) copy-start(bf16[128,2048]{1,0:T(8,128)(2,1)} %param.49) | copy-start | bytes 1572868
  126.1 207.6 %all-gather.16.cloned.1.call-start = ((), (), s32[]{:S(2)}) async-start(), calls=%async_computation.10 | async-start | bytes 8454144 | tf_op jit(solution)/shard_map/all_gather | solution.py:320
  126.7 237.1 %all-gather.24.cloned.1.call-start = ((), (), s32[]{:S(2)}) async-start(), calls=%async_computation.14 | async-start | bytes 2621440 | tf_op jit(solution)/shard_map/all_gather | solution.py:74
  126.8 2.3 collective-permute-start.9
  130.7 286.9 %all-gather.22.cloned.1.call-start = ((), (), s32[]{:S(2)}) async-start(), calls=%async_computation.13 | async-start | bytes 4456448 | tf_op jit(solution)/shard_map/all_gather | solution.py:324
  204.4 20.2 %collective-permute-start.2 = (bf16[1,8,512,512]{3,2,1,0:T(8,128)(2,1)}, bf16[1,8,512,512]{3,2,1,0:T(8,128)(2,1)}, u32[]{:S(2)}, u32[]{:S(2)}) collective-permute-start(bf16[1,8,512,512]{3,2,1,0:T(8,128)(2,1)} %constant_dynamic-slice_fusion.12), channel_id=1, source_target_pairs={{0,1},{1,0},{2,3},{3,2},{4,5},{5,4},{6,7},{7,6},{8,9},{9,8},{10,11... | collective-permute-start | bytes 12582920 | tf_op jit(solution)/shard_map/ppermute | solution.py:66
  247.1 14.3 %all-to-all-start.1 = ((bf16[4,128,512]{1,2,0:T(8,128)(2,1)}), bf16[4,128,512]{1,2,0:T(8,128)(2,1)}, u32[]{:S(2)}, u32[]{:S(2)}) async-start(bf16[4,128,512]{1,2,0:T(8,128)(2,1)} %copy.343), calls=%async_computation.1 | async-start | bytes 1048576 | tf_op jit(solution)/shard_map/all_to_all | solution.py:359
  251.3 199.1 %all-gather.18.cloned.1.call-start = ((), (), s32[]{:S(2)}) async-start(), calls=%async_computation.11 | async-start | bytes 2621440 | tf_op jit(solution)/shard_map/all_gather | solution.py:74
  260.7 212.6 %collective-permute-start.3 = (bf16[2048,2048]{1,0:T(8,128)(2,1)}, bf16[2048,2048]{1,0:T(8,128)(2,1)}, u32[]{:S(2)}, u32[]{:S(2)}) collective-permute-start(bf16[2048,2048]{1,0:T(8,128)(2,1)} %all-gather.20.cloned.1.call-done), channel_id=1, source_target_pairs={{0,1},{1,0},{2,3},{3,2},{4,5},{5,4},{6,7},{7,6},{8,9},{9,8},{10,11... | collective-permute-start | bytes 25165832 | tf_op jit(solution)/shard_map/ppermute | solution.py:66
  265.8 74.2 %copy-start.99 = (f32[2048]{0:T(1024)S(1)}, f32[2048]{0:T(1024)}, u32[]{:S(2)}) copy-start(f32[2048]{0:T(1024)} %param.27) | copy-start | bytes 24580
  341.0 425.7 %reduce-scatter.3.cloned.1.call-start = ((), (), s32[]{:S(2)}) async-start(), calls=%async_computation.15 | async-start | bytes 8912896 | tf_op jit(solution)/shard_map/reduce_scatter | solution.py:429
  417.6 66.6 %collective-permute-start.4 = (bf16[1024,2048]{1,0:T(8,128)(2,1)}, bf16[1024,2048]{1,0:T(8,128)(2,1)}, u32[]{:S(2)}, u32[]{:S(2)}) collective-permute-start(bf16[1024,2048]{1,0:T(8,128)(2,1)} %all-gather.22.cloned.1.call-done), channel_id=1, source_target_pairs={{0,1},{1,0},{2,3},{3,2},{4,5},{5,4},{6,7},{7,6},{8,9},{9,8},{10,11... | collective-permute-start | bytes 12582920 | tf_op jit(solution)/shard_map/ppermute | solution.py:66
  454.2 18.6 %copy-start.37 = (bf16[512,256]{1,0:T(8,128)(2,1)}, bf16[512,256]{1,0:T(8,128)(2,1)S(1)}, u32[]{:S(2)}) copy-start(bf16[512,256]{1,0:T(8,128)(2,1)S(1)} %fusion.29) | copy-start | bytes 786436
  469.6 22.8 %copy-start.28 = (bf16[512,1024]{1,0:T(8,128)(2,1)}, bf16[512,1024]{1,0:T(8,128)(2,1)S(1)}, u32[]{:S(2)}) copy-start(bf16[512,1024]{1,0:T(8,128)(2,1)S(1)} %get-tuple-element.116) | copy-start | bytes 3145732
  469.6 37.7 %copy-start.30 = (bf16[512,1024]{1,0:T(8,128)(2,1)}, bf16[512,1024]{1,0:T(8,128)(2,1)S(1)}, u32[]{:S(2)}) copy-start(bf16[512,1024]{1,0:T(8,128)(2,1)S(1)} %get-tuple-element.115) | copy-start | bytes 3145732
  469.6 40.1 %copy-start.32 = (bf16[512,1024]{1,0:T(8,128)(2,1)}, bf16[512,1024]{1,0:T(8,128)(2,1)S(1)}, u32[]{:S(2)}) copy-start(bf16[512,1024]{1,0:T(8,128)(2,1)S(1)} %get-tuple-element.114) | copy-start | bytes 3145732
  490.4 26.3 %copy-start.14 = (bf16[512,1024]{1,0:T(8,128)(2,1)}, bf16[512,1024]{1,0:T(8,128)(2,1)S(1)}, u32[]{:S(2)}) copy-start(bf16[512,1024]{1,0:T(8,128)(2,1)S(1)} %get-tuple-element.111) | copy-start | bytes 3145732
  490.4 31.1 %copy-start.33 = (bf16[512,1024]{1,0:T(8,128)(2,1)}, bf16[512,1024]{1,0:T(8,128)(2,1)S(1)}, u32[]{:S(2)}) copy-start(bf16[512,1024]{1,0:T(8,128)(2,1)S(1)} %get-tuple-element.112) | copy-start | bytes 3145732
  502.8 20.2 %collective-permute-start.5 = (bf16[128,2176]{1,0:T(8,128)(2,1)}, bf16[128,2176]{1,0:T(8,128)(2,1)}, u32[]{:S(2)}, u32[]{:S(2)}) collective-permute-start(bf16[128,2176]{1,0:T(8,128)(2,1)} %get-tuple-element.123), channel_id=1, source_target_pairs={{0,4},{2,6},{4,0},{6,2},{1,5},{3,7},{5,1},{7,3},{8,12},{10,14},{12... | collective-permute-start | bytes 1671176 | tf_op jit(solution)/shard_map/ppermute | solution.py:70
  504.2 27.8 %collective-permute-start.6 = (bf16[128,2176]{1,0:T(8,128)(2,1)}, bf16[128,2176]{1,0:T(8,128)(2,1)}, u32[]{:S(2)}, u32[]{:S(2)}) collective-permute-start(bf16[128,2176]{1,0:T(8,128)(2,1)} %get-tuple-element.124), channel_id=1, source_target_pairs={{0,2},{2,4},{4,6},{6,0},{1,3},{3,5},{5,7},{7,1},{8,10},{10,12},{12... | collective-permute-start | bytes 1671176 | tf_op jit(solution)/shard_map/ppermute | solution.py:70
  504.2 27.8 %collective-permute-start.7 = (bf16[128,2176]{1,0:T(8,128)(2,1)}, bf16[128,2176]{1,0:T(8,128)(2,1)}, u32[]{:S(2)}, u32[]{:S(2)}) collective-permute-start(bf16[128,2176]{1,0:T(8,128)(2,1)} %get-tuple-element.125), channel_id=1, source_target_pairs={{0,6},{2,0},{4,2},{6,4},{1,7},{3,1},{5,3},{7,5},{8,14},{10,8},{12,... | collective-permute-start | bytes 1671176 | tf_op jit(solution)/shard_map/ppermute | solution.py:70
  522.3 20.4 %collective-permute-start.10 = (bf16[128,2304]{1,0:T(8,128)(2,1)S(1)}, bf16[128,2304]{1,0:T(8,128)(2,1)S(1)}, u32[]{:S(2)}, u32[]{:S(2)}) collective-permute-start(bf16[128,2304]{1,0:T(8,128)(2,1)S(1)} %get-tuple-element.120), channel_id=1, source_target_pairs={{0,4},{2,6},{4,0},{6,2},{1,5},{3,7},{5,1},{7,3},{8,12},{10,14},{12... | collective-permute-start | bytes 1769480 | tf_op jit(solution)/shard_map/ppermute | solution.py:70
  522.6 33.6 %collective-permute-start.11 = (bf16[128,2304]{1,0:T(8,128)(2,1)S(1)}, bf16[128,2304]{1,0:T(8,128)(2,1)S(1)}, u32[]{:S(2)}, u32[]{:S(2)}) collective-permute-start(bf16[128,2304]{1,0:T(8,128)(2,1)S(1)} %get-tuple-element.121), channel_id=1, source_target_pairs={{0,2},{2,4},{4,6},{6,0},{1,3},{3,5},{5,7},{7,1},{8,10},{10,12},{12... | collective-permute-start | bytes 1769480 | tf_op jit(solution)/shard_map/ppermute | solution.py:70
  522.9 33.3 %collective-permute-start.12 = (bf16[128,2304]{1,0:T(8,128)(2,1)S(1)}, bf16[128,2304]{1,0:T(8,128)(2,1)S(1)}, u32[]{:S(2)}, u32[]{:S(2)}) collective-permute-start(bf16[128,2304]{1,0:T(8,128)(2,1)S(1)} %get-tuple-element.122), channel_id=1, source_target_pairs={{0,6},{2,0},{4,2},{6,4},{1,7},{3,1},{5,3},{7,5},{8,14},{10,8},{12,... | collective-permute-start | bytes 1769480 | tf_op jit(solution)/shard_map/ppermute | solution.py:70
  534.6 22.1 %copy-start.9 = (f32[128,2048]{1,0:T(8,128)S(1)}, f32[128,2048]{1,0:T(8,128)}, u32[]{:S(2)}) copy-start(f32[128,2048]{1,0:T(8,128)} %copy-done.8) | copy-start | bytes 3145732
  534.6 22.1 %copy-start.73 = (bf16[2048,256]{1,0:T(8,128)(2,1)S(1)}, bf16[2048,256]{1,0:T(8,128)(2,1)}, u32[]{:S(2)}) copy-start(bf16[2048,256]{1,0:T(8,128)(2,1)} %param.41) | copy-start | bytes 3145732
  564.0 11.4 %copy-start.5 = (s32[512,1]{1,0:T(8,128)S(1)}, s32[512,1]{1,0:T(8,128)}, u32[]{:S(2)}) copy-start(s32[512,1]{1,0:T(8,128)} %copy.341.pos_ref) | copy-start | bytes 6148
  564.0 11.4 %copy-start.7 = (f32[2,512,1]{2,1,0:T(8,128)S(1)}, f32[2,512,1]{2,1,0:T(8,128)}, u32[]{:S(2)}) copy-start(f32[2,512,1]{2,1,0:T(8,128)} %copy-done.6) | copy-start | bytes 12292
  596.9 31.3 %collective-permute-start.13 = (bf16[8,512,512]{2,1,0:T(8,128)(2,1)}, bf16[8,512,512]{2,1,0:T(8,128)(2,1)}, u32[]{:S(2)}, u32[]{:S(2)}) collective-permute-start(bf16[8,512,512]{2,1,0:T(8,128)(2,1)} %get-tuple-element.22), channel_id=1, source_target_pairs={{0,1},{1,0},{2,3},{3,2},{4,5},{5,4},{6,7},{7,6},{8,9},{9,8},{10,11... | collective-permute-start | bytes 12582920 | tf_op jit(solution)/shard_map/ppermute | solution.py:66
  668.6 13.2 %copy-start.15 = (bf16[512,1024]{1,0:T(8,128)(2,1)S(1)}, bf16[512,1024]{1,0:T(8,128)(2,1)}, u32[]{:S(2)}) copy-start(bf16[512,1024]{1,0:T(8,128)(2,1)} %copy-done.14) | copy-start | bytes 3145732
  669.5 11.9 %copy-start.31 = (bf16[512,1024]{1,0:T(8,128)(2,1)S(1)}, bf16[512,1024]{1,0:T(8,128)(2,1)}, u32[]{:S(2)}) copy-start(bf16[512,1024]{1,0:T(8,128)(2,1)} %copy-done.30) | copy-start | bytes 3145732
  687.2 12.8 %copy-start.17 = (bf16[128,2048]{1,0:T(8,128)(2,1)S(1)}, bf16[128,2048]{1,0:T(8,128)(2,1)}, u32[]{:S(2)}) copy-start(bf16[128,2048]{1,0:T(8,128)(2,1)} %copy-done.16) | copy-start | bytes 1572868
  688.3 16.9 %copy-start.86 = (bf16[128,256]{1,0:T(8,128)(2,1)S(1)}, bf16[128,256]{1,0:T(8,128)(2,1)}, u32[]{:S(2)}) copy-start(bf16[128,256]{1,0:T(8,128)(2,1)} %copy-done.85) | copy-start | bytes 196612
  700.9 18.6 %copy-start.92 = (bf16[128,128]{1,0:T(8,128)(2,1)S(1)}, bf16[128,128]{1,0:T(8,128)(2,1)}, u32[]{:S(2)}) copy-start(bf16[128,128]{1,0:T(8,128)(2,1)} %copy-done.91) | copy-start | bytes 98308
  700.9 28.8 %copy-start.25 = (bf16[512,512]{1,0:T(8,128)(2,1)S(1)}, bf16[512,512]{1,0:T(8,128)(2,1)}, u32[]{:S(2)}) copy-start(bf16[512,512]{1,0:T(8,128)(2,1)} %convert_element_type.203) | copy-start | bytes 1572868
  700.9 29.8 %all-to-all-start.4 = ((bf16[128,4,512]{2,0,1:T(8,128)(2,1)}), bf16[128,4,512]{2,0,1:T(8,128)(2,1)}, u32[]{:S(2)}, u32[]{:S(2)}) async-start(bf16[128,4,512]{2,0,1:T(8,128)(2,1)} %bitcast.309), calls=%async_computation.5 | async-start | bytes 1048576 | tf_op jit(solution)/shard_map/all_to_all | solution.py:469
  705.2 200.9 %reduce-scatter.5.cloned.1.call-start = ((), (), s32[]{:S(2)}) async-start(), calls=%async_computation.16 | async-start | bytes 5947392 | tf_op jit(solution)/shard_map/reduce_scatter | solution.py:490
  717.2 15.6 %copy-start.2 = (f32[512,512]{1,0:T(8,128)S(1)}, f32[512,512]{1,0:T(8,128)}, u32[]{:S(2)}) copy-start(f32[512,512]{1,0:T(8,128)} %copy-done.1) | copy-start | bytes 3145732
  740.6 26.1 %copy-start.53 = (f32[512,128]{0,1:T(8,128)S(1)}, f32[512,128]{0,1:T(8,128)}, u32[]{:S(2)}) copy-start(f32[512,128]{0,1:T(8,128)} %copy-done.52) | copy-start | bytes 786436
  740.8 27.1 %copy-start.51 = (f32[512,128]{0,1:T(8,128)S(1)}, f32[512,128]{0,1:T(8,128)}, u32[]{:S(2)}) copy-start(f32[512,128]{0,1:T(8,128)} %copy-done.50) | copy-start | bytes 786436
  775.2 15.3 %collective-permute-start.14 = (bf16[128,2432]{1,0:T(8,128)(2,1)S(1)}, bf16[128,2432]{1,0:T(8,128)(2,1)S(1)}, u32[]{:S(2)}, u32[]{:S(2)}) collective-permute-start(bf16[128,2432]{1,0:T(8,128)(2,1)S(1)} %get-tuple-element.117), channel_id=1, source_target_pairs={{0,4},{2,6},{4,0},{6,2},{1,5},{3,7},{5,1},{7,3},{8,12},{10,14},{12... | collective-permute-start | bytes 1867784 | tf_op jit(solution)/shard_map/ppermute | solution.py:70
  778.1 27.1 %collective-permute-start.16 = (bf16[128,2432]{1,0:T(8,128)(2,1)S(1)}, bf16[128,2432]{1,0:T(8,128)(2,1)S(1)}, u32[]{:S(2)}, u32[]{:S(2)}) collective-permute-start(bf16[128,2432]{1,0:T(8,128)(2,1)S(1)} %get-tuple-element.118), channel_id=1, source_target_pairs={{0,6},{2,0},{4,2},{6,4},{1,7},{3,1},{5,3},{7,5},{8,14},{10,8},{12,... | collective-permute-start | bytes 1867784 | tf_op jit(solution)/shard_map/ppermute | solution.py:70
  779.2 26.9 %collective-permute-start.15 = (bf16[128,2432]{1,0:T(8,128)(2,1)S(1)}, bf16[128,2432]{1,0:T(8,128)(2,1)S(1)}, u32[]{:S(2)}, u32[]{:S(2)}) collective-permute-start(bf16[128,2432]{1,0:T(8,128)(2,1)S(1)} %get-tuple-element.119), channel_id=1, source_target_pairs={{0,2},{2,4},{4,6},{6,0},{1,3},{3,5},{5,7},{7,1},{8,10},{10,12},{12... | collective-permute-start | bytes 1867784 | tf_op jit(solution)/shard_map/ppermute | solution.py:70
  784.9 21.6 %copy-start.84 = (f32[128,384]{1,0:T(8,128)S(1)}, f32[128,384]{1,0:T(8,128)}, u32[]{:S(2)}) copy-start(f32[128,384]{1,0:T(8,128)} %copy.363) | copy-start | bytes 589828
  821.0 90.1 %copy-start.11 = (bf16[64,2048]{1,0:T(8,128)(2,1)S(1)}, bf16[64,2048]{1,0:T(8,128)(2,1)}, u32[]{:S(2)}) copy-start(bf16[64,2048]{1,0:T(8,128)(2,1)} %copy-done.10) | copy-start | bytes 786436
  821.0 90.1 %copy-start.22 = (bf16[64,2048]{1,0:T(8,128)(2,1)S(1)}, bf16[64,2048]{1,0:T(8,128)(2,1)}, u32[]{:S(2)}) copy-start(bf16[64,2048]{1,0:T(8,128)(2,1)} %copy-done.21) | copy-start | bytes 786436
  821.0 90.2 %copy-start.101 = (f32[2048]{0:T(1024)S(1)}, f32[2048]{0:T(1024)}, u32[]{:S(2)}) copy-start(f32[2048]{0:T(1024)} %param.26) | copy-start | bytes 24580
  821.0 162.6 %all-gather.26.cloned.1.call-start = ((), (), s32[]{:S(2)}) async-start(), calls=%async_computation.17 | async-start | bytes 11624448 | tf_op jit(solution)/shard_map/all_gather | solution.py:491
  908.7 4.2 collective-permute-start.8
  912.5 1.6 collective-permute-start.17
  (83 other events, 299.7 us)
Sparse Core Ops, SparseCore 0:
  21.3 44.7 all-gather.11
  68.3 31.1 all-gather.9
  108.4 79.1 all-gather.13
  189.6 70.9 all-gather.19
  263.5 70.1 all-gather.15
  335.8 27.9 all-gather.23
  365.9 51.6 all-gather.21
  419.9 30.4 all-gather.17
  668.6 98.0 reduce-scatter.2
  821.1 84.8 reduce-scatter.4
  910.0 73.5 all-gather.25

commit v2 on v1

v2 whole, which is shorter than its diff:
```python
from functools import partial

import jax
import jax.numpy as jnp
from jax import lax
from jax.experimental import pallas as pl
from jax.experimental.pallas import tpu as pltpu
from jax.sharding import Mesh, PartitionSpec as P

HEAD_SIZE = 256
RANK = 16
HALF = 64
GROUP = 512

ALL = ("zh", "zl", "x", "y", "c")
PLANE = ("zh", "zl", "x")

norm_eps = 1e-06
rope_theta = 1000042.0
neg_big = -1e30
far = 1 << 30

f32 = jnp.float32
bf16 = jnp.bfloat16


def product(left, right):
    return jnp.dot(left, right, preferred_element_type=f32)


def times_transposed(left, right):
    return lax.dot_general(left, right, (((1,), (1,)), ((), ())), preferred_element_type=f32)


def inner_rows(left, right):
    return lax.dot_general(left, right, (((0,), (0,)), ((), ())), preferred_element_type=f32)


def row_scale(value_matrix):
    return lax.rsqrt(jnp.mean(value_matrix * value_matrix, axis=-1, keepdims=True) + norm_eps)


def norm_back(value_matrix, scale, gain, grad):
    scaled = gain * grad
    return scale * scaled - value_matrix * (scale * scale * scale) * jnp.mean(
        value_matrix * scaled, axis=-1, keepdims=True
    )


def rotate(value_matrix):
    middle = value_matrix.shape[-1] // 2
    return jnp.concatenate([-value_matrix[..., middle:], value_matrix[..., :middle]], axis=-1)


def rope_tables(positions, width):
    middle = width // 2
    inverse = rope_theta ** (-(jnp.arange(middle, dtype=f32) * 2.0) / width)
    angles = positions.astype(f32)[:, None] * inverse[None, :]
    cos_half, sin_half = jnp.cos(angles), jnp.sin(angles)
    cos_table = jnp.concatenate([cos_half, cos_half], axis=-1)[:, None, :]
    sin_table = jnp.concatenate([sin_half, sin_half], axis=-1)[:, None, :]
    return (cos_table, sin_table)


RING = {"x": ("x",), "y": ("y",), "z": ("zh", "zl")}


def swap_cores(value):
    return lax.ppermute(value, "c", [(0, 1), (1, 0)])


def shift(value, ring, step):
    return lax.ppermute(value, RING[ring], [(i, (i + step) % 4) for i in range(4)])


def place_in(ring):
    return lax.axis_index(RING[ring])


def gather_near(value, ring, axis=0):
    return jnp.concatenate([value] + [shift(value, ring, -step) for step in (1, 2, 3)], axis=axis)


def gather_ring(value, ring):
    at = place_in(ring)
    whole_ring = jnp.zeros((4,) + value.shape, value.dtype)
    whole_ring = lax.dynamic_update_index_in_dim(whole_ring, value, at, 0)
    for step in (1, 2, 3):
        got = shift(value, ring, -step)
        whole_ring = lax.dynamic_update_index_in_dim(whole_ring, got, (at + step) % 4, 0)
    return whole_ring


def sum_near(blocks):
    got = [shift(blocks[step], "y", step) for step in (2, 1, 3)]
    total = blocks[0].astype(f32)
    for term in got:
        total = total + term.astype(f32)
    return total


def sum_ring(terms, ring):
    at = place_in(ring)
    got = [
        shift(lax.dynamic_index_in_dim(terms, (at + step) % 4, 0, keepdims=False).astype(bf16), ring, step)
        for step in (1, 2, 3)
    ]
    total = lax.dynamic_index_in_dim(terms, at, 0, keepdims=False)
    for term in got:
        total = total + term.astype(f32)
    return total


CORNER = ("zh", "zl", "c")
PARTNER = [(4 * zh + 2 * zl + c, 4 * zh + 2 * (1 - zl) + c) for zh in (0, 1) for zl in (0, 1) for c in (0, 1)]
LATER = [[(2 * zl + 1, 4 + 2 * (zl ^ flip)) for zl in (0, 1)] for flip in (0, 1)]
EARLIER = [[(to, came) for came, to in pairs] for pairs in LATER]
ROW_AHEAD = ("zh", "x", "c")


def shift_ahead(value, step):
    return lax.ppermute(value, ROW_AHEAD, [(8 + 2 * i, 8 + 2 * ((i + step) % 4)) for i in range(4)])


def gather_keys(key):
    line = gather_near(key[None], "x")
    own = jnp.stack([line, lax.ppermute(line, CORNER, PARTNER)])
    ahead = jnp.stack([lax.ppermute(line, CORNER, LATER[0]), lax.ppermute(line, CORNER, LATER[1])])
    return own, ahead


def gather_values(value):
    pair = jnp.stack([value, lax.ppermute(value, CORNER, PARTNER)])
    pair_ahead = jnp.stack([lax.ppermute(value, CORNER, LATER[0]), lax.ppermute(value, CORNER, LATER[1])])
    own = gather_near(pair[None], "x")
    ahead = jnp.concatenate([pair_ahead[None]] + [shift_ahead(pair_ahead, -step)[None] for step in (1, 2, 3)])
    return own, ahead


def row_before(own, ahead, c):
    return jnp.where(c == 0, ahead, lax.ppermute(own, "c", [(0, 1)]))


def sum_keys(own, before, c):
    got = lax.ppermute(before, "c", [(1, 0)])
    own = own.astype(f32) + got.astype(f32)
    line = own[0] + lax.ppermute(own[1].astype(bf16), CORNER, PARTNER).astype(f32)
    for flip in (0, 1):
        line = line + lax.ppermute(before[flip], CORNER, EARLIER[flip]).astype(f32)
    sent = line.astype(bf16)
    total = line[0]
    for step in (1, 2, 3):
        total = total + shift(sent[step], "x", step).astype(f32)
    return total


def sum_values(own, before, c):
    got = lax.ppermute(before, "c", [(1, 0)])
    own = own.astype(f32) + got.astype(f32)
    sent = own.astype(bf16)
    pair, pair_before = own[0], before[0].astype(f32)
    for step in (1, 2, 3):
        pair = pair + shift(sent[step], "x", step).astype(f32)
        pair_before = pair_before + shift_ahead(before[step], step).astype(f32)
    sent_before = pair_before.astype(bf16)
    total = pair[0] + lax.ppermute(pair[1].astype(bf16), CORNER, PARTNER).astype(f32)
    for flip in (0, 1):
        total = total + lax.ppermute(sent_before[flip], CORNER, EARLIER[flip]).astype(f32)
    return total


def allowed_mask(own_pos, own_start, key_pos):
    return (key_pos <= own_pos) & (key_pos >= own_start)


def attend_kernel(
    active,
    q_ref,
    pos_ref,
    start_ref,
    kpos_ref,
    kprev_ref,
    kown_ref,
    vprev_ref,
    vown_ref,
    mixed_ref,
    lse_ref,
    top,
    total,
    accum,
):
    step = pl.program_id(0)

    @pl.when(step == 0)
    def _():
        top[...] = jnp.full(top.shape, neg_big, f32)
        total[...] = jnp.zeros(total.shape, f32)
        accum[...] = jnp.zeros(accum.shape, f32)

    for side, k_ref, v_ref in ((0, kprev_ref, vprev_ref), (1, kown_ref, vown_ref)):

        @pl.when(active[side * 8 + step] != 0)
        def _():
            key, value = k_ref[0, 0], v_ref[0, 0]
            allowed = allowed_mask(pos_ref[...], start_ref[...], kpos_ref[0, side])
            for head in range(2):
                scores = times_transposed(q_ref[:, head * HEAD_SIZE : (head + 1) * HEAD_SIZE], key)
                scores = jnp.where(allowed, scores, neg_big)
                top_old = top[head]
                top_new = jnp.maximum(top_old, jnp.max(scores, axis=-1, keepdims=True))
                weights_p = jnp.where(allowed, jnp.exp(scores - top_new), 0.0)
                damping = jnp.exp(top_old - top_new)
                total[head] = total[head] * damping + jnp.sum(weights_p, axis=-1, keepdims=True)
                accum[head] = accum[head] * damping + product(weights_p.astype(bf16), value)
                top[head] = top_new

    @pl.when(step == 7)
    def _():
        for head in range(2):
            mixed_ref[:, head * HEAD_SIZE : (head + 1) * HEAD_SIZE] = accum[head] / total[head]
            lse_ref[head] = top[head] + jnp.log(total[head])


def attend_back_kernel(
    active,
    q_ref,
    pos_ref,
    start_ref,
    kpos_ref,
    kprev_ref,
    kown_ref,
    vprev_ref,
    vown_ref,
    mixed_ref,
    lse_ref,
    dout_ref,
    dq_ref,
    dkprev_ref,
    dkown_ref,
    dvprev_ref,
    dvown_ref,
    delta,
):
    step = pl.program_id(0)

    @pl.when(step == 0)
    def _():
        dq_ref[...] = jnp.zeros(dq_ref.shape, f32)
        for head in range(2):
            cols = slice(head * HEAD_SIZE, (head + 1) * HEAD_SIZE)
            delta[head] = jnp.sum(dout_ref[:, cols].astype(f32) * mixed_ref[:, cols], axis=-1, keepdims=True)

    for side, k_ref, v_ref, dk_ref, dv_ref in (
        (0, kprev_ref, vprev_ref, dkprev_ref, dvprev_ref),
        (1, kown_ref, vown_ref, dkown_ref, dvown_ref),
    ):

        @pl.when(active[side * 8 + step] == 0)
        def _():
            dk_ref[...] = jnp.zeros(dk_ref.shape, bf16)
            dv_ref[...] = jnp.zeros(dv_ref.shape, bf16)

        @pl.when(active[side * 8 + step] != 0)
        def _():
            key, value = k_ref[0, 0], v_ref[0, 0]
            allowed = allowed_mask(pos_ref[...], start_ref[...], kpos_ref[0, side])
            dk = jnp.zeros((GROUP, HEAD_SIZE), f32)
            dv = jnp.zeros((GROUP, HEAD_SIZE), f32)
            for head in range(2):
                cols = slice(head * HEAD_SIZE, (head + 1) * HEAD_SIZE)
                query, dout = q_ref[:, cols], dout_ref[:, cols]
                scores = times_transposed(query, key)
                weights_p = jnp.where(allowed, jnp.exp(scores - lse_ref[head]), 0.0)
                dprobs = times_transposed(dout, value)
                dscores = (weights_p * (dprobs - delta[head])).astype(bf16)
                dq_ref[:, cols] += product(dscores, key)
                dk = dk + inner_rows(dscores, query)
                dv = dv + inner_rows(weights_p.astype(bf16), dout)
            dk_ref[0, 0] = dk.astype(bf16)
            dv_ref[0, 0] = dv.astype(bf16)


def whole(shape):
    return pl.BlockSpec(shape, lambda i, *refs: (0,) * len(shape))


def key_spec():
    return pl.BlockSpec((1, 1, GROUP, HEAD_SIZE), lambda i, active: (i // 4, i % 4, 0, 0))


def value_spec():
    return pl.BlockSpec((1, 1, GROUP, HEAD_SIZE), lambda i, active: (i % 4, i // 4, 0, 0))


def common_specs():
    return [
        whole((GROUP, GROUP)),
        whole((GROUP, 1)),
        whole((GROUP, 1)),
        pl.BlockSpec((1, 2, 1, GROUP), lambda i, active: (i, 0, 0, 0)),
        key_spec(),
        key_spec(),
        value_spec(),
        value_spec(),
    ]


def attend(active, *operands):
    return pl.pallas_call(
        attend_kernel,
        grid_spec=pltpu.PrefetchScalarGridSpec(
            num_scalar_prefetch=1,
            grid=(8,),
            in_specs=common_specs(),
            out_specs=[whole((GROUP, GROUP)), whole((2, GROUP, 1))],
            scratch_shapes=[
                pltpu.VMEM((2, GROUP, 1), f32),
                pltpu.VMEM((2, GROUP, 1), f32),
                pltpu.VMEM((2, GROUP, HEAD_SIZE), f32),
            ],
        ),
        out_shape=[
            jax.ShapeDtypeStruct((GROUP, GROUP), f32),
            jax.ShapeDtypeStruct((2, GROUP, 1), f32),
        ],
        compiler_params=pltpu.CompilerParams(vmem_limit_bytes=40 << 20),
        cost_estimate=pl.CostEstimate(flops=6 << 30, bytes_accessed=10 << 20, transcendentals=8 << 20),
        name="attend",
    )(active, *operands)


def attend_back(active, *operands):
    return pl.pallas_call(
        attend_back_kernel,
        grid_spec=pltpu.PrefetchScalarGridSpec(
            num_scalar_prefetch=1,
            grid=(8,),
            in_specs=common_specs() + [whole((GROUP, GROUP)), whole((2, GROUP, 1)), whole((GROUP, GROUP))],
            out_specs=[whole((GROUP, GROUP)), key_spec(), key_spec(), value_spec(), value_spec()],
            scratch_shapes=[pltpu.VMEM((2, GROUP, 1), f32)],
        ),
        out_shape=[jax.ShapeDtypeStruct((GROUP, GROUP), f32)]
        + [jax.ShapeDtypeStruct((2, 4, GROUP, HEAD_SIZE), bf16)] * 2
        + [jax.ShapeDtypeStruct((4, 2, GROUP, HEAD_SIZE), bf16)] * 2,
        compiler_params=pltpu.CompilerParams(vmem_limit_bytes=40 << 20),
        cost_estimate=pl.CostEstimate(flops=12 << 30, bytes_accessed=20 << 20, transcendentals=8 << 20),
        name="attend_back",
    )(active, *operands)


def local(
    hidden_in,
    gain_attn,
    gain_ffn,
    w_query,
    w_key,
    w_value,
    w_out,
    w_gate,
    w_up,
    w_down,
    qkv_shrink,
    query_expand,
    key_expand,
    value_expand,
    out_shrink,
    out_expand,
    gateup_shrink,
    gate_expand,
    up_expand,
    down_shrink,
    down_expand,
    lengths,
    adapter,
    packed_pos,
    cotangent,
):
    zh, zl, x, y, c = (lax.axis_index(name) for name in ALL)
    row = 2 * zh + c
    mine, other = 2 * y + c, 2 * y + 1 - c
    factor = HEAD_SIZE ** (-0.5)
    rank = out_shrink.shape[1]

    def to_rows(value):
        own = lax.dynamic_slice_in_dim(value, c * HALF, HALF, 0)
        sent = lax.dynamic_slice_in_dim(value, (1 - c) * HALF, HALF, 0)
        return jnp.concatenate([own, swap_cores(sent)], axis=0)

    def from_rows(value):
        own, got = value[:HALF], swap_cores(value[HALF:])
        return jnp.where(c == 0, jnp.concatenate([own, got], 0), jnp.concatenate([got, own], 0))

    hidden = to_rows(hidden_in)
    cot = to_rows(cotangent)

    def roll(array, by, axis):
        return lax.dynamic_slice_in_dim(jnp.concatenate([array, array], axis), by, array.shape[axis], axis)

    spread = packed_pos.reshape(2, 2, 4, 4, 2, 2, HALF)
    spread = jnp.transpose(spread, (0, 5, 1, 2, 3, 4, 6))
    rows_pos = jnp.stack([spread[:, 0], spread[:, 1, :, :, :, ::-1]], axis=1).reshape(4, 2, 4, 4, 128)
    rows_pos = roll(roll(roll(rows_pos, zl, 1), x, 2), y, 3).reshape(4, 8, GROUP)
    own_row = lax.dynamic_index_in_dim(rows_pos, row, 0, keepdims=False)
    prev_row = lax.dynamic_index_in_dim(rows_pos, jnp.maximum(row - 1, 0), 0, keepdims=False)
    prev_row = jnp.where(row == 0, far, prev_row)
    key_pos = jnp.stack([prev_row, own_row], axis=1)
    group_pos = own_row[0]
    seq_ends = jnp.cumsum(lengths)
    starts = seq_ends - lengths
    member = (group_pos[:, None] >= starts[None, :]) & (group_pos[:, None] < seq_ends[None, :])
    member_int = member.astype(jnp.int32)
    group_start = jnp.sum(member_int * starts[None, :], axis=1)
    group_owner = jnp.sum(member_int * adapter[None, :], axis=1)
    low, high = jnp.min(group_start), jnp.max(group_pos)
    active = (jnp.min(key_pos, axis=2) <= high) & (jnp.max(key_pos, axis=2) >= low)
    active = jnp.transpose(active).reshape(16).astype(jnp.int32)
    columns = jnp.arange(rank, dtype=jnp.int32) // RANK
    select_g = (group_owner[:, None] == columns[None, :]).astype(f32)
    select = select_g[:128]
    cos_table, sin_table = rope_tables(group_pos - group_start, HEAD_SIZE)

    def column_slices(weight):
        rows_here, width = weight.shape
        parts = jnp.transpose(weight.reshape(rows_here, 16, 8, width // 128), (2, 0, 1, 3))
        return parts.reshape(8, rows_here, width // 8)

    heads_q = w_query.reshape(16, 4, 512)
    heads_kv = jnp.concatenate([w_key.reshape(16, 4, 256), w_value.reshape(16, 4, 256)], axis=2)
    qkv_parts = jnp.transpose(jnp.stack([heads_q, heads_kv], axis=2), (1, 2, 0, 3)).reshape(8, 16, 512)
    parts = jnp.concatenate([qkv_parts, column_slices(w_gate), column_slices(w_up)], axis=2)
    parts = lax.all_to_all(parts, ("y", "c"), split_axis=0, concat_axis=0, tiled=True).reshape(128, 2560)
    first = gather_ring(gather_ring(parts[:, :256], "x"), "z").reshape(2048, 256)
    second = jnp.swapaxes(gather_ring(gather_ring(parts[:, 256:512], "z"), "x"), 0, 1).reshape(2048, 256)
    qkv_mine = jnp.concatenate([first, second], axis=1)
    qkv_other = swap_cores(qkv_mine)
    wo = lax.all_gather(w_out, ALL, axis=0, tiled=True)
    wd_mine = lax.all_gather(w_down, PLANE, axis=0, tiled=True)
    wgu_mine = lax.all_gather(parts[:, 512:], PLANE, axis=0, tiled=True)
    wgu_other, wd_other = swap_cores(wgu_mine), swap_cores(wd_mine)

    def columns_of(array, width):
        return lax.dynamic_slice_in_dim(array, y * width, width, 1)

    inputs = hidden.astype(f32)
    scale_in = row_scale(inputs)
    normed = (inputs * scale_in * gain_attn).astype(bf16)
    normed_g = gather_near(normed, "y")
    cot_g = gather_near(cot, "y")
    q_expand = columns_of(query_expand, 512)
    k_expand = columns_of(key_expand, 256)
    v_expand = columns_of(value_expand, 256)
    low_qkv = (product(normed_g, qkv_shrink) * jnp.tile(select_g, (1, 3))).astype(bf16)
    lin_mine, lin_other = product(normed_g, qkv_mine), product(normed_g, qkv_other)
    query_lin = jnp.where(c == 0, lin_mine, lin_other) + product(low_qkv[:, :rank], q_expand)
    kv_lin = jnp.where(c == 0, lin_other, lin_mine)
    key_lin = kv_lin[:, :256] + product(low_qkv[:, rank : 2 * rank], k_expand)
    value_lin = kv_lin[:, 256:] + product(low_qkv[:, 2 * rank :], v_expand)
    query_heads = query_lin.reshape(GROUP, 2, HEAD_SIZE)
    key_heads = key_lin.reshape(GROUP, 1, HEAD_SIZE)
    query = (query_heads * cos_table + rotate(query_heads) * sin_table).astype(bf16)
    query = (query * bf16(factor)).reshape(GROUP, 512)
    key = (key_heads * cos_table + rotate(key_heads) * sin_table).astype(bf16).reshape(GROUP, 256)

    k_own, k_ahead = gather_keys(key)
    v_own, v_ahead = gather_values(value_lin.astype(bf16))
    k_prev, v_prev = row_before(k_own, k_ahead, c), row_before(v_own, v_ahead, c)
    attended = (
        query,
        group_pos[:, None],
        group_start[:, None],
        key_pos.reshape(8, 2, 1, GROUP),
        k_prev,
        k_own,
        v_prev,
        v_own,
    )
    mixed_f, lse = attend(active, *attended)
    mixed = mixed_f.astype(bf16)

    heads = jnp.zeros((4, 128, 512), bf16)
    heads = lax.dynamic_update_index_in_dim(heads, mixed[:128], y, 0)
    for step in (1, 2, 3):
        got = shift(mixed[step * 128 : (step + 1) * 128], "y", step)
        heads = lax.dynamic_update_index_in_dim(heads, got, (y - step) % 4, 0)
    mixed_tok = jnp.transpose(heads, (1, 0, 2)).reshape(128, 2048)
    low_out = (product(mixed_tok, out_shrink) * select).astype(bf16)
    middle = inputs + product(mixed_tok, wo) + product(low_out, out_expand)
    scale_mid = row_scale(middle)
    normed_mid = (middle * scale_mid * gain_ffn).astype(bf16)
    normed_mid_g = gather_near(normed_mid, "y")

    select_two = jnp.tile(select_g, (1, 2))
    low_gu = (product(normed_mid_g, gateup_shrink) * select_two).astype(bf16)
    grad_low_down = (times_transposed(cot_g, down_expand) * select_g).astype(bf16)
    result = jnp.zeros((GROUP, 2048), f32)
    low_down_part = jnp.zeros((GROUP, rank), f32)
    grad_mid_part = jnp.zeros((GROUP, 2048), f32)
    grad_low_part = jnp.zeros((GROUP, 2 * rank), f32)
    unit_grads = []
    units = 1024
    for wgu, wd, at in ((wgu_mine, wd_mine, mine), (wgu_other, wd_other, other)):
        wg, wu = wgu[:, :units], wgu[:, units:]
        g_expand = lax.dynamic_slice_in_dim(gate_expand.reshape(rank, 16, 8, 64), at, 1, 2).reshape(rank, units)
        u_expand = lax.dynamic_slice_in_dim(up_expand.reshape(rank, 16, 8, 64), at, 1, 2).reshape(rank, units)
        d_shrink = lax.dynamic_slice_in_dim(down_shrink.reshape(16, 8, 64, rank), at, 1, 1).reshape(units, rank)
        gate_pre = product(normed_mid_g, wg) + product(low_gu[:, :rank], g_expand)
        up_pre = product(normed_mid_g, wu) + product(low_gu[:, rank:], u_expand)
        sigmoid_g = jax.nn.sigmoid(gate_pre)
        silu_gate = gate_pre * sigmoid_g
        active_units = (silu_gate * up_pre).astype(bf16)
        result = result + product(active_units, wd)
        low_down_part = low_down_part + product(active_units, d_shrink)
        grad_active = times_transposed(cot_g, wd) + times_transposed(grad_low_down, d_shrink)
        grad_gate = (grad_active * up_pre * sigmoid_g * (1.0 + gate_pre * (1.0 - sigmoid_g))).astype(bf16)
        grad_up = (grad_active * silu_gate).astype(bf16)
        grad_mid_part = grad_mid_part + times_transposed(grad_gate, wg) + times_transposed(grad_up, wu)
        grad_low_part = grad_low_part + jnp.concatenate(
            [times_transposed(grad_gate, g_expand), times_transposed(grad_up, u_expand)], axis=1
        )
        unit_grads.append(
            (
                inner_rows(grad_gate, low_gu[:, :rank]),
                inner_rows(grad_up, low_gu[:, rank:]),
                inner_rows(active_units, grad_low_down),
            )
        )

    def sum_tokens(part):
        sent = part.astype(bf16)
        return sum_near([sent[i * 128 : (i + 1) * 128] for i in range(4)])

    back_low = sum_tokens(grad_low_part)
    back = sum_tokens(grad_mid_part)
    ahead_low = sum_tokens(low_down_part)
    ahead = sum_tokens(result)
    low_down = (ahead_low * select).astype(bf16)
    output = (middle + ahead + product(low_down, down_expand)).astype(bf16)
    grad_low_gu = (back_low * jnp.tile(select, (1, 2))).astype(bf16)
    grad_normed_mid = back + times_transposed(grad_low_gu, gateup_shrink)
    cot_f = cot.astype(f32)
    grad_middle = cot_f + norm_back(middle, scale_mid, gain_ffn, grad_normed_mid)
    grad_attn_out = grad_middle.astype(bf16)
    grad_low_out = (times_transposed(grad_attn_out, out_expand) * select).astype(bf16)
    grad_mixed = (times_transposed(grad_attn_out, wo) + times_transposed(grad_low_out, out_shrink)).astype(bf16)

    def slices_near(array):
        def columns_at(step):
            return lax.dynamic_slice_in_dim(array, ((y + step) % 4) * 512, 512, 1)

        return jnp.concatenate([columns_at(0)] + [shift(columns_at(4 - step), "y", -step) for step in (1, 2, 3)])

    dout = slices_near(grad_mixed)
    dq, dk_prev, dk_own, dv_prev, dv_own = attend_back(active, *attended, mixed_f, lse, dout)
    dk, dv = sum_keys(dk_own, dk_prev, c), sum_values(dv_own, dv_prev, c)
    query_back = (dq * factor).astype(bf16).astype(f32).reshape(GROUP, 2, HEAD_SIZE)
    key_back = dk.astype(bf16).astype(f32).reshape(GROUP, 1, HEAD_SIZE)
    grad_value = dv.astype(bf16)
    grad_query = (query_back * cos_table - rotate(query_back * sin_table)).astype(bf16).reshape(GROUP, 512)
    grad_key = (key_back * cos_table - rotate(key_back * sin_table)).astype(bf16).reshape(GROUP, 256)
    grad_kv = jnp.concatenate([grad_key, grad_value], axis=1)

    grad_low_part = jnp.concatenate(
        [
            times_transposed(grad_query, q_expand),
            times_transposed(grad_key, k_expand),
            times_transposed(grad_value, v_expand),
        ],
        axis=1,
    )
    grad_low_qkv = (sum_tokens(grad_low_part) * jnp.tile(select, (1, 3))).astype(bf16)
    for_mine = jnp.where(c == 0, grad_query, grad_kv)
    for_other = jnp.where(c == 0, grad_kv, grad_query)
    grad_normed_part = times_transposed(for_mine, qkv_mine) + times_transposed(for_other, qkv_other)
    grad_normed = sum_tokens(grad_normed_part) + times_transposed(grad_low_qkv, qkv_shrink)
    grad_input = (grad_middle + norm_back(inputs, scale_in, gain_attn, grad_normed)).astype(bf16)

    def features(array):
        return lax.dynamic_slice_in_dim(array, y * 512, 512, 1)

    def by_halves(pair_at):
        own, others = unit_grads[0][pair_at], unit_grads[1][pair_at]
        own, others = own.reshape(16, 1, 64, rank), others.reshape(16, 1, 64, rank)
        ordered = jnp.where(c == 0, jnp.concatenate([own, others], 1), jnp.concatenate([others, own], 1))
        return ordered.reshape(32, 64, rank)

    def by_rows(array):
        return array.reshape(32, array.shape[0] // 32, rank)

    low_near = gather_near(jnp.concatenate([low_down, grad_low_gu, grad_low_out, low_out], axis=1), "y")
    low_down_g, grad_low_gu_g = low_near[:, :rank], low_near[:, rank : 3 * rank]
    grad_low_out_g, low_out_g = low_near[:, 3 * rank : 4 * rank], low_near[:, 4 * rank :]
    grad_gateup = inner_rows(features(normed_mid_g), grad_low_gu_g)
    early = [
        by_halves(0),
        by_halves(1),
        by_halves(2),
        by_rows(inner_rows(mixed, grad_low_out_g)),
        by_rows(inner_rows(slices_near(grad_attn_out), low_out_g)),
        by_rows(inner_rows(features(cot_g), low_down_g)),
        by_rows(grad_gateup[:, :rank]),
        by_rows(grad_gateup[:, rank:]),
    ]
    early_sum = lax.psum_scatter(
        jnp.concatenate(early, axis=1), PLANE + ("c",), scatter_dimension=0, tiled=False
    )
    early_all = lax.all_gather(early_sum.astype(bf16), ALL, axis=0, tiled=False)

    grad_qkv = inner_rows(features(normed_g), gather_near(grad_low_qkv, "y"))
    late = [
        by_rows(inner_rows(grad_query, low_qkv[:, :rank])),
        by_rows(inner_rows(grad_key, low_qkv[:, rank : 2 * rank])),
        by_rows(inner_rows(grad_value, low_qkv[:, 2 * rank :])),
        by_rows(grad_qkv[:, :rank]),
        by_rows(grad_qkv[:, rank : 2 * rank]),
        by_rows(grad_qkv[:, 2 * rank :]),
    ]
    terms = jnp.concatenate(late, axis=1)
    terms = terms.reshape(16, 2, terms.shape[1], rank)
    kept = lax.dynamic_index_in_dim(terms, c, 1, keepdims=False)
    given = lax.dynamic_index_in_dim(terms, 1 - c, 1, keepdims=False).astype(bf16)
    terms = (kept + swap_cores(given).astype(f32)).reshape(4, 4, -1, rank)
    late_sum = sum_ring(sum_ring(terms, "z"), "x").astype(bf16)
    late_all = gather_ring(gather_ring(gather_ring(late_sum, "x"), "z"), "y")
    late_other = swap_cores(late_all)
    late_all = jnp.where(c == 0, jnp.stack([late_all, late_other], 3), jnp.stack([late_other, late_all], 3))

    def cut(array, axis, pieces):
        found, at = [], 0
        for piece in pieces:
            found.append(lax.slice_in_dim(array, at, at + piece.shape[1], axis=axis).astype(f32))
            at += piece.shape[1]
        return found

    def rows_order(array):
        ordered = jnp.transpose(array.reshape(16, 4, 2, array.shape[1], rank), (1, 0, 2, 3, 4))
        return ordered.reshape(-1, rank)

    early_found = cut(early_all, 1, early)
    g_gate, g_up, g_down_shrink = (array.reshape(-1, rank) for array in early_found[:3])
    g_out_shrink, g_out_expand, g_down_expand, g_gate_low, g_up_low = (rows_order(a) for a in early_found[3:])
    g_q, g_k, g_v, g_q_low, g_k_low, g_v_low = (a.reshape(-1, rank) for a in cut(late_all, 4, late))
    return (
        from_rows(output),
        from_rows(grad_input),
        jnp.concatenate([g_q_low, g_k_low, g_v_low], axis=1),
        g_q.T,
        g_k.T,
        g_v.T,
        g_out_shrink,
        g_out_expand.T,
        jnp.concatenate([g_gate_low, g_up_low], axis=1),
        g_gate.T,
        g_up.T,
        g_down_shrink,
        g_down_expand.T,
    )


def solution(mesh):
    fine = Mesh(mesh.devices.reshape(2, 2, 4, 4, 2), ALL)
    split = P(ALL, None)
    placed = (split, P(), P()) + (split,) * 7 + (P(),) * 14 + (split,)
    return jax.shard_map(
        local,
        mesh=fine,
        in_specs=placed,
        out_specs=(split, split) + (P(),) * 11,
        check_vma=False,
    )
```

time: 1050 us -> 898 us (0.86)
  waiting for transfers between devices: 509 us -> 351 us
  starting transfers between devices: 39.4 us -> 175 us
  blocking collectives: 89.5 us -> 16.8 us
  local copies, waits for them, and re-layouts: 177 us -> 118 us
  other arithmetic: 51.6 us -> 72.5 us
    all_gather x7 -> x2, waiting for transfers between devices: 233 us -> 0.01 us  [the longest x1 0.01 us: local(): wgu_mine = lax.all_gather(parts[:, 512:], PLANE, axis=0, tiled=True)]
    ppermute x9 -> x103, waiting for transfers between devices: 48.7 us -> 265 us  [the longest x81 207 us: shift(): lax.ppermute(value, RING[ring], [(i, (i + step) % 4) for i in range(4)])]
    ppermute x9 -> x103, starting transfers between devices: 12.2 us -> 162 us  [the longest x81 104 us: shift(): lax.ppermute(value, RING[ring], [(i, (i + step) % 4) for i in range(4)])]
    all_gather x1, waiting for transfers between devices: 67.9 us -> 0.02 us  [local(): wo = lax.all_gather(w_out, ALL, axis=0, tiled=True)]
    all_gather x5 -> x0, blocking collectives: 52.5 us -> none  [gather_y(): return lax.all_gather(value, 'y', axis=0, tiled=True)]
    all_gather x1, waiting for transfers between devices: 47.8 us -> 0.01 us  [local(): wd_mine = lax.all_gather(w_down, PLANE, axis=0, tiled=True)]
    unnamed x257 -> x266, local copies, waits for them, and re-layouts: 80.8 us -> 55 us
    reduce_scatter x2 -> x1, waiting for transfers between devices: 108 us -> 83.9 us  [local(): lax.psum_scatter(jnp.concatenate(early, axis=1), PLANE + ('c',), scatter_...]
  transfers between devices with their start and end apart: 31 -> 117, of which waited for: 20 -> 52; matrix products, arithmetic and copies ran while one was open for 19% -> 24% of each run, Pallas kernels for 2% -> 4%
where the time goes in v2:
time: 898 us; the launch traced here: 896 us
  waiting for transfers between devices  351 us (39%)
  starting transfers between devices  175 us (19%)
  local copies, waits for them, and re-layouts  118 us (13%)
  matrix products  113 us (13%)
  other arithmetic  72.5 us (8%)
  Pallas kernels  32.7 us (4%)
  between operations  17.2 us (2%)
  blocking collectives  16.8 us (2%)
    ppermute x81, waiting for transfers between devices, shift(): lax.ppermute(value, RING[ring], [(i, (i + step) % 4) for i in range(4)])  207 us
    ppermute x81, starting transfers between devices, shift(): lax.ppermute(value, RING[ring], [(i, (i + step) % 4) for i in range(4)])  104 us
    reduce_scatter x1, waiting for transfers between devices, local(): lax.psum_scatter(jnp.concatenate(early, axis=1), PLANE + ('c',), scatter_...  83.9 us
    unnamed x266, local copies, waits for them, and re-layouts  55 us
    dot_general x23, matrix products, product(): return jnp.dot(left, right, preferred_element_type=f32)  50.4 us
    dot_general x23, matrix products, times_transposed(): lax.dot_general(left, right, (((1,), (1,)), ((), ())), preferred_element_...  49.7 us
    ppermute x6, starting transfers between devices, shift_ahead(): lax.ppermute(value, ROW_AHEAD, [(8 + 2 * i, 8 + 2 * ((i + step) % 4)) for...  18.9 us
  transfers between devices with their start and end apart: 117, of which 52 were waited for; matrix products, arithmetic and copies ran while one was open for 24% of the time, Pallas kernels for 4%

profile of v2, /device:TPU:1, one launch (start us, length us, event | category | flops | bytes accessed | tf_op | source)
XLA Modules:
  0.0 895.6 jit_solution(5459496412902335829)
XLA Ops:
  11.3 16.8 %all_to_all.5 = bf16[8,16,2560]{2,1,0:T(8,128)(2,1)S(1)} all-to-all(bf16[8,16,2560]{2,1,0:T(8,128)(2,1)S(1)} %pad_maximum_fusion.7), channel_id=1, replica_groups=mesh['zh'=2,'zl'=2,'x'=4,'y'=4,'c'=2] {'y','c'}, dimensions={0} | all-to-all | bytes 1310720 | tf_op jit(solution)/shard_map/all_to_all | solution.py:431
  34.6 4.1 copy.354
  47.6 3.8 collective-permute-start.10
  54.9 3.8 collective-permute-start.7
  61.1 3.3 collective-permute-start.13
  64.5 5.0 collective-permute-done.7
  74.1 4.2 collective-permute-done.9
  78.5 5.7 collective-permute-done.15
  94.7 4.1 copy.353
  104.1 8.7 collective-permute-done.1
  112.8 4.4 collective-permute-done.3
  122.7 4.2 broadcast_select_fusion
  127.9 3.6 collective-permute-start.29
  137.2 6.7 collective-permute-done.29
  151.7 5.9 collective-permute-done.19
  157.6 3.2 collective-permute-start.32
  165.7 6.7 collective-permute-done.30
  173.8 11.1 %collective-permute-done.32 = bf16[1,2,512,256]{3,2,1,0:T(8,128)(2,1)S(1)} collective-permute-done((bf16[1,2,512,256]{3,2,1,0:T(8,128)(2,1)S(1)}, bf16[1,2,512,256]{3,2,1,0:T(8,128)(2,1)S(1)}, u32[]{:S(2)}, u32[]{:S(2)}) %collective-permute-start.32) | collective-permute-done | bytes 524320 | tf_op jit(solution)/shard_map/ppermute | solution.py:73
  187.8 7.2 collective-permute-start.24
  205.8 12.3 %collective-permute-start.27 = (bf16[2,512,256]{2,1,0:T(8,128)(2,1)}, bf16[2,512,256]{2,1,0:T(8,128)(2,1)}, u32[]{:S(2)}, u32[]{:S(2)}) collective-permute-start(bf16[2,512,256]{2,1,0:T(8,128)(2,1)} %get-tuple-element.198), channel_id=1, source_target_pairs={{64,80},{72,88},{80,64},{88,72},{66,82},{74,90},{82,66},{90,74},{6... | collective-permute-start | bytes 1572872 | tf_op jit(solution)/shard_map/ppermute | solution.py:122
  223.2 11.0 %collective-permute-start.20 = (bf16[4,512,256]{2,1,0:T(8,128)(2,1)}, bf16[4,512,256]{2,1,0:T(8,128)(2,1)}, u32[]{:S(2)}, u32[]{:S(2)}) collective-permute-start(bf16[4,512,256]{2,1,0:T(8,128)(2,1)} %copy-done.69), channel_id=1, source_target_pairs={{1,64},{33,96},{3,66},{35,98},{5,68},{37,100},{7,70},{39,102},{9,7... | collective-permute-start | bytes 3145736 | tf_op jit(solution)/shard_map/ppermute | solution.py:128
  241.0 3.6 maximum_select_fusion.2.vprev_ref
  244.7 12.2 %collective-permute-done.20 = bf16[4,512,256]{2,1,0:T(8,128)(2,1)} collective-permute-done((bf16[4,512,256]{2,1,0:T(8,128)(2,1)}, bf16[4,512,256]{2,1,0:T(8,128)(2,1)}, u32[]{:S(2)}, u32[]{:S(2)}) %collective-permute-start.20) | collective-permute-done | bytes 1048608 | tf_op jit(solution)/shard_map/ppermute | solution.py:128
  256.8 11.4 %collective-permute-done.21 = bf16[4,512,256]{2,1,0:T(8,128)(2,1)} collective-permute-done((bf16[4,512,256]{2,1,0:T(8,128)(2,1)}, bf16[4,512,256]{2,1,0:T(8,128)(2,1)}, u32[]{:S(2)}, u32[]{:S(2)}) %collective-permute-start.21) | collective-permute-done | bytes 1048608 | tf_op jit(solution)/shard_map/ppermute | solution.py:128
  271.1 16.0 %attend.1 = (f32[512,512]{1,0:T(8,128)S(1)}, f32[2,512,1]{2,1,0:T(8,128)S(1)}) custom-call(s32[16]{0:T(128)S(1)} %reshape.515.active, bf16[512,512]{1,0:T(8,128)(2,1)S(1)} %fusion.61.q_ref, s32[512,1]{1,0:T(8,128)S(1)} %copy.346.pos_ref, s32[512,1]{1,0:T(8,128)S(1)} %copy.347.start_ref, s32[8,2,1,512]{3,2,1,0:T(1,128)S(1)} %reshape.469.kpos_ref, ...), custom_call_target="tpu_custom_call" | custom-call | flops 6442450944 | bytes 10485760 | tf_op jit(solution)/shard_map/attend/pallas_call | solution.py:309
  307.6 6.5 convolution_add_fusion.3
  314.2 5.3 multiply_reduce_fusion.1
  322.2 6.1 convolution_add_fusion.2
  328.3 4.6 collective-permute-done.37
  334.3 12.2 %collective-permute-done.39 = bf16[128,2048]{1,0:T(8,128)(2,1)S(1)} collective-permute-done((bf16[128,2048]{1,0:T(8,128)(2,1)S(1)}, bf16[128,2048]{1,0:T(8,128)(2,1)S(1)}, u32[]{:S(2)}, u32[]{:S(2)}) %collective-permute-start.39) | collective-permute-done | bytes 524320 | tf_op jit(solution)/shard_map/ppermute | solution.py:73
  351.3 3.4 multiply_convert_fusion.3
  361.4 4.6 fusion.246
  370.8 6.1 fusion.34
  376.8 6.2 multiply_convert_fusion.1
  387.1 4.8 add_convert_fusion.2
  399.7 4.6 fusion.4
  404.2 4.8 add_convert_fusion.1
  417.4 17.8 %collective-permute-done.56 = bf16[128,256]{0,1:T(8,128)(2,1)S(1)} collective-permute-done((bf16[128,256]{0,1:T(8,128)(2,1)S(1)}, bf16[128,256]{0,1:T(8,128)(2,1)S(1)}, u32[]{:S(2)}, u32[]{:S(2)}) %collective-permute-start.56) | collective-permute-done | bytes 65568 | tf_op jit(solution)/shard_map/ppermute | solution.py:73
  443.0 9.4 %collective-permute-done.42 = bf16[128,2048]{1,0:T(8,128)(2,1)S(1)} collective-permute-done((bf16[128,2048]{1,0:T(8,128)(2,1)S(1)}, bf16[128,2048]{1,0:T(8,128)(2,1)S(1)}, u32[]{:S(2)}, u32[]{:S(2)}) %collective-permute-start.42) | collective-permute-done | bytes 524320 | tf_op jit(solution)/shard_map/ppermute | solution.py:73
  452.4 12.4 %collective-permute-done.43 = bf16[128,2048]{1,0:T(8,128)(2,1)S(1)} collective-permute-done((bf16[128,2048]{1,0:T(8,128)(2,1)S(1)}, bf16[128,2048]{1,0:T(8,128)(2,1)S(1)}, u32[]{:S(2)}, u32[]{:S(2)}) %collective-permute-start.43) | collective-permute-done | bytes 524320 | tf_op jit(solution)/shard_map/ppermute | solution.py:73
  475.6 5.5 collective-permute-done.108
  490.2 6.3 fusion.255
  502.5 3.8 collective-permute-done.61
  507.2 83.9 %reduce-scatter.2.cloned.1.call-done = f32[1,272,128]{2,1,0:T(8,128)} async-done(((f32[32,272,128]{2,1,0:T(8,128)}), f32[1,272,128]{2,1,0:T(8,128)}) %reduce-scatter.2.cloned.1.call-update) | async-done | bytes 139280 | tf_op jit(solution)/shard_map/reduce_scatter | solution.py:603
  596.9 16.8 %attend_back.1 = (f32[512,512]{1,0:T(8,128)S(1)}, bf16[2,4,512,256]{3,2,1,0:T(8,128)(2,1)}, bf16[2,4,512,256]{3,2,1,0:T(8,128)(2,1)S(1)}, bf16[4,2,512,256]{3,2,1,0:T(8,128)(2,1)}, bf16[4,2,512,256]{3,2,1,0:T(8,128)(2,1)S(1)}) custom-call(s32[16]{0:T(128)S(1)} %reshape.515.active, bf16[512,512]{1,0:T(8,128)(2,1)S(1)} %fusion.61.q_ref, ...), custom_call_target="tpu_custom_call" | custom-call | flops 12884901888 | bytes 20971520 | tf_op jit(solution)/shard_map/attend_back/pallas_call | solution.py:333
  635.3 3.1 slice_bitcast_fusion.3
  647.9 6.3 collective-permute-start.71
  657.4 14.3 %collective-permute-done.70 = bf16[2,512,256]{2,1,0:T(8,128)(2,1)S(1)} collective-permute-done((bf16[2,512,256]{2,1,0:T(8,128)(2,1)S(1)}, bf16[2,512,256]{2,1,0:T(8,128)(2,1)S(1)}, u32[]{:S(2)}, u32[]{:S(2)}) %collective-permute-start.70) | collective-permute-done | bytes 524320 | tf_op jit(solution)/shard_map/ppermute | solution.py:73
  673.0 11.0 %collective-permute-done.71 = bf16[2,512,256]{2,1,0:T(8,128)(2,1)S(1)} collective-permute-done((bf16[2,512,256]{2,1,0:T(8,128)(2,1)S(1)}, bf16[2,512,256]{2,1,0:T(8,128)(2,1)S(1)}, u32[]{:S(2)}, u32[]{:S(2)}) %collective-permute-start.71) | collective-permute-done | bytes 524320 | tf_op jit(solution)/shard_map/ppermute | solution.py:73
  686.7 12.3 %collective-permute-done.77 = bf16[512,256]{1,0:T(8,128)(2,1)S(1)} collective-permute-done((bf16[512,256]{1,0:T(8,128)(2,1)S(1)}, bf16[512,256]{1,0:T(8,128)(2,1)S(1)}, u32[]{:S(2)}, u32[]{:S(2)}) %collective-permute-start.77) | collective-permute-done | bytes 262176 | tf_op jit(solution)/shard_map/ppermute | solution.py:168
  702.2 14.0 %collective-permute-done.73 = bf16[512,256]{1,0:T(8,128)(2,1)} collective-permute-done((bf16[512,256]{1,0:T(8,128)(2,1)S(1)}, bf16[512,256]{1,0:T(8,128)(2,1)}, u32[]{:S(2)}, u32[]{:S(2)}) %collective-permute-start.73) | collective-permute-done | bytes 262176 | tf_op jit(solution)/shard_map/ppermute | solution.py:166
  717.6 3.0 fusion.226
  725.4 9.2 %collective-permute-done.66 = bf16[512,256]{1,0:T(8,128)(2,1)S(1)} collective-permute-done((bf16[512,256]{1,0:T(8,128)(2,1)S(1)}, bf16[512,256]{1,0:T(8,128)(2,1)S(1)}, u32[]{:S(2)}, u32[]{:S(2)}) %collective-permute-start.66) | collective-permute-done | bytes 262176 | tf_op jit(solution)/shard_map/ppermute | solution.py:73
  757.2 4.2 collective-permute-start.89
  773.3 3.2 collective-permute-start.94
  778.0 4.0 collective-permute-start.48
  784.9 11.4 %collective-permute-done.80 = bf16[128,2048]{1,0:T(8,128)(2,1)S(1)} collective-permute-done((bf16[128,2048]{1,0:T(8,128)(2,1)S(1)}, bf16[128,2048]{1,0:T(8,128)(2,1)S(1)}, u32[]{:S(2)}, u32[]{:S(2)}) %collective-permute-start.80) | collective-permute-done | bytes 524320 | tf_op jit(solution)/shard_map/ppermute | solution.py:73
  797.1 3.3 collective-permute-start.97
  814.0 3.8 collective-permute-done.102
  819.8 9.3 %collective-permute-done.104 = bf16[4,4,80,128]{3,2,1,0:T(8,128)(2,1)S(1)} collective-permute-done((bf16[4,4,80,128]{3,2,1,0:T(8,128)(2,1)S(1)}, bf16[4,4,80,128]{3,2,1,0:T(8,128)(2,1)S(1)}, u32[]{:S(2)}, u32[]{:S(2)}) %collective-permute-start.104) | collective-permute-done | bytes 327712 | tf_op jit(solution)/shard_map/ppermute | solution.py:73
  850.6 6.4 fusion.230
  859.4 5.6 copy.387
  865.0 3.9 convert_bitcast_fusion
  868.9 5.6 copy.388
  (715 shorter events, 340.7 us)
Async XLA Ops:
  7.2 237.5 %all-gather.9.cloned.1.call-start = ((), (), s32[]{:S(2)}) async-start(), calls=%async_computation.4 | async-start | bytes 4456448 | tf_op jit(solution)/shard_map/all_gather | solution.py:437
  7.9 306.2 %all-gather.7.cloned.1.call-start = ((), (), s32[]{:S(2)}) async-start(), calls=%async_computation.3 | async-start | bytes 8912896 | tf_op jit(solution)/shard_map/all_gather | solution.py:438
  29.0 285.2 %all-gather.5.cloned.1.call-start = ((), (), s32[]{:S(2)}) async-start(), calls=%async_computation.2 | async-start | bytes 8454144 | tf_op jit(solution)/shard_map/all_gather | solution.py:436
  32.6 67.1 %collective-permute-start.49 = (bf16[64,2048]{1,0:T(8,128)(2,1)}, bf16[64,2048]{1,0:T(8,128)(2,1)}, u32[]{:S(2)}, u32[]{:S(2)}) collective-permute-start(bf16[64,2048]{1,0:T(8,128)(2,1)} %get-tuple-element.190), channel_id=1, source_target_pairs={{0,1},{1,0},{2,3},{3,2},{4,5},{5,4},{6,7},{7,6},{8,9},{9,8},{10,11... | collective-permute-start | bytes 786440 | tf_op jit(solution)/shard_map/ppermute | solution.py:69
  32.8 558.3 %reduce-scatter.2.cloned.1.call-start = ((), (), s32[]{:S(2)}) async-start(), calls=%async_computation.5 | async-start | bytes 4595712 | tf_op jit(solution)/shard_map/reduce_scatter | solution.py:603
  54.9 14.7 %collective-permute-start.7 = (bf16[4,128,256]{2,1,0:T(8,128)(2,1)S(1)}, bf16[4,128,256]{2,1,0:T(8,128)(2,1)S(1)}, u32[]{:S(2)}, u32[]{:S(2)}) collective-permute-start(bf16[4,128,256]{2,1,0:T(8,128)(2,1)S(1)} %bitcast_dynamic-update-slice_fusion.20), channel_id=1, source_target_pairs={{0,96},{32,0},{64,32},{96,64},{1,97},{33,1},{65,33},{97,65},{2,98}... | collective-permute-start | bytes 786440 | tf_op jit(solution)/shard_map/ppermute | solution.py:73
  59.0 19.3 %collective-permute-start.9 = (bf16[4,128,256]{2,1,0:T(8,128)(2,1)S(1)}, bf16[4,128,256]{2,1,0:T(8,128)(2,1)S(1)}, u32[]{:S(2)}, u32[]{:S(2)}) collective-permute-start(bf16[4,128,256]{2,1,0:T(8,128)(2,1)S(1)} %bitcast_dynamic-update-slice_fusion.20), channel_id=1, source_target_pairs={{0,32},{32,64},{64,96},{96,0},{1,33},{33,65},{65,97},{97,1},{2,34}... | collective-permute-start | bytes 786440 | tf_op jit(solution)/shard_map/ppermute | solution.py:73
  61.1 17.2 %collective-permute-start.13 = (bf16[4,128,256]{2,1,0:T(8,128)(2,1)S(1)}, bf16[4,128,256]{2,1,0:T(8,128)(2,1)S(1)}, u32[]{:S(2)}, u32[]{:S(2)}) collective-permute-start(bf16[4,128,256]{2,1,0:T(8,128)(2,1)S(1)} %bitcast_dynamic-update-slice_fusion.16), channel_id=1, source_target_pairs={{0,24},{8,0},{16,8},{24,16},{1,25},{9,1},{17,9},{25,17},{2,26},{10... | collective-permute-start | bytes 786440 | tf_op jit(solution)/shard_map/ppermute | solution.py:73
  85.9 36.7 %collective-permute-start.16 = (bf16[2048,512]{1,0:T(8,128)(2,1)}, bf16[2048,512]{1,0:T(8,128)(2,1)}, u32[]{:S(2)}, u32[]{:S(2)}) collective-permute-start(bf16[2048,512]{1,0:T(8,128)(2,1)} %pad_maximum_fusion.1), channel_id=1, source_target_pairs={{0,1},{1,0},{2,3},{3,2},{4,5},{5,4},{6,7},{7,6},{8,9},{9,8},{10,11... | collective-permute-start | bytes 6291464 | tf_op jit(solution)/shard_map/ppermute | solution.py:69
  88.1 24.7 %collective-permute-start.1 = (bf16[128,2048]{1,0:T(8,128)(2,1)}, bf16[128,2048]{1,0:T(8,128)(2,1)}, u32[]{:S(2)}, u32[]{:S(2)}) collective-permute-start(bf16[128,2048]{1,0:T(8,128)(2,1)} %fusion.45), channel_id=1, source_target_pairs={{0,6},{2,0},{4,2},{6,4},{1,7},{3,1},{5,3},{7,5},{8,14},{10,8},{12,... | collective-permute-start | bytes 1572872 | tf_op jit(solution)/shard_map/ppermute | solution.py:73
  90.3 22.5 %collective-permute-start.2 = (bf16[128,2048]{1,0:T(8,128)(2,1)}, bf16[128,2048]{1,0:T(8,128)(2,1)}, u32[]{:S(2)}, u32[]{:S(2)}) collective-permute-start(bf16[128,2048]{1,0:T(8,128)(2,1)} %fusion.45), channel_id=1, source_target_pairs={{0,4},{2,6},{4,0},{6,2},{1,5},{3,7},{5,1},{7,3},{8,12},{10,14},{12... | collective-permute-start | bytes 1572872 | tf_op jit(solution)/shard_map/ppermute | solution.py:73
  90.7 26.5 %collective-permute-start.3 = (bf16[128,2048]{1,0:T(8,128)(2,1)}, bf16[128,2048]{1,0:T(8,128)(2,1)}, u32[]{:S(2)}, u32[]{:S(2)}) collective-permute-start(bf16[128,2048]{1,0:T(8,128)(2,1)} %fusion.45), channel_id=1, source_target_pairs={{0,2},{2,4},{4,6},{6,0},{1,3},{3,5},{5,7},{7,1},{8,10},{10,12},{12... | collective-permute-start | bytes 1572872 | tf_op jit(solution)/shard_map/ppermute | solution.py:73
  101.8 60.3 %collective-permute-start.50 = (bf16[128,2048]{1,0:T(8,128)(2,1)}, bf16[128,2048]{1,0:T(8,128)(2,1)}, u32[]{:S(2)}, u32[]{:S(2)}) collective-permute-start(bf16[128,2048]{1,0:T(8,128)(2,1)} %pad_maximum_fusion.12), channel_id=1, source_target_pairs={{0,6},{2,0},{4,2},{6,4},{1,7},{3,1},{5,3},{7,5},{8,14},{10,8},{12,... | collective-permute-start | bytes 1572872 | tf_op jit(solution)/shard_map/ppermute | solution.py:73
  127.9 16.0 %collective-permute-start.29 = (bf16[512,256]{1,0:T(8,128)(2,1)S(1)}, bf16[512,256]{1,0:T(8,128)(2,1)S(1)}, u32[]{:S(2)}, u32[]{:S(2)}) collective-permute-start(bf16[512,256]{1,0:T(8,128)(2,1)S(1)} %fusion.71), channel_id=1, source_target_pairs={{0,32},{1,33},{32,0},{33,1},{64,96},{65,97},{96,64},{97,65},{2,34}... | collective-permute-start | bytes 786440 | tf_op jit(solution)/shard_map/ppermute | solution.py:133
  132.7 17.0 %collective-permute-start.17 = (bf16[1,512,256]{2,1,0:T(8,128)(2,1)}, bf16[1,512,256]{2,1,0:T(8,128)(2,1)}, u32[]{:S(2)}, u32[]{:S(2)}) collective-permute-start(bf16[1,512,256]{2,1,0:T(8,128)(2,1)} %get-tuple-element.211), channel_id=1, source_target_pairs={{0,24},{8,0},{16,8},{24,16},{1,25},{9,1},{17,9},{25,17},{2,26},{10... | collective-permute-start | bytes 786440 | tf_op jit(solution)/shard_map/ppermute | solution.py:73
  134.1 17.0 %collective-permute-start.18 = (bf16[1,512,256]{2,1,0:T(8,128)(2,1)}, bf16[1,512,256]{2,1,0:T(8,128)(2,1)}, u32[]{:S(2)}, u32[]{:S(2)}) collective-permute-start(bf16[1,512,256]{2,1,0:T(8,128)(2,1)} %get-tuple-element.211), channel_id=1, source_target_pairs={{0,16},{8,24},{16,0},{24,8},{1,17},{9,25},{17,1},{25,9},{2,18},{10... | collective-permute-start | bytes 786440 | tf_op jit(solution)/shard_map/ppermute | solution.py:73
  134.8 22.8 %collective-permute-start.19 = (bf16[1,512,256]{2,1,0:T(8,128)(2,1)}, bf16[1,512,256]{2,1,0:T(8,128)(2,1)}, u32[]{:S(2)}, u32[]{:S(2)}) collective-permute-start(bf16[1,512,256]{2,1,0:T(8,128)(2,1)} %get-tuple-element.211), channel_id=1, source_target_pairs={{0,8},{8,16},{16,24},{24,0},{1,9},{9,17},{17,25},{25,1},{2,10},{10... | collective-permute-start | bytes 786440 | tf_op jit(solution)/shard_map/ppermute | solution.py:73
  144.6 18.9 %collective-permute-start.51 = (bf16[128,2048]{1,0:T(8,128)(2,1)}, bf16[128,2048]{1,0:T(8,128)(2,1)}, u32[]{:S(2)}, u32[]{:S(2)}) collective-permute-start(bf16[128,2048]{1,0:T(8,128)(2,1)} %pad_maximum_fusion.12), channel_id=1, source_target_pairs={{0,4},{2,6},{4,0},{6,2},{1,5},{3,7},{5,1},{7,3},{8,12},{10,14},{12... | collective-permute-start | bytes 1572872 | tf_op jit(solution)/shard_map/ppermute | solution.py:73
  149.7 22.7 %collective-permute-start.30 = (bf16[1,2,512,256]{3,2,1,0:T(8,128)(2,1)S(1)}, bf16[1,2,512,256]{3,2,1,0:T(8,128)(2,1)S(1)}, u32[]{:S(2)}, u32[]{:S(2)}) collective-permute-start(bf16[1,2,512,256]{3,2,1,0:T(8,128)(2,1)S(1)} %maximum_bitcast_fusion), channel_id=1, source_target_pairs={{0,24},{8,0},{16,8},{24,16},{1,25},{9,1},{17,9},{25,17},{2,26},{10... | collective-permute-start | bytes 1572872 | tf_op jit(solution)/shard_map/ppermute | solution.py:73
  151.1 22.7 %collective-permute-start.31 = (bf16[1,2,512,256]{3,2,1,0:T(8,128)(2,1)S(1)}, bf16[1,2,512,256]{3,2,1,0:T(8,128)(2,1)S(1)}, u32[]{:S(2)}, u32[]{:S(2)}) collective-permute-start(bf16[1,2,512,256]{3,2,1,0:T(8,128)(2,1)S(1)} %maximum_bitcast_fusion), channel_id=1, source_target_pairs={{0,16},{8,24},{16,0},{24,8},{1,17},{9,25},{17,1},{25,9},{2,18},{10... | collective-permute-start | bytes 1572872 | tf_op jit(solution)/shard_map/ppermute | solution.py:73
  157.6 27.3 %collective-permute-start.32 = (bf16[1,2,512,256]{3,2,1,0:T(8,128)(2,1)S(1)}, bf16[1,2,512,256]{3,2,1,0:T(8,128)(2,1)S(1)}, u32[]{:S(2)}, u32[]{:S(2)}) collective-permute-start(bf16[1,2,512,256]{3,2,1,0:T(8,128)(2,1)S(1)} %maximum_bitcast_fusion), channel_id=1, source_target_pairs={{0,8},{8,16},{16,24},{24,0},{1,9},{9,17},{17,25},{25,1},{2,10},{10... | collective-permute-start | bytes 1572872 | tf_op jit(solution)/shard_map/ppermute | solution.py:73
  162.1 34.1 %collective-permute-start.22 = (bf16[4,512,256]{2,1,0:T(8,128)(2,1)S(1)}, bf16[4,512,256]{2,1,0:T(8,128)(2,1)S(1)}, u32[]{:S(2)}, u32[]{:S(2)}) collective-permute-start(bf16[4,512,256]{2,1,0:T(8,128)(2,1)S(1)} %get-tuple-element.163), channel_id=1, source_target_pairs={{0,32},{1,33},{32,0},{33,1},{64,96},{65,97},{96,64},{97,65},{2,34}... | collective-permute-start | bytes 3145736 | tf_op jit(solution)/shard_map/ppermute | solution.py:127
  163.5 24.2 %collective-permute-start.52 = (bf16[128,2048]{1,0:T(8,128)(2,1)}, bf16[128,2048]{1,0:T(8,128)(2,1)S(1)}, u32[]{:S(2)}, u32[]{:S(2)}) collective-permute-start(bf16[128,2048]{1,0:T(8,128)(2,1)} %pad_maximum_fusion.12), channel_id=1, source_target_pairs={{0,2},{2,4},{4,6},{6,0},{1,3},{3,5},{5,7},{7,1},{8,10},{10,12},{12... | collective-permute-start | bytes 1572872 | tf_op jit(solution)/shard_map/ppermute | solution.py:73
  186.4 54.4 %collective-permute-start.33 = (bf16[4,2,512,256]{3,2,1,0:T(8,128)(2,1)}, bf16[4,2,512,256]{3,2,1,0:T(8,128)(2,1)}, u32[]{:S(2)}, u32[]{:S(2)}) collective-permute-start(bf16[4,2,512,256]{3,2,1,0:T(8,128)(2,1)} %pad_maximum_fusion.3.vown_ref), channel_id=1, source_target_pairs={{0,1},{2,3},{4,5},{6,7},{8,9},{10,11},{12,13},{14,15},{16,17},{18,... | collective-permute-start | bytes 6291464 | tf_op jit(solution)/shard_map/ppermute | solution.py:141
  197.8 70.4 %collective-permute-start.23 = (bf16[2,4,512,256]{3,2,1,0:T(8,128)(2,1)}, bf16[2,4,512,256]{3,2,1,0:T(8,128)(2,1)}, u32[]{:S(2)}, u32[]{:S(2)}) collective-permute-start(bf16[2,4,512,256]{3,2,1,0:T(8,128)(2,1)} %pad_maximum_fusion.2.kown_ref), channel_id=1, source_target_pairs={{0,1},{2,3},{4,5},{6,7},{8,9},{10,11},{12,13},{14,15},{16,17},{18,... | collective-permute-start | bytes 6291464 | tf_op jit(solution)/shard_map/ppermute | solution.py:141
  202.6 31.6 %collective-permute-start.26 = (bf16[2,512,256]{2,1,0:T(8,128)(2,1)}, bf16[2,512,256]{2,1,0:T(8,128)(2,1)}, u32[]{:S(2)}, u32[]{:S(2)}) collective-permute-start(bf16[2,512,256]{2,1,0:T(8,128)(2,1)} %get-tuple-element.198), channel_id=1, source_target_pairs={{64,88},{72,64},{80,72},{88,80},{66,90},{74,66},{82,74},{90,82},{6... | collective-permute-start | bytes 1572872 | tf_op jit(solution)/shard_map/ppermute | solution.py:122
  205.8 32.6 %collective-permute-start.27 = (bf16[2,512,256]{2,1,0:T(8,128)(2,1)}, bf16[2,512,256]{2,1,0:T(8,128)(2,1)}, u32[]{:S(2)}, u32[]{:S(2)}) collective-permute-start(bf16[2,512,256]{2,1,0:T(8,128)(2,1)} %get-tuple-element.198), channel_id=1, source_target_pairs={{64,80},{72,88},{80,64},{88,72},{66,82},{74,90},{82,66},{90,74},{6... | collective-permute-start | bytes 1572872 | tf_op jit(solution)/shard_map/ppermute | solution.py:122
  223.2 33.7 %collective-permute-start.20 = (bf16[4,512,256]{2,1,0:T(8,128)(2,1)}, bf16[4,512,256]{2,1,0:T(8,128)(2,1)}, u32[]{:S(2)}, u32[]{:S(2)}) collective-permute-start(bf16[4,512,256]{2,1,0:T(8,128)(2,1)} %copy-done.69), channel_id=1, source_target_pairs={{1,64},{33,96},{3,66},{35,98},{5,68},{37,100},{7,70},{39,102},{9,7... | collective-permute-start | bytes 3145736 | tf_op jit(solution)/shard_map/ppermute | solution.py:128
  234.2 34.0 %collective-permute-start.21 = (bf16[4,512,256]{2,1,0:T(8,128)(2,1)}, bf16[4,512,256]{2,1,0:T(8,128)(2,1)}, u32[]{:S(2)}, u32[]{:S(2)}) collective-permute-start(bf16[4,512,256]{2,1,0:T(8,128)(2,1)} %copy-done.69), channel_id=1, source_target_pairs={{1,96},{33,64},{3,98},{35,66},{5,100},{37,68},{7,102},{39,70},{9,1... | collective-permute-start | bytes 3145736 | tf_op jit(solution)/shard_map/ppermute | solution.py:128
  244.7 77.5 %collective-permute-start.41 = (bf16[1024,2048]{1,0:T(8,128)(2,1)}, bf16[1024,2048]{1,0:T(8,128)(2,1)}, u32[]{:S(2)}, u32[]{:S(2)}) collective-permute-start(bf16[1024,2048]{1,0:T(8,128)(2,1)} %all-gather.9.cloned.1.call-done), channel_id=1, source_target_pairs={{0,1},{1,0},{2,3},{3,2},{4,5},{5,4},{6,7},{7,6},{8,9},{9,8},{10,11... | collective-permute-start | bytes 12582920 | tf_op jit(solution)/shard_map/ppermute | solution.py:69
  314.1 56.6 %collective-permute-start.40 = (bf16[2048,2048]{1,0:T(8,128)(2,1)}, bf16[2048,2048]{1,0:T(8,128)(2,1)}, u32[]{:S(2)}, u32[]{:S(2)}) collective-permute-start(bf16[2048,2048]{1,0:T(8,128)(2,1)} %all-gather.7.cloned.1.call-done), channel_id=1, source_target_pairs={{0,1},{1,0},{2,3},{3,2},{4,5},{5,4},{6,7},{7,6},{8,9},{9,8},{10,11... | collective-permute-start | bytes 25165832 | tf_op jit(solution)/shard_map/ppermute | solution.py:69
  319.8 14.5 %collective-permute-start.38 = (bf16[128,2048]{1,0:T(8,128)(2,1)S(1)}, bf16[128,2048]{1,0:T(8,128)(2,1)S(1)}, u32[]{:S(2)}, u32[]{:S(2)}) collective-permute-start(bf16[128,2048]{1,0:T(8,128)(2,1)S(1)} %multiply_convert_fusion.7), channel_id=1, source_target_pairs={{0,4},{2,6},{4,0},{6,2},{1,5},{3,7},{5,1},{7,3},{8,12},{10,14},{12... | collective-permute-start | bytes 1572872 | tf_op jit(solution)/shard_map/ppermute | solution.py:73
  321.7 24.7 %collective-permute-start.39 = (bf16[128,2048]{1,0:T(8,128)(2,1)S(1)}, bf16[128,2048]{1,0:T(8,128)(2,1)S(1)}, u32[]{:S(2)}, u32[]{:S(2)}) collective-permute-start(bf16[128,2048]{1,0:T(8,128)(2,1)S(1)} %multiply_convert_fusion.7), channel_id=1, source_target_pairs={{0,2},{2,4},{4,6},{6,0},{1,3},{3,5},{5,7},{7,1},{8,10},{10,12},{12... | collective-permute-start | bytes 1572872 | tf_op jit(solution)/shard_map/ppermute | solution.py:73
  394.3 17.3 %collective-permute-start.45 = (bf16[128,128]{0,1:T(8,128)(2,1)}, bf16[128,128]{0,1:T(8,128)(2,1)S(1)}, u32[]{:S(2)}, u32[]{:S(2)}) collective-permute-start(bf16[128,128]{0,1:T(8,128)(2,1)} %get-tuple-element.217), channel_id=1, source_target_pairs={{0,4},{2,6},{4,0},{6,2},{1,5},{3,7},{5,1},{7,3},{8,12},{10,14},{12... | collective-permute-start | bytes 98312 | tf_op jit(solution)/shard_map/ppermute | solution.py:73
  396.1 18.6 %collective-permute-start.46 = (bf16[128,128]{0,1:T(8,128)(2,1)}, bf16[128,128]{0,1:T(8,128)(2,1)S(1)}, u32[]{:S(2)}, u32[]{:S(2)}) collective-permute-start(bf16[128,128]{0,1:T(8,128)(2,1)} %get-tuple-element.219), channel_id=1, source_target_pairs={{0,2},{2,4},{4,6},{6,0},{1,3},{3,5},{5,7},{7,1},{8,10},{10,12},{12... | collective-permute-start | bytes 98312 | tf_op jit(solution)/shard_map/ppermute | solution.py:73
  396.1 20.4 %collective-permute-start.47 = (bf16[128,128]{0,1:T(8,128)(2,1)}, bf16[128,128]{0,1:T(8,128)(2,1)}, u32[]{:S(2)}, u32[]{:S(2)}) collective-permute-start(bf16[128,128]{0,1:T(8,128)(2,1)} %get-tuple-element.218), channel_id=1, source_target_pairs={{0,6},{2,0},{4,2},{6,4},{1,7},{3,1},{5,3},{7,5},{8,14},{10,8},{12,... | collective-permute-start | bytes 98312 | tf_op jit(solution)/shard_map/ppermute | solution.py:73
  409.1 30.4 %collective-permute-start.53 = (bf16[128,2048]{1,0:T(8,128)(2,1)S(1)}, bf16[128,2048]{1,0:T(8,128)(2,1)S(1)}, u32[]{:S(2)}, u32[]{:S(2)}) collective-permute-start(bf16[128,2048]{1,0:T(8,128)(2,1)S(1)} %get-tuple-element.144), channel_id=1, source_target_pairs={{0,4},{2,6},{4,0},{6,2},{1,5},{3,7},{5,1},{7,3},{8,12},{10,14},{12... | collective-permute-start | bytes 1572872 | tf_op jit(solution)/shard_map/ppermute | solution.py:73
  409.2 33.1 %collective-permute-start.54 = (bf16[128,2048]{1,0:T(8,128)(2,1)S(1)}, bf16[128,2048]{1,0:T(8,128)(2,1)S(1)}, u32[]{:S(2)}, u32[]{:S(2)}) collective-permute-start(bf16[128,2048]{1,0:T(8,128)(2,1)S(1)} %get-tuple-element.146), channel_id=1, source_target_pairs={{0,2},{2,4},{4,6},{6,0},{1,3},{3,5},{5,7},{7,1},{8,10},{10,12},{12... | collective-permute-start | bytes 1572872 | tf_op jit(solution)/shard_map/ppermute | solution.py:73
  411.6 30.7 %collective-permute-start.55 = (bf16[128,2048]{1,0:T(8,128)(2,1)S(1)}, bf16[128,2048]{1,0:T(8,128)(2,1)S(1)}, u32[]{:S(2)}, u32[]{:S(2)}) collective-permute-start(bf16[128,2048]{1,0:T(8,128)(2,1)S(1)} %get-tuple-element.145), channel_id=1, source_target_pairs={{0,6},{2,0},{4,2},{6,4},{1,7},{3,1},{5,3},{7,5},{8,14},{10,8},{12,... | collective-permute-start | bytes 1572872 | tf_op jit(solution)/shard_map/ppermute | solution.py:73
  414.7 20.5 %collective-permute-start.56 = (bf16[128,256]{0,1:T(8,128)(2,1)S(1)}, bf16[128,256]{0,1:T(8,128)(2,1)S(1)}, u32[]{:S(2)}, u32[]{:S(2)}) collective-permute-start(bf16[128,256]{0,1:T(8,128)(2,1)S(1)} %copy-done.100), channel_id=1, source_target_pairs={{0,4},{2,6},{4,0},{6,2},{1,5},{3,7},{5,1},{7,3},{8,12},{10,14},{12... | collective-permute-start | bytes 196616 | tf_op jit(solution)/shard_map/ppermute | solution.py:73
  416.5 21.7 %collective-permute-start.57 = (bf16[128,256]{0,1:T(8,128)(2,1)S(1)}, bf16[128,256]{0,1:T(8,128)(2,1)S(1)}, u32[]{:S(2)}, u32[]{:S(2)}) collective-permute-start(bf16[128,256]{0,1:T(8,128)(2,1)S(1)} %copy-done.99), channel_id=1, source_target_pairs={{0,2},{2,4},{4,6},{6,0},{1,3},{3,5},{5,7},{7,1},{8,10},{10,12},{12... | collective-permute-start | bytes 196616 | tf_op jit(solution)/shard_map/ppermute | solution.py:73
  438.6 26.1 %collective-permute-start.43 = (bf16[128,2048]{1,0:T(8,128)(2,1)S(1)}, bf16[128,2048]{1,0:T(8,128)(2,1)S(1)}, u32[]{:S(2)}, u32[]{:S(2)}) collective-permute-start(bf16[128,2048]{1,0:T(8,128)(2,1)S(1)} %copy-done.86), channel_id=1, source_target_pairs={{0,2},{2,4},{4,6},{6,0},{1,3},{3,5},{5,7},{7,1},{8,10},{10,12},{12... | collective-permute-start | bytes 1572872 | tf_op jit(solution)/shard_map/ppermute | solution.py:73
  439.5 25.2 %collective-permute-start.44 = (bf16[128,2048]{1,0:T(8,128)(2,1)S(1)}, bf16[128,2048]{1,0:T(8,128)(2,1)S(1)}, u32[]{:S(2)}, u32[]{:S(2)}) collective-permute-start(bf16[128,2048]{1,0:T(8,128)(2,1)S(1)} %copy-done.85), channel_id=1, source_target_pairs={{0,6},{2,0},{4,2},{6,4},{1,7},{3,1},{5,3},{7,5},{8,14},{10,8},{12,... | collective-permute-start | bytes 1572872 | tf_op jit(solution)/shard_map/ppermute | solution.py:73
  490.2 360.4 %all-gather.11.cloned.1.call-start = ((), (), s32[]{:S(2)}) async-start(), calls=%async_computation.6 | async-start | bytes 8982528 | tf_op jit(solution)/shard_map/all_gather | solution.py:606
  616.3 37.9 %collective-permute-start.62 = (bf16[2,4,512,256]{3,2,1,0:T(8,128)(2,1)}, bf16[2,4,512,256]{3,2,1,0:T(8,128)(2,1)}, u32[]{:S(2)}, u32[]{:S(2)}) collective-permute-start(bf16[2,4,512,256]{3,2,1,0:T(8,128)(2,1)} %get-tuple-element.24), channel_id=1, source_target_pairs={{1,0},{3,2},{5,4},{7,6},{9,8},{11,10},{13,12},{15,14},{17,16},{19,... | collective-permute-start | bytes 6291464 | tf_op jit(solution)/shard_map/ppermute | solution.py:145
  618.9 24.5 %collective-permute-start.69 = (bf16[4,2,512,256]{3,2,1,0:T(8,128)(2,1)}, bf16[4,2,512,256]{3,2,1,0:T(8,128)(2,1)}, u32[]{:S(2)}, u32[]{:S(2)}) collective-permute-start(bf16[4,2,512,256]{3,2,1,0:T(8,128)(2,1)} %get-tuple-element.26), channel_id=1, source_target_pairs={{1,0},{3,2},{5,4},{7,6},{9,8},{11,10},{13,12},{15,14},{17,16},{19,... | collective-permute-start | bytes 6291464 | tf_op jit(solution)/shard_map/ppermute | solution.py:158
  624.0 14.8 %collective-permute-start.74 = (bf16[2,512,256]{2,1,0:T(8,128)(2,1)}, bf16[2,512,256]{2,1,0:T(8,128)(2,1)}, u32[]{:S(2)}, u32[]{:S(2)}) collective-permute-start(bf16[2,512,256]{2,1,0:T(8,128)(2,1)} %get-tuple-element.138), channel_id=1, source_target_pairs={{64,72},{72,80},{80,88},{88,64},{66,74},{74,82},{82,90},{90,66},{6... | collective-permute-start | bytes 1572872 | tf_op jit(solution)/shard_map/ppermute | solution.py:122
  625.5 14.8 %collective-permute-start.75 = (bf16[2,512,256]{2,1,0:T(8,128)(2,1)}, bf16[2,512,256]{2,1,0:T(8,128)(2,1)}, u32[]{:S(2)}, u32[]{:S(2)}) collective-permute-start(bf16[2,512,256]{2,1,0:T(8,128)(2,1)} %get-tuple-element.140), channel_id=1, source_target_pairs={{64,80},{72,88},{80,64},{88,72},{66,82},{74,90},{82,66},{90,74},{6... | collective-permute-start | bytes 1572872 | tf_op jit(solution)/shard_map/ppermute | solution.py:122
  627.0 14.7 %collective-permute-start.76 = (bf16[2,512,256]{2,1,0:T(8,128)(2,1)}, bf16[2,512,256]{2,1,0:T(8,128)(2,1)}, u32[]{:S(2)}, u32[]{:S(2)}) collective-permute-start(bf16[2,512,256]{2,1,0:T(8,128)(2,1)} %get-tuple-element.139), channel_id=1, source_target_pairs={{64,88},{72,64},{80,72},{88,80},{66,90},{74,66},{82,74},{90,82},{6... | collective-permute-start | bytes 1572872 | tf_op jit(solution)/shard_map/ppermute | solution.py:122
  638.9 78.7 %collective-permute-start.64 = (bf16[4,512,256]{2,1,0:T(8,128)(2,1)}, bf16[4,512,256]{2,1,0:T(8,128)(2,1)}, u32[]{:S(2)}, u32[]{:S(2)}) collective-permute-start(bf16[4,512,256]{2,1,0:T(8,128)(2,1)} %get-tuple-element.136), channel_id=1, source_target_pairs={{64,1},{96,33},{66,3},{98,35},{68,5},{100,37},{70,7},{102,39},{72,... | collective-permute-start | bytes 3145736 | tf_op jit(solution)/shard_map/ppermute | solution.py:149
  640.3 77.2 %collective-permute-start.65 = (bf16[4,512,256]{2,1,0:T(8,128)(2,1)}, bf16[4,512,256]{2,1,0:T(8,128)(2,1)}, u32[]{:S(2)}, u32[]{:S(2)}) collective-permute-start(bf16[4,512,256]{2,1,0:T(8,128)(2,1)} %get-tuple-element.137), channel_id=1, source_target_pairs={{96,1},{64,33},{98,3},{66,35},{100,5},{68,37},{102,7},{70,39},{104... | collective-permute-start | bytes 3145736 | tf_op jit(solution)/shard_map/ppermute | solution.py:149
  645.8 25.9 %collective-permute-start.70 = (bf16[2,512,256]{2,1,0:T(8,128)(2,1)S(1)}, bf16[2,512,256]{2,1,0:T(8,128)(2,1)S(1)}, u32[]{:S(2)}, u32[]{:S(2)}) collective-permute-start(bf16[2,512,256]{2,1,0:T(8,128)(2,1)S(1)} %get-tuple-element.141), channel_id=1, source_target_pairs={{0,8},{8,16},{16,24},{24,0},{1,9},{9,17},{17,25},{25,1},{2,10},{10... | collective-permute-start | bytes 1572872 | tf_op jit(solution)/shard_map/ppermute | solution.py:73
  647.9 36.1 %collective-permute-start.71 = (bf16[2,512,256]{2,1,0:T(8,128)(2,1)S(1)}, bf16[2,512,256]{2,1,0:T(8,128)(2,1)S(1)}, u32[]{:S(2)}, u32[]{:S(2)}) collective-permute-start(bf16[2,512,256]{2,1,0:T(8,128)(2,1)S(1)} %get-tuple-element.143), channel_id=1, source_target_pairs={{0,16},{8,24},{16,0},{24,8},{1,17},{9,25},{17,1},{25,9},{2,18},{10... | collective-permute-start | bytes 1572872 | tf_op jit(solution)/shard_map/ppermute | solution.py:73
  654.2 31.1 %collective-permute-start.72 = (bf16[2,512,256]{2,1,0:T(8,128)(2,1)S(1)}, bf16[2,512,256]{2,1,0:T(8,128)(2,1)S(1)}, u32[]{:S(2)}, u32[]{:S(2)}) collective-permute-start(bf16[2,512,256]{2,1,0:T(8,128)(2,1)S(1)} %get-tuple-element.142), channel_id=1, source_target_pairs={{0,24},{8,0},{16,8},{24,16},{1,25},{9,1},{17,9},{25,17},{2,26},{10... | collective-permute-start | bytes 1572872 | tf_op jit(solution)/shard_map/ppermute | solution.py:73
  671.7 27.3 %collective-permute-start.77 = (bf16[512,256]{1,0:T(8,128)(2,1)S(1)}, bf16[512,256]{1,0:T(8,128)(2,1)S(1)}, u32[]{:S(2)}, u32[]{:S(2)}) collective-permute-start(bf16[512,256]{1,0:T(8,128)(2,1)S(1)} %get-tuple-element.184), channel_id=1, source_target_pairs={{64,1},{96,33},{66,3},{98,35},{68,5},{100,37},{70,7},{102,39},{72,... | collective-permute-start | bytes 786440 | tf_op jit(solution)/shard_map/ppermute | solution.py:168
  684.0 18.1 %collective-permute-start.78 = (bf16[512,256]{1,0:T(8,128)(2,1)S(1)}, bf16[512,256]{1,0:T(8,128)(2,1)}, u32[]{:S(2)}, u32[]{:S(2)}) collective-permute-start(bf16[512,256]{1,0:T(8,128)(2,1)S(1)} %get-tuple-element.185), channel_id=1, source_target_pairs={{96,1},{64,33},{98,3},{66,35},{100,5},{68,37},{102,7},{70,39},{104... | collective-permute-start | bytes 786440 | tf_op jit(solution)/shard_map/ppermute | solution.py:168
  685.3 32.2 %collective-permute-start.63 = (bf16[4,512,256]{2,1,0:T(8,128)(2,1)}, bf16[4,512,256]{2,1,0:T(8,128)(2,1)}, u32[]{:S(2)}, u32[]{:S(2)}) collective-permute-start(bf16[4,512,256]{2,1,0:T(8,128)(2,1)} %fusion.51), channel_id=1, source_target_pairs={{0,32},{1,33},{32,0},{33,1},{64,96},{65,97},{96,64},{97,65},{2,34}... | collective-permute-start | bytes 3145736 | tf_op jit(solution)/shard_map/ppermute | solution.py:147
  699.0 17.2 %collective-permute-start.73 = (bf16[512,256]{1,0:T(8,128)(2,1)S(1)}, bf16[512,256]{1,0:T(8,128)(2,1)}, u32[]{:S(2)}, u32[]{:S(2)}) collective-permute-start(bf16[512,256]{1,0:T(8,128)(2,1)S(1)} %fusion.103), channel_id=1, source_target_pairs={{0,32},{1,33},{32,0},{33,1},{64,96},{65,97},{96,64},{97,65},{2,34}... | collective-permute-start | bytes 786440 | tf_op jit(solution)/shard_map/ppermute | solution.py:166
  769.6 15.3 %collective-permute-start.79 = (bf16[128,2048]{1,0:T(8,128)(2,1)S(1)}, bf16[128,2048]{1,0:T(8,128)(2,1)S(1)}, u32[]{:S(2)}, u32[]{:S(2)}) collective-permute-start(bf16[128,2048]{1,0:T(8,128)(2,1)S(1)} %get-tuple-element.133), channel_id=1, source_target_pairs={{0,4},{2,6},{4,0},{6,2},{1,5},{3,7},{5,1},{7,3},{8,12},{10,14},{12... | collective-permute-start | bytes 1572872 | tf_op jit(solution)/shard_map/ppermute | solution.py:73
  770.6 25.6 %collective-permute-start.80 = (bf16[128,2048]{1,0:T(8,128)(2,1)S(1)}, bf16[128,2048]{1,0:T(8,128)(2,1)S(1)}, u32[]{:S(2)}, u32[]{:S(2)}) collective-permute-start(bf16[128,2048]{1,0:T(8,128)(2,1)S(1)} %get-tuple-element.135), channel_id=1, source_target_pairs={{0,2},{2,4},{4,6},{6,0},{1,3},{3,5},{5,7},{7,1},{8,10},{10,12},{12... | collective-permute-start | bytes 1572872 | tf_op jit(solution)/shard_map/ppermute | solution.py:73
  770.7 25.6 %collective-permute-start.81 = (bf16[128,2048]{1,0:T(8,128)(2,1)S(1)}, bf16[128,2048]{1,0:T(8,128)(2,1)S(1)}, u32[]{:S(2)}, u32[]{:S(2)}) collective-permute-start(bf16[128,2048]{1,0:T(8,128)(2,1)S(1)} %get-tuple-element.134), channel_id=1, source_target_pairs={{0,6},{2,0},{4,2},{6,4},{1,7},{3,1},{5,3},{7,5},{8,14},{10,8},{12,... | collective-permute-start | bytes 1572872 | tf_op jit(solution)/shard_map/ppermute | solution.py:73
  778.0 53.9 %collective-permute-start.48 = (bf16[64,2048]{1,0:T(8,128)(2,1)S(1)}, bf16[64,2048]{1,0:T(8,128)(2,1)S(1)}, u32[]{:S(2)}, u32[]{:S(2)}) collective-permute-start(bf16[64,2048]{1,0:T(8,128)(2,1)S(1)} %get-tuple-element.192), channel_id=1, source_target_pairs={{0,1},{1,0},{2,3},{3,2},{4,5},{5,4},{6,7},{7,6},{8,9},{9,8},{10,11... | collective-permute-start | bytes 786440 | tf_op jit(solution)/shard_map/ppermute | solution.py:69
  782.1 18.3 %collective-permute-start.96 = (bf16[80,128]{1,0:T(8,128)(2,1)S(1)}, bf16[80,128]{1,0:T(8,128)(2,1)S(1)}, u32[]{:S(2)}, u32[]{:S(2)}) collective-permute-start(bf16[80,128]{1,0:T(8,128)(2,1)S(1)} %get-tuple-element.97), channel_id=1, source_target_pairs={{0,24},{8,0},{16,8},{24,16},{1,25},{9,1},{17,9},{25,17},{2,26},{10... | collective-permute-start | bytes 61448 | tf_op jit(solution)/shard_map/ppermute | solution.py:73
  812.9 16.2 %collective-permute-start.104 = (bf16[4,4,80,128]{3,2,1,0:T(8,128)(2,1)S(1)}, bf16[4,4,80,128]{3,2,1,0:T(8,128)(2,1)S(1)}, u32[]{:S(2)}, u32[]{:S(2)}) collective-permute-start(bf16[4,4,80,128]{3,2,1,0:T(8,128)(2,1)S(1)} %bitcast_dynamic-update-slice_fusion.12), channel_id=1, source_target_pairs={{0,2},{2,4},{4,6},{6,0},{1,3},{3,5},{5,7},{7,1},{8,10},{10,12},{12... | collective-permute-start | bytes 983048 | tf_op jit(solution)/shard_map/ppermute | solution.py:73
  (173 other events, 2462.4 us)
Sparse Core Ops, SparseCore 0:
  10.2 67.1 all-gather.8
  80.1 84.4 all-gather.6
  167.6 94.8 all-gather.4
  490.3 100.6 reduce-scatter.1
  593.9 82.8 all-gather.10

commit v3 on v2

--- a/solution.py
+++ b/solution.py
@@ -13,7 +13,6 @@
 GROUP = 512
 
 ALL = ("zh", "zl", "x", "y", "c")
-PLANE = ("zh", "zl", "x")
 
 norm_eps = 1e-06
 rope_theta = 1000042.0
@@ -91,8 +90,8 @@
     return whole_ring
 
 
-def sum_near(blocks):
-    got = [shift(blocks[step], "y", step) for step in (2, 1, 3)]
+def sum_near(blocks, ring):
+    got = [shift(blocks[step], ring, step) for step in (2, 1, 3)]
     total = blocks[0].astype(f32)
     for term in got:
         total = total + term.astype(f32)
@@ -122,51 +121,49 @@
     return lax.ppermute(value, ROW_AHEAD, [(8 + 2 * i, 8 + 2 * ((i + step) % 4)) for i in range(4)])
 
 
-def gather_keys(key):
-    line = gather_near(key[None], "x")
-    own = jnp.stack([line, lax.ppermute(line, CORNER, PARTNER)])
-    ahead = jnp.stack([lax.ppermute(line, CORNER, LATER[0]), lax.ppermute(line, CORNER, LATER[1])])
-    return own, ahead
-
-
-def gather_values(value):
-    pair = jnp.stack([value, lax.ppermute(value, CORNER, PARTNER)])
-    pair_ahead = jnp.stack([lax.ppermute(value, CORNER, LATER[0]), lax.ppermute(value, CORNER, LATER[1])])
-    own = gather_near(pair[None], "x")
-    ahead = jnp.concatenate([pair_ahead[None]] + [shift_ahead(pair_ahead, -step)[None] for step in (1, 2, 3)])
-    return own, ahead
-
-
-def row_before(own, ahead, c):
-    return jnp.where(c == 0, ahead, lax.ppermute(own, "c", [(0, 1)]))
-
-
-def sum_keys(own, before, c):
-    got = lax.ppermute(before, "c", [(1, 0)])
-    own = own.astype(f32) + got.astype(f32)
-    line = own[0] + lax.ppermute(own[1].astype(bf16), CORNER, PARTNER).astype(f32)
+def after(value, *others):
+    return lax.optimization_barrier((value,) + others)[0]
+
+
+def gather_row(key, value, c):
+    lines = [key] + [shift(key, "x", -step) for step in (1, 2, 3)]
+    pair = [value, lax.ppermute(value, CORNER, PARTNER)]
+    pair_ahead = [lax.ppermute(value, CORNER, pairs) for pairs in LATER]
+    lines, pair, pair_ahead = lax.optimization_barrier((lines, pair, pair_ahead))
+    line, pair, pair_ahead = jnp.stack(lines), jnp.stack(pair), jnp.stack(pair_ahead)
+    k_own = jnp.stack([line, lax.ppermute(line, CORNER, PARTNER)])
+    k_ahead = jnp.stack([lax.ppermute(line, CORNER, pairs) for pairs in LATER])
+    v_own = jnp.stack([pair] + [shift(pair, "x", -step) for step in (1, 2, 3)])
+    v_ahead = jnp.stack([pair_ahead] + [shift_ahead(pair_ahead, -step) for step in (1, 2, 3)])
+    k_prev = jnp.where(c == 0, k_ahead, lax.ppermute(k_own, "c", [(0, 1)]))
+    v_prev = jnp.where(c == 0, v_ahead, lax.ppermute(v_own, "c", [(0, 1)]))
+    return k_own, k_prev, v_own, v_prev
+
+
+def sum_row(k_own, k_prev, v_own, v_prev):
+    k_got, v_got = (lax.ppermute(prev, "c", [(1, 0)]) for prev in (k_prev, v_prev))
+    k_own, v_own = k_own.astype(f32) + k_got.astype(f32), v_own.astype(f32) + v_got.astype(f32)
+    k_sent, v_sent = k_own[1].astype(bf16), v_own.astype(bf16)
+    line, pair, pair_prev = k_own[0], v_own[0], v_prev[0].astype(f32)
+    lines = [lax.ppermute(k_sent, CORNER, PARTNER)]
+    lines += [lax.ppermute(k_prev[flip], CORNER, EARLIER[flip]) for flip in (0, 1)]
+    pairs = [shift(v_sent[step], "x", step) for step in (1, 2, 3)]
+    pairs_prev = [shift_ahead(v_prev[step], step) for step in (1, 2, 3)]
+    lines, pairs, pairs_prev = lax.optimization_barrier((lines, pairs, pairs_prev))
+    for term in lines:
+        line = line + term.astype(f32)
+    for term in pairs:
+        pair = pair + term.astype(f32)
+    for term in pairs_prev:
+        pair_prev = pair_prev + term.astype(f32)
+    k_total, v_total = line[0], pair[0]
+    k_sent, v_sent, prev_sent = line.astype(bf16), pair[1].astype(bf16), pair_prev.astype(bf16)
+    for step in (1, 2, 3):
+        k_total = k_total + shift(k_sent[step], "x", step).astype(f32)
+    v_total = v_total + lax.ppermute(v_sent, CORNER, PARTNER).astype(f32)
     for flip in (0, 1):
-        line = line + lax.ppermute(before[flip], CORNER, EARLIER[flip]).astype(f32)
-    sent = line.astype(bf16)
-    total = line[0]
-    for step in (1, 2, 3):
-        total = total + shift(sent[step], "x", step).astype(f32)
-    return total
-
-
-def sum_values(own, before, c):
-    got = lax.ppermute(before, "c", [(1, 0)])
-    own = own.astype(f32) + got.astype(f32)
-    sent = own.astype(bf16)
-    pair, pair_before = own[0], before[0].astype(f32)
-    for step in (1, 2, 3):
-        pair = pair + shift(sent[step], "x", step).astype(f32)
-        pair_before = pair_before + shift_ahead(before[step], step).astype(f32)
-    sent_before = pair_before.astype(bf16)
-    total = pair[0] + lax.ppermute(pair[1].astype(bf16), CORNER, PARTNER).astype(f32)
-    for flip in (0, 1):
-        total = total + lax.ppermute(sent_before[flip], CORNER, EARLIER[flip]).astype(f32)
-    return total
+        v_total = v_total + lax.ppermute(prev_sent[flip], CORNER, EARLIER[flip]).astype(f32)
+    return k_total, v_total
 
 
 def allowed_mask(own_pos, own_start, key_pos):
@@ -377,7 +374,6 @@
 ):
     zh, zl, x, y, c = (lax.axis_index(name) for name in ALL)
     row = 2 * zh + c
-    mine, other = 2 * y + c, 2 * y + 1 - c
     factor = HEAD_SIZE ** (-0.5)
     rank = out_shrink.shape[1]
 
@@ -410,32 +406,42 @@
     member = (group_pos[:, None] >= starts[None, :]) & (group_pos[:, None] < seq_ends[None, :])
     member_int = member.astype(jnp.int32)
     group_start = jnp.sum(member_int * starts[None, :], axis=1)
-    group_owner = jnp.sum(member_int * adapter[None, :], axis=1)
+
+    def selected(pos):
+        inside = (pos[:, None] >= starts[None, :]) & (pos[:, None] < seq_ends[None, :])
+        owner = jnp.sum(inside.astype(jnp.int32) * adapter[None, :], axis=1)
+        return (owner[:, None] == (jnp.arange(rank, dtype=jnp.int32) // RANK)[None, :]).astype(f32)
+
     low, high = jnp.min(group_start), jnp.max(group_pos)
     active = (jnp.min(key_pos, axis=2) <= high) & (jnp.max(key_pos, axis=2) >= low)
     active = jnp.transpose(active).reshape(16).astype(jnp.int32)
-    columns = jnp.arange(rank, dtype=jnp.int32) // RANK
-    select_g = (group_owner[:, None] == columns[None, :]).astype(f32)
-    select = select_g[:128]
+    select_y = selected(group_pos)
+    select_x = selected(own_row.reshape(2, 4, 4, 128)[0, :, 0].reshape(GROUP))
+    select = select_y[:128]
     cos_table, sin_table = rope_tables(group_pos - group_start, HEAD_SIZE)
 
     def column_slices(weight):
-        rows_here, width = weight.shape
-        parts = jnp.transpose(weight.reshape(rows_here, 16, 8, width // 128), (2, 0, 1, 3))
-        return parts.reshape(8, rows_here, width // 8)
+        parts = weight.reshape(16, 4, 4, 4, 2, 64)
+        return jnp.transpose(parts, (2, 4, 0, 1, 3, 5)).reshape(8, 16, 1024)
+
+    def units_at(array, axis, core):
+        shape = array.shape
+        array = array.reshape(shape[:axis] + (4, 4, 4, 2, 64) + shape[axis + 1 :])
+        array = lax.dynamic_slice_in_dim(array, x, 1, axis + 1)
+        array = lax.dynamic_slice_in_dim(array, core, 1, axis + 3)
+        return array.reshape(shape[:axis] + (1024,) + shape[axis + 1 :])
 
     heads_q = w_query.reshape(16, 4, 512)
     heads_kv = jnp.concatenate([w_key.reshape(16, 4, 256), w_value.reshape(16, 4, 256)], axis=2)
     qkv_parts = jnp.transpose(jnp.stack([heads_q, heads_kv], axis=2), (1, 2, 0, 3)).reshape(8, 16, 512)
-    parts = jnp.concatenate([qkv_parts, column_slices(w_gate), column_slices(w_up)], axis=2)
-    parts = lax.all_to_all(parts, ("y", "c"), split_axis=0, concat_axis=0, tiled=True).reshape(128, 2560)
-    first = gather_ring(gather_ring(parts[:, :256], "x"), "z").reshape(2048, 256)
-    second = jnp.swapaxes(gather_ring(gather_ring(parts[:, 256:512], "z"), "x"), 0, 1).reshape(2048, 256)
-    qkv_mine = jnp.concatenate([first, second], axis=1)
-    qkv_other = swap_cores(qkv_mine)
+    qkv_parts = lax.all_to_all(qkv_parts, ("y", "c"), split_axis=0, concat_axis=0, tiled=True).reshape(128, 512)
+    gate_up = jnp.concatenate([column_slices(w_gate), column_slices(w_up)], axis=2)
+    gate_up = lax.all_to_all(gate_up, ("x", "c"), split_axis=0, concat_axis=0, tiled=True).reshape(128, 2048)
     wo = lax.all_gather(w_out, ALL, axis=0, tiled=True)
-    wd_mine = lax.all_gather(w_down, PLANE, axis=0, tiled=True)
-    wgu_mine = lax.all_gather(parts[:, 512:], PLANE, axis=0, tiled=True)
+    ffn = jnp.concatenate([gate_up, w_down], axis=0)
+    ffn = lax.all_gather(ffn, ("zh", "zl", "y"), axis=0, tiled=False)
+    wd_mine = ffn[:, 128:].reshape(1024, 2048)
+    wgu_mine = jnp.transpose(ffn[:, :128].reshape(4, 4, 4, 32, 2048), (0, 2, 1, 3, 4)).reshape(2048, 2048)
     wgu_other, wd_other = swap_cores(wgu_mine), swap_cores(wd_mine)
 
     def columns_of(array, width):
@@ -445,11 +451,15 @@
     scale_in = row_scale(inputs)
     normed = (inputs * scale_in * gain_attn).astype(bf16)
     normed_g = gather_near(normed, "y")
-    cot_g = gather_near(cot, "y")
+    qkv_parts = after(qkv_parts, normed)
+    first = gather_ring(gather_ring(qkv_parts[:, :256], "x"), "z").reshape(2048, 256)
+    second = jnp.swapaxes(gather_ring(gather_ring(qkv_parts[:, 256:], "z"), "x"), 0, 1).reshape(2048, 256)
+    qkv_mine = jnp.concatenate([first, second], axis=1)
+    qkv_other = swap_cores(qkv_mine)
     q_expand = columns_of(query_expand, 512)
     k_expand = columns_of(key_expand, 256)
     v_expand = columns_of(value_expand, 256)
-    low_qkv = (product(normed_g, qkv_shrink) * jnp.tile(select_g, (1, 3))).astype(bf16)
+    low_qkv = (product(normed_g, qkv_shrink) * jnp.tile(select_y, (1, 3))).astype(bf16)
     lin_mine, lin_other = product(normed_g, qkv_mine), product(normed_g, qkv_other)
     query_lin = jnp.where(c == 0, lin_mine, lin_other) + product(low_qkv[:, :rank], q_expand)
     kv_lin = jnp.where(c == 0, lin_other, lin_mine)
@@ -461,9 +471,7 @@
     query = (query * bf16(factor)).reshape(GROUP, 512)
     key = (key_heads * cos_table + rotate(key_heads) * sin_table).astype(bf16).reshape(GROUP, 256)
 
-    k_own, k_ahead = gather_keys(key)
-    v_own, v_ahead = gather_values(value_lin.astype(bf16))
-    k_prev, v_prev = row_before(k_own, k_ahead, c), row_before(v_own, v_ahead, c)
+    k_own, k_prev, v_own, v_prev = gather_row(key, value_lin.astype(bf16), c)
     attended = (
         query,
         group_pos[:, None],
@@ -476,6 +484,7 @@
     )
     mixed_f, lse = attend(active, *attended)
     mixed = mixed_f.astype(bf16)
+    cot_g = gather_near(after(cot, k_prev, v_prev), "x")
 
     heads = jnp.zeros((4, 128, 512), bf16)
     heads = lax.dynamic_update_index_in_dim(heads, mixed[:128], y, 0)
@@ -487,22 +496,21 @@
     middle = inputs + product(mixed_tok, wo) + product(low_out, out_expand)
     scale_mid = row_scale(middle)
     normed_mid = (middle * scale_mid * gain_ffn).astype(bf16)
-    normed_mid_g = gather_near(normed_mid, "y")
-
-    select_two = jnp.tile(select_g, (1, 2))
+    normed_mid_g = gather_near(normed_mid, "x")
+
+    select_two = jnp.tile(select_x, (1, 2))
     low_gu = (product(normed_mid_g, gateup_shrink) * select_two).astype(bf16)
-    grad_low_down = (times_transposed(cot_g, down_expand) * select_g).astype(bf16)
+    grad_low_down = (times_transposed(cot_g, down_expand) * select_x).astype(bf16)
     result = jnp.zeros((GROUP, 2048), f32)
     low_down_part = jnp.zeros((GROUP, rank), f32)
     grad_mid_part = jnp.zeros((GROUP, 2048), f32)
     grad_low_part = jnp.zeros((GROUP, 2 * rank), f32)
     unit_grads = []
     units = 1024
-    for wgu, wd, at in ((wgu_mine, wd_mine, mine), (wgu_other, wd_other, other)):
+    for wgu, wd, core in ((wgu_mine, wd_mine, c), (wgu_other, wd_other, 1 - c)):
         wg, wu = wgu[:, :units], wgu[:, units:]
-        g_expand = lax.dynamic_slice_in_dim(gate_expand.reshape(rank, 16, 8, 64), at, 1, 2).reshape(rank, units)
-        u_expand = lax.dynamic_slice_in_dim(up_expand.reshape(rank, 16, 8, 64), at, 1, 2).reshape(rank, units)
-        d_shrink = lax.dynamic_slice_in_dim(down_shrink.reshape(16, 8, 64, rank), at, 1, 1).reshape(units, rank)
+        g_expand, u_expand = units_at(gate_expand, 1, core), units_at(up_expand, 1, core)
+        d_shrink = units_at(down_shrink, 0, core)
         gate_pre = product(normed_mid_g, wg) + product(low_gu[:, :rank], g_expand)
         up_pre = product(normed_mid_g, wu) + product(low_gu[:, rank:], u_expand)
         sigmoid_g = jax.nn.sigmoid(gate_pre)
@@ -525,16 +533,15 @@
             )
         )
 
-    def sum_tokens(part):
+    def sum_tokens(part, ring):
         sent = part.astype(bf16)
-        return sum_near([sent[i * 128 : (i + 1) * 128] for i in range(4)])
-
-    back_low = sum_tokens(grad_low_part)
-    back = sum_tokens(grad_mid_part)
-    ahead_low = sum_tokens(low_down_part)
-    ahead = sum_tokens(result)
-    low_down = (ahead_low * select).astype(bf16)
-    output = (middle + ahead + product(low_down, down_expand)).astype(bf16)
+        return sum_near([sent[i * 128 : (i + 1) * 128] for i in range(4)], ring)
+
+    back_low = sum_tokens(grad_low_part, "x")
+    back = sum_tokens(grad_mid_part, "x")
+    low_down_sum = sum_tokens(low_down_part, "x")
+
+    low_down = (low_down_sum * select).astype(bf16)
     grad_low_gu = (back_low * jnp.tile(select, (1, 2))).astype(bf16)
     grad_normed_mid = back + times_transposed(grad_low_gu, gateup_shrink)
     cot_f = cot.astype(f32)
@@ -550,8 +557,10 @@
         return jnp.concatenate([columns_at(0)] + [shift(columns_at(4 - step), "y", -step) for step in (1, 2, 3)])
 
     dout = slices_near(grad_mixed)
+    ahead = sum_tokens(after(result.astype(bf16), dout), "x")
+    output = (middle + ahead + product(low_down, down_expand)).astype(bf16)
     dq, dk_prev, dk_own, dv_prev, dv_own = attend_back(active, *attended, mixed_f, lse, dout)
-    dk, dv = sum_keys(dk_own, dk_prev, c), sum_values(dv_own, dv_prev, c)
+    dk, dv = sum_row(dk_own, dk_prev, dv_own, dv_prev)
     query_back = (dq * factor).astype(bf16).astype(f32).reshape(GROUP, 2, HEAD_SIZE)
     key_back = dk.astype(bf16).astype(f32).reshape(GROUP, 1, HEAD_SIZE)
     grad_value = dv.astype(bf16)
@@ -567,15 +576,15 @@
         ],
         axis=1,
     )
-    grad_low_qkv = (sum_tokens(grad_low_part) * jnp.tile(select, (1, 3))).astype(bf16)
+    grad_low_qkv = (sum_tokens(grad_low_part, "y") * jnp.tile(select, (1, 3))).astype(bf16)
     for_mine = jnp.where(c == 0, grad_query, grad_kv)
     for_other = jnp.where(c == 0, grad_kv, grad_query)
     grad_normed_part = times_transposed(for_mine, qkv_mine) + times_transposed(for_other, qkv_other)
-    grad_normed = sum_tokens(grad_normed_part) + times_transposed(grad_low_qkv, qkv_shrink)
+    grad_normed = sum_tokens(grad_normed_part, "y") + times_transposed(grad_low_qkv, qkv_shrink)
     grad_input = (grad_middle + norm_back(inputs, scale_in, gain_attn, grad_normed)).astype(bf16)
 
-    def features(array):
-        return lax.dynamic_slice_in_dim(array, y * 512, 512, 1)
+    def features(array, at):
+        return lax.dynamic_slice_in_dim(array, at * 512, 512, 1)
 
     def by_halves(pair_at):
         own, others = unit_grads[0][pair_at], unit_grads[1][pair_at]
@@ -586,26 +595,30 @@
     def by_rows(array):
         return array.reshape(32, array.shape[0] // 32, rank)
 
-    low_near = gather_near(jnp.concatenate([low_down, grad_low_gu, grad_low_out, low_out], axis=1), "y")
-    low_down_g, grad_low_gu_g = low_near[:, :rank], low_near[:, rank : 3 * rank]
-    grad_low_out_g, low_out_g = low_near[:, 3 * rank : 4 * rank], low_near[:, 4 * rank :]
-    grad_gateup = inner_rows(features(normed_mid_g), grad_low_gu_g)
+    low_near = gather_near(jnp.concatenate([low_down, grad_low_gu], axis=1), "x")
+    grad_gateup = inner_rows(features(normed_mid_g, x), low_near[:, rank:])
+    out_terms = jnp.concatenate([inner_rows(mixed_tok, grad_low_out), inner_rows(grad_attn_out, low_out)], axis=1)
+    out_terms = out_terms.astype(bf16).reshape(4, 512, 2 * rank)
+    out_terms = sum_near(
+        [lax.dynamic_index_in_dim(out_terms, (x + step) % 4, 0, keepdims=False) for step in range(4)], "x"
+    )
     early = [
         by_halves(0),
         by_halves(1),
         by_halves(2),
-        by_rows(inner_rows(mixed, grad_low_out_g)),
-        by_rows(inner_rows(slices_near(grad_attn_out), low_out_g)),
-        by_rows(inner_rows(features(cot_g), low_down_g)),
+        by_rows(out_terms[:, :rank]),
+        by_rows(out_terms[:, rank:]),
+        by_rows(inner_rows(features(cot_g, x), low_near[:, :rank])),
         by_rows(grad_gateup[:, :rank]),
         by_rows(grad_gateup[:, rank:]),
     ]
     early_sum = lax.psum_scatter(
-        jnp.concatenate(early, axis=1), PLANE + ("c",), scatter_dimension=0, tiled=False
+        jnp.concatenate(early, axis=1), ("zh", "zl", "y", "c"), scatter_dimension=0, tiled=False
     )
-    early_all = lax.all_gather(early_sum.astype(bf16), ALL, axis=0, tiled=False)
-
-    grad_qkv = inner_rows(features(normed_g), gather_near(grad_low_qkv, "y"))
+    early_sum = after(early_sum.astype(bf16), dq)
+    early_all = lax.all_gather(early_sum, ALL, axis=0, tiled=False)
+
+    grad_qkv = inner_rows(features(normed_g, y), gather_near(grad_low_qkv, "y"))
     late = [
         by_rows(inner_rows(grad_query, low_qkv[:, :rank])),
         by_rows(inner_rows(grad_key, low_qkv[:, rank : 2 * rank])),
@@ -632,7 +645,7 @@
         return found
 
     def rows_order(array):
-        ordered = jnp.transpose(array.reshape(16, 4, 2, array.shape[1], rank), (1, 0, 2, 3, 4))
+        ordered = jnp.transpose(array.reshape(4, 4, 8, array.shape[1], rank), (1, 0, 2, 3, 4))
         return ordered.reshape(-1, rank)
 
     early_found = cut(early_all, 1, early)

time: 898 us -> 861 us (0.959); the launches traced: 896 us -> 849 us
  waiting for transfers between devices: 351 us -> 272 us
  local copies, waits for them, and re-layouts: 118 us -> 139 us
  matrix products: 113 us -> 126 us
    ppermute x81, waiting for transfers between devices: 207 us -> 153 us  [shift(): lax.ppermute(value, RING[ring], [(i, (i + step) % 4) for i in range(4)])]
    reduce_scatter x1, waiting for transfers between devices: 83.9 us -> 36.4 us  [local(): lax.psum_scatter(jnp.concatenate(early, axis=1), ('zh', 'zl', 'y', 'c'),...]
    ppermute x16, waiting for transfers between devices: 57.9 us -> 78.1 us  [the longest x2 30.1 us: sum_row(): lax.ppermute(prev_sent[flip], CORNER, EARLIER[flip]).astype(f32)]
    slice x8 -> x14, local copies, waits for them, and re-layouts: 4.47 us -> 19.9 us  [the longest x1 8.28 us: local(): ffn[:, :128].reshape(4, 4, 4, 32, 2048)]
    ppermute x6, starting transfers between devices: 18.9 us -> 5.87 us  [shift_ahead(): lax.ppermute(value, ROW_AHEAD, [(8 + 2 * i, 8 + 2 * ((i + step) % 4)) for...]
    dot_general x23, matrix products: 50.4 us -> 61.7 us  [product(): return jnp.dot(left, right, preferred_element_type=f32)]
    transpose x2 -> x3, local copies, waits for them, and re-layouts: 1.7 us -> 12.3 us  [the longest x1 8.31 us: local(): jnp.transpose(ffn[:, :128].reshape(4, 4, 4, 32, 2048), (0, 2, 1, 3, 4))]
    ppermute x9, starting transfers between devices: 12.6 us -> 22.4 us  [swap_cores(): return lax.ppermute(value, 'c', [(0, 1), (1, 0)])]
  transfers between devices with their start and end apart: 117 -> 117, of which waited for: 52 -> 52; matrix products, arithmetic and copies ran while one was open for 24% -> 28% of each run, Pallas kernels for 4% -> 3%
where the time goes in v3:
time: 861 us; the launch traced here: 849 us
  waiting for transfers between devices  272 us (32%)
  starting transfers between devices  179 us (21%)
  local copies, waits for them, and re-layouts  139 us (16%)
  matrix products  126 us (15%)
  other arithmetic  75.9 us (9%)
  Pallas kernels  25.2 us (3%)
  between operations  17.2 us (2%)
  blocking collectives  15.1 us (2%)
    ppermute x81, waiting for transfers between devices, shift(): lax.ppermute(value, RING[ring], [(i, (i + step) % 4) for i in range(4)])  153 us
    ppermute x81, starting transfers between devices, shift(): lax.ppermute(value, RING[ring], [(i, (i + step) % 4) for i in range(4)])  97.3 us
    dot_general x23, matrix products, product(): return jnp.dot(left, right, preferred_element_type=f32)  61.7 us
    unnamed x273, local copies, waits for them, and re-layouts  57.3 us
    dot_general x23, matrix products, times_transposed(): lax.dot_general(left, right, (((1,), (1,)), ((), ())), preferred_element_...  46.7 us
    reduce_scatter x1, waiting for transfers between devices, local(): lax.psum_scatter(jnp.concatenate(early, axis=1), ('zh', 'zl', 'y', 'c'),...  36.4 us
    ppermute x2, waiting for transfers between devices, sum_row(): lax.ppermute(prev_sent[flip], CORNER, EARLIER[flip]).astype(f32)  30.1 us
    ppermute x9, starting transfers between devices, swap_cores(): return lax.ppermute(value, 'c', [(0, 1), (1, 0)])  22.4 us
  transfers between devices with their start and end apart: 117, of which 52 were waited for; matrix products, arithmetic and copies ran while one was open for 28% of the time, Pallas kernels for 3%

profile of v3, /device:TPU:1, one launch (start us, length us, event | category | flops | bytes accessed | tf_op | source)
XLA Modules:
  0.0 849.1 jit_solution(2683246563561526566)
XLA Ops:
  11.1 15.1 %all_to_all.10 = bf16[8,16,2048]{2,1,0:T(8,128)(2,1)S(1)} all-to-all(bf16[8,16,2048]{2,1,0:T(8,128)(2,1)S(1)} %pad_maximum_fusion.13), channel_id=1, replica_groups=mesh['zh'=2,'zl'=2,'x'=4,'y'=4,'c'=2] {'x','c'}, dimensions={0} | all-to-all | bytes 1048576 | tf_op jit(solution)/shard_map/all_to_all | solution.py:439
  29.3 4.6 all-to-all-start
  39.3 3.7 collective-permute-start.10
  60.8 3.1 collective-permute-done.9
  67.6 7.2 collective-permute-start.16
  84.3 14.4 %collective-permute-done.3 = bf16[128,2048]{1,0:T(8,128)(2,1)S(1)} collective-permute-done((bf16[128,2048]{1,0:T(8,128)(2,1)}, bf16[128,2048]{1,0:T(8,128)(2,1)S(1)}, u32[]{:S(2)}, u32[]{:S(2)}) %collective-permute-start.3) | collective-permute-done | bytes 524320 | tf_op jit(solution)/shard_map/ppermute | solution.py:72
  98.7 11.3 %collective-permute-done.2 = bf16[128,2048]{1,0:T(8,128)(2,1)S(1)} collective-permute-done((bf16[128,2048]{1,0:T(8,128)(2,1)}, bf16[128,2048]{1,0:T(8,128)(2,1)S(1)}, u32[]{:S(2)}, u32[]{:S(2)}) %collective-permute-start.2) | collective-permute-done | bytes 524320 | tf_op jit(solution)/shard_map/ppermute | solution.py:72
  115.1 4.2 broadcast_select_fusion
  124.7 5.8 collective-permute-start.21
  130.5 3.2 collective-permute-done.17
  137.8 3.8 collective-permute-done.21
  150.5 7.0 collective-permute-done.32
  157.5 11.6 %collective-permute-done.31 = bf16[2,512,256]{2,1,0:T(8,128)(2,1)} collective-permute-done((bf16[2,512,256]{2,1,0:T(8,128)(2,1)}, bf16[2,512,256]{2,1,0:T(8,128)(2,1)}, u32[]{:S(2)}, u32[]{:S(2)}) %collective-permute-start.31) | collective-permute-done | bytes 524320 | tf_op jit(solution)/shard_map/ppermute | solution.py:72
  169.6 3.2 pad_maximum_fusion.3.vown_ref
  175.5 4.1 copy.320
  181.5 14.8 %collective-permute-done.25 = bf16[4,512,256]{2,1,0:T(8,128)(2,1)} collective-permute-done((bf16[4,512,256]{2,1,0:T(8,128)(2,1)}, bf16[4,512,256]{2,1,0:T(8,128)(2,1)}, u32[]{:S(2)}, u32[]{:S(2)}) %collective-permute-start.25) | collective-permute-done | bytes 1048608 | tf_op jit(solution)/shard_map/ppermute | solution.py:134
  202.7 4.2 copy.319
  220.7 5.0 collective-permute-start.24
  225.7 6.7 collective-permute-start.23
  239.4 9.5 %collective-permute-done.24 = bf16[4,512,256]{2,1,0:T(8,128)(2,1)S(1)} collective-permute-done((bf16[4,512,256]{2,1,0:T(8,128)(2,1)}, bf16[4,512,256]{2,1,0:T(8,128)(2,1)S(1)}, u32[]{:S(2)}, u32[]{:S(2)}) %collective-permute-start.24) | collective-permute-done | bytes 1048608 | tf_op jit(solution)/shard_map/ppermute | solution.py:135
  250.8 11.7 %attend.1 = (f32[512,512]{1,0:T(8,128)S(1)}, f32[2,512,1]{2,1,0:T(8,128)S(1)}) custom-call(s32[16]{0:T(128)S(1)} %reshape.573.active, bf16[512,512]{1,0:T(8,128)(2,1)S(1)} %fusion.61.q_ref, s32[512,1]{1,0:T(8,128)S(1)} %copy.310.pos_ref, s32[512,1]{1,0:T(8,128)S(1)} %copy.311.start_ref, s32[8,2,1,512]{3,2,1,0:T(1,128)S(1)} %reshape.518.kpos_ref, ...), custom_call_target="tpu_custom_call" | custom-call | flops 6442450944 | bytes 10485760 | tf_op jit(solution)/shard_map/attend/pallas_call | solution.py:306
  269.8 6.6 collective-permute-start.43
  285.5 10.8 %collective-permute-done.43 = bf16[128,2048]{1,0:T(8,128)(2,1)} collective-permute-done((bf16[128,2048]{1,0:T(8,128)(2,1)}, bf16[128,2048]{1,0:T(8,128)(2,1)}, u32[]{:S(2)}, u32[]{:S(2)}) %collective-permute-start.43) | collective-permute-done | bytes 524320 | tf_op jit(solution)/shard_map/ppermute | solution.py:72
  303.2 5.3 multiply_reduce_fusion.1
  312.7 8.3 slice.441
  321.0 8.3 copy.318
  332.0 3.2 pad_maximum_fusion.4
  346.1 5.3 fusion.28
  353.8 4.9 multiply_convert_fusion.3
  371.0 4.7 convolution_add_fusion.2
  375.8 5.3 fusion.34
  381.1 6.2 multiply_convert_fusion.1
  389.3 4.6 fusion.4
  393.9 4.8 add_convert_fusion.1
  410.0 5.9 collective-permute-done.60
  423.3 17.4 %collective-permute-done.50 = bf16[128,256]{0,1:T(8,128)(2,1)} collective-permute-done((bf16[128,256]{0,1:T(8,128)(2,1)}, bf16[128,256]{0,1:T(8,128)(2,1)}, u32[]{:S(2)}, u32[]{:S(2)}) %collective-permute-start.50) | collective-permute-done | bytes 65568 | tf_op jit(solution)/shard_map/ppermute | solution.py:72
  440.7 3.5 collective-permute-done.49
  473.4 5.8 collective-permute-done.107
  491.9 4.8 fusion.221
  496.8 6.3 fusion.191
  508.3 4.7 add_convert_fusion.2
  516.7 13.5 %attend_back.1 = (f32[512,512]{1,0:T(8,128)S(1)}, bf16[2,4,512,256]{3,2,1,0:T(8,128)(2,1)}, bf16[2,4,512,256]{3,2,1,0:T(8,128)(2,1)S(1)}, bf16[4,2,512,256]{3,2,...) custom-call(s32[16]{0:T(128)S(1)} %reshape.573.active, bf16[512,512]{1,0:T(8,128)(2,1)S(1)} %fusion.61.q_ref, ...), custom_call_target="tpu_custom_call" | custom-call | flops 12884901888 | bytes 20971520 | tf_op jit(solution)/shard_map/attend_back/pallas_call | solution.py:330
  534.2 10.5 %collective-permute-start.62 = (bf16[2,4,512,256]{3,2,1,0:T(8,128)(2,1)}, bf16[2,4,512,256]{3,2,1,0:T(8,128)(2,1)}, u32[]{:S(2)}, u32[]{:S(2)}) collective-permute-start(bf16[2,4,512,256]{3,2,1,0:T(8,128)(2,1)} %get-tuple-element.56), channel_id=1, source_target_pairs={{1,0},{3,2},{5,4},{7,6},{9,8},{11,10},{13,12},{15,14},{17,16},{19,... | collective-permute-start | bytes 6291464 | tf_op jit(solution)/shard_map/ppermute | solution.py:144
  544.7 36.4 %reduce-scatter.2.cloned.1.call-done = f32[1,272,128]{2,1,0:T(8,128)} async-done(((f32[32,272,128]{2,1,0:T(8,128)}), f32[1,272,128]{2,1,0:T(8,128)}) %reduce-scatter.2.cloned.1.call-update) | async-done | bytes 139280 | tf_op jit(solution)/shard_map/reduce_scatter | solution.py:615
  586.7 5.5 collective-permute-start.66
  614.8 19.8 %collective-permute-done.64 = bf16[4,512,256]{2,1,0:T(8,128)(2,1)S(1)} collective-permute-done((bf16[4,512,256]{2,1,0:T(8,128)(2,1)S(1)}, bf16[4,512,256]{2,1,0:T(8,128)(2,1)S(1)}, u32[]{:S(2)}, u32[]{:S(2)}) %collective-permute-start.64) | collective-permute-done | bytes 1048608 | tf_op jit(solution)/shard_map/ppermute | solution.py:149
  640.1 3.3 collective-permute-done.69
  647.6 3.5 collective-permute-start.76
  651.7 3.6 collective-permute-start.75
  655.3 30.1 %collective-permute-done.78 = bf16[512,256]{1,0:T(8,128)(2,1)S(1)} collective-permute-done((bf16[512,256]{1,0:T(8,128)(2,1)S(1)}, bf16[512,256]{1,0:T(8,128)(2,1)S(1)}, u32[]{:S(2)}, u32[]{:S(2)}) %collective-permute-start.78) | collective-permute-done | bytes 262176 | tf_op jit(solution)/shard_map/ppermute | solution.py:165
  687.1 4.8 collective-permute-done.73
  703.4 2.9 collective-permute-start.87
  714.3 4.4 collective-permute-start.92
  732.6 4.6 collective-permute-start.61
  739.8 9.0 %collective-permute-done.79 = bf16[128,2048]{1,0:T(8,128)(2,1)S(1)} collective-permute-done((bf16[128,2048]{1,0:T(8,128)(2,1)S(1)}, bf16[128,2048]{1,0:T(8,128)(2,1)S(1)}, u32[]{:S(2)}, u32[]{:S(2)}) %collective-permute-start.79) | collective-permute-done | bytes 524320 | tf_op jit(solution)/shard_map/ppermute | solution.py:72
  764.4 3.2 collective-permute-done.102
  769.2 3.4 collective-permute-done.104
  772.6 8.7 %collective-permute-start.105 = (bf16[4,4,4,80,128]{4,3,2,1,0:T(8,128)(2,1)S(1)}, bf16[4,4,4,80,128]{4,3,2,1,0:T(8,128)(2,1)S(1)}, u32[]{:S(2)}, u32[]{:S(2)}) collective-permute-start(bf16[4,4,4,80,128]{4,3,2,1,0:T(8,128)(2,1)S(1)} %bitcast_dynamic-update-slice_fusion), channel_id=1, source_target_pairs={{0,1},{1,0},{2,3},{3,2},{4,5},{5,4},{6,7},{7,6},{8,9},{9,8},{10,11... | collective-permute-start | bytes 3932168 | tf_op jit(solution)/shard_map/ppermute | solution.py:68
  800.9 3.1 fusion.203
  804.1 6.0 fusion.204
  819.2 5.6 copy.361
  824.8 3.9 convert_bitcast_fusion
  828.7 5.6 copy.362
  834.2 3.9 bitcast_convert_fusion
  (732 shorter events, 355.8 us)
Async XLA Ops:
  7.2 296.0 %all-gather.6.cloned.1.call-start = ((), (), s32[]{:S(2)}) async-start(), calls=%async_computation.3 | async-start | bytes 8454144 | tf_op jit(solution)/shard_map/all_gather | solution.py:440
  7.9 304.8 %all-gather.8.cloned.1.call-start = ((), (), s32[]{:S(2)}) async-start(), calls=%async_computation.5 | async-start | bytes 13369344 | tf_op jit(solution)/shard_map/all_gather | solution.py:442
  33.9 547.3 %reduce-scatter.2.cloned.1.call-start = ((), (), s32[]{:S(2)}) async-start(), calls=%async_computation.4 | async-start | bytes 4595712 | tf_op jit(solution)/shard_map/reduce_scatter | solution.py:615
  49.4 14.6 %collective-permute-start.14 = (bf16[4,128,256]{2,1,0:T(8,128)(2,1)S(1)}, bf16[4,128,256]{2,1,0:T(8,128)(2,1)S(1)}, u32[]{:S(2)}, u32[]{:S(2)}) collective-permute-start(bf16[4,128,256]{2,1,0:T(8,128)(2,1)S(1)} %bitcast_dynamic-update-slice_fusion.16), channel_id=1, source_target_pairs={{0,16},{8,24},{16,0},{24,8},{1,17},{9,25},{17,1},{25,9},{2,18},{10... | collective-permute-start | bytes 786440 | tf_op jit(solution)/shard_map/ppermute | solution.py:72
  50.2 15.7 %collective-permute-start.15 = (bf16[4,128,256]{2,1,0:T(8,128)(2,1)S(1)}, bf16[4,128,256]{2,1,0:T(8,128)(2,1)S(1)}, u32[]{:S(2)}, u32[]{:S(2)}) collective-permute-start(bf16[4,128,256]{2,1,0:T(8,128)(2,1)S(1)} %bitcast_dynamic-update-slice_fusion.16), channel_id=1, source_target_pairs={{0,8},{8,16},{16,24},{24,0},{1,9},{9,17},{17,25},{25,1},{2,10},{10... | collective-permute-start | bytes 786440 | tf_op jit(solution)/shard_map/ppermute | solution.py:72
  67.6 47.5 %collective-permute-start.16 = (bf16[2048,512]{1,0:T(8,128)(2,1)}, bf16[2048,512]{1,0:T(8,128)(2,1)}, u32[]{:S(2)}, u32[]{:S(2)}) collective-permute-start(bf16[2048,512]{1,0:T(8,128)(2,1)} %pad_maximum_fusion.1), channel_id=1, source_target_pairs={{0,1},{1,0},{2,3},{3,2},{4,5},{5,4},{6,7},{7,6},{8,9},{9,8},{10,11... | collective-permute-start | bytes 6291464 | tf_op jit(solution)/shard_map/ppermute | solution.py:68
  79.5 19.3 %collective-permute-start.3 = (bf16[128,2048]{1,0:T(8,128)(2,1)}, bf16[128,2048]{1,0:T(8,128)(2,1)S(1)}, u32[]{:S(2)}, u32[]{:S(2)}) collective-permute-start(bf16[128,2048]{1,0:T(8,128)(2,1)} %fusion.45), channel_id=1, source_target_pairs={{0,2},{2,4},{4,6},{6,0},{1,3},{3,5},{5,7},{7,1},{8,10},{10,12},{12... | collective-permute-start | bytes 1572872 | tf_op jit(solution)/shard_map/ppermute | solution.py:72
  79.5 30.6 %collective-permute-start.2 = (bf16[128,2048]{1,0:T(8,128)(2,1)}, bf16[128,2048]{1,0:T(8,128)(2,1)S(1)}, u32[]{:S(2)}, u32[]{:S(2)}) collective-permute-start(bf16[128,2048]{1,0:T(8,128)(2,1)} %fusion.45), channel_id=1, source_target_pairs={{0,4},{2,6},{4,0},{6,2},{1,5},{3,7},{5,1},{7,3},{8,12},{10,14},{12... | collective-permute-start | bytes 1572872 | tf_op jit(solution)/shard_map/ppermute | solution.py:72
  80.0 30.1 %collective-permute-start.1 = (bf16[128,2048]{1,0:T(8,128)(2,1)}, bf16[128,2048]{1,0:T(8,128)(2,1)S(1)}, u32[]{:S(2)}, u32[]{:S(2)}) collective-permute-start(bf16[128,2048]{1,0:T(8,128)(2,1)} %fusion.45), channel_id=1, source_target_pairs={{0,6},{2,0},{4,2},{6,4},{1,7},{3,1},{5,3},{7,5},{8,14},{10,8},{12,... | collective-permute-start | bytes 1572872 | tf_op jit(solution)/shard_map/ppermute | solution.py:72
  120.4 13.3 %collective-permute-start.17 = (bf16[512,256]{1,0:T(8,128)(2,1)S(1)}, bf16[512,256]{1,0:T(8,128)(2,1)S(1)}, u32[]{:S(2)}, u32[]{:S(2)}) collective-permute-start(bf16[512,256]{1,0:T(8,128)(2,1)S(1)} %get-tuple-element.42), channel_id=1, source_target_pairs={{0,24},{8,0},{16,8},{24,16},{1,25},{9,1},{17,9},{25,17},{2,26},{10... | collective-permute-start | bytes 786440 | tf_op jit(solution)/shard_map/ppermute | solution.py:72
  123.0 14.7 %collective-permute-start.19 = (bf16[512,256]{1,0:T(8,128)(2,1)S(1)}, bf16[512,256]{1,0:T(8,128)(2,1)S(1)}, u32[]{:S(2)}, u32[]{:S(2)}) collective-permute-start(bf16[512,256]{1,0:T(8,128)(2,1)S(1)} %get-tuple-element.42), channel_id=1, source_target_pairs={{0,8},{8,16},{16,24},{24,0},{1,9},{9,17},{17,25},{25,1},{2,10},{10... | collective-permute-start | bytes 786440 | tf_op jit(solution)/shard_map/ppermute | solution.py:72
  124.6 13.2 %collective-permute-start.20 = (bf16[512,256]{1,0:T(8,128)(2,1)S(1)}, bf16[512,256]{1,0:T(8,128)(2,1)S(1)}, u32[]{:S(2)}, u32[]{:S(2)}) collective-permute-start(bf16[512,256]{1,0:T(8,128)(2,1)S(1)} %fusion.71), channel_id=1, source_target_pairs={{0,32},{1,33},{32,0},{33,1},{64,96},{65,97},{96,64},{97,65},{2,34}... | collective-permute-start | bytes 786440 | tf_op jit(solution)/shard_map/ppermute | solution.py:130
  124.7 16.8 %collective-permute-start.21 = (bf16[512,256]{1,0:T(8,128)(2,1)S(1)}, bf16[512,256]{1,0:T(8,128)(2,1)S(1)}, u32[]{:S(2)}, u32[]{:S(2)}) collective-permute-start(bf16[512,256]{1,0:T(8,128)(2,1)S(1)} %fusion.71), channel_id=1, source_target_pairs={{1,64},{33,96},{3,66},{35,98},{5,68},{37,100},{7,70},{39,102},{9,7... | collective-permute-start | bytes 786440 | tf_op jit(solution)/shard_map/ppermute | solution.py:131
  142.6 14.9 %collective-permute-start.32 = (bf16[2,512,256]{2,1,0:T(8,128)(2,1)}, bf16[2,512,256]{2,1,0:T(8,128)(2,1)}, u32[]{:S(2)}, u32[]{:S(2)}) collective-permute-start(bf16[2,512,256]{2,1,0:T(8,128)(2,1)} %get-tuple-element.225), channel_id=1, source_target_pairs={{0,8},{8,16},{16,24},{24,0},{1,9},{9,17},{17,25},{25,1},{2,10},{10... | collective-permute-start | bytes 1572872 | tf_op jit(solution)/shard_map/ppermute | solution.py:72
  143.9 25.2 %collective-permute-start.31 = (bf16[2,512,256]{2,1,0:T(8,128)(2,1)}, bf16[2,512,256]{2,1,0:T(8,128)(2,1)}, u32[]{:S(2)}, u32[]{:S(2)}) collective-permute-start(bf16[2,512,256]{2,1,0:T(8,128)(2,1)} %get-tuple-element.225), channel_id=1, source_target_pairs={{0,16},{8,24},{16,0},{24,8},{1,17},{9,25},{17,1},{25,9},{2,18},{10... | collective-permute-start | bytes 1572872 | tf_op jit(solution)/shard_map/ppermute | solution.py:72
  145.9 23.8 %collective-permute-start.30 = (bf16[2,512,256]{2,1,0:T(8,128)(2,1)}, bf16[2,512,256]{2,1,0:T(8,128)(2,1)}, u32[]{:S(2)}, u32[]{:S(2)}) collective-permute-start(bf16[2,512,256]{2,1,0:T(8,128)(2,1)} %get-tuple-element.225), channel_id=1, source_target_pairs={{0,24},{8,0},{16,8},{24,16},{1,25},{9,1},{17,9},{25,17},{2,26},{10... | collective-permute-start | bytes 1572872 | tf_op jit(solution)/shard_map/ppermute | solution.py:72
  148.6 47.6 %collective-permute-start.25 = (bf16[4,512,256]{2,1,0:T(8,128)(2,1)}, bf16[4,512,256]{2,1,0:T(8,128)(2,1)}, u32[]{:S(2)}, u32[]{:S(2)}) collective-permute-start(bf16[4,512,256]{2,1,0:T(8,128)(2,1)} %get-tuple-element.191), channel_id=1, source_target_pairs={{0,32},{1,33},{32,0},{33,1},{64,96},{65,97},{96,64},{97,65},{2,34}... | collective-permute-start | bytes 3145736 | tf_op jit(solution)/shard_map/ppermute | solution.py:134
  150.1 62.2 %collective-permute-start.42 = (bf16[64,2048]{1,0:T(8,128)(2,1)}, bf16[64,2048]{1,0:T(8,128)(2,1)}, u32[]{:S(2)}, u32[]{:S(2)}) collective-permute-start(bf16[64,2048]{1,0:T(8,128)(2,1)} %get-tuple-element.217), channel_id=1, source_target_pairs={{0,1},{1,0},{2,3},{3,2},{4,5},{5,4},{6,7},{7,6},{8,9},{9,8},{10,11... | collective-permute-start | bytes 786440 | tf_op jit(solution)/shard_map/ppermute | solution.py:68
  172.8 64.4 %collective-permute-start.33 = (bf16[4,2,512,256]{3,2,1,0:T(8,128)(2,1)}, bf16[4,2,512,256]{3,2,1,0:T(8,128)(2,1)}, u32[]{:S(2)}, u32[]{:S(2)}) collective-permute-start(bf16[4,2,512,256]{3,2,1,0:T(8,128)(2,1)} %pad_maximum_fusion.3.vown_ref), channel_id=1, source_target_pairs={{0,1},{2,3},{4,5},{6,7},{8,9},{10,11},{12,13},{14,15},{16,17},{18,... | collective-permute-start | bytes 6291464 | tf_op jit(solution)/shard_map/ppermute | solution.py:139
  199.0 49.9 %collective-permute-start.26 = (bf16[2,4,512,256]{3,2,1,0:T(8,128)(2,1)}, bf16[2,4,512,256]{3,2,1,0:T(8,128)(2,1)}, u32[]{:S(2)}, u32[]{:S(2)}) collective-permute-start(bf16[2,4,512,256]{3,2,1,0:T(8,128)(2,1)} %pad_maximum_fusion.2.kown_ref), channel_id=1, source_target_pairs={{0,1},{2,3},{4,5},{6,7},{8,9},{10,11},{12,13},{14,15},{16,17},{18,... | collective-permute-start | bytes 6291464 | tf_op jit(solution)/shard_map/ppermute | solution.py:138
  210.9 14.9 %collective-permute-start.29 = (bf16[2,512,256]{2,1,0:T(8,128)(2,1)}, bf16[2,512,256]{2,1,0:T(8,128)(2,1)}, u32[]{:S(2)}, u32[]{:S(2)}) collective-permute-start(bf16[2,512,256]{2,1,0:T(8,128)(2,1)} %get-tuple-element.223), channel_id=1, source_target_pairs={{64,72},{72,80},{80,88},{88,64},{66,74},{74,82},{82,90},{90,66},{6... | collective-permute-start | bytes 1572872 | tf_op jit(solution)/shard_map/ppermute | solution.py:121
  214.1 19.7 %collective-permute-start.28 = (bf16[2,512,256]{2,1,0:T(8,128)(2,1)}, bf16[2,512,256]{2,1,0:T(8,128)(2,1)}, u32[]{:S(2)}, u32[]{:S(2)}) collective-permute-start(bf16[2,512,256]{2,1,0:T(8,128)(2,1)} %get-tuple-element.223), channel_id=1, source_target_pairs={{64,80},{72,88},{80,64},{88,72},{66,82},{74,90},{82,66},{90,74},{6... | collective-permute-start | bytes 1572872 | tf_op jit(solution)/shard_map/ppermute | solution.py:121
  220.7 28.3 %collective-permute-start.24 = (bf16[4,512,256]{2,1,0:T(8,128)(2,1)}, bf16[4,512,256]{2,1,0:T(8,128)(2,1)S(1)}, u32[]{:S(2)}, u32[]{:S(2)}) collective-permute-start(bf16[4,512,256]{2,1,0:T(8,128)(2,1)} %get-tuple-element.191), channel_id=1, source_target_pairs={{1,96},{33,64},{3,98},{35,66},{5,100},{37,68},{7,102},{39,70},{9,1... | collective-permute-start | bytes 3145736 | tf_op jit(solution)/shard_map/ppermute | solution.py:135
  225.7 23.2 %collective-permute-start.23 = (bf16[4,512,256]{2,1,0:T(8,128)(2,1)}, bf16[4,512,256]{2,1,0:T(8,128)(2,1)S(1)}, u32[]{:S(2)}, u32[]{:S(2)}) collective-permute-start(bf16[4,512,256]{2,1,0:T(8,128)(2,1)} %get-tuple-element.191), channel_id=1, source_target_pairs={{1,64},{33,96},{3,66},{35,98},{5,68},{37,100},{7,70},{39,102},{9,7... | collective-permute-start | bytes 3145736 | tf_op jit(solution)/shard_map/ppermute | solution.py:135
  264.4 13.0 %collective-permute-start.34 = (bf16[128,512]{1,0:T(8,128)(2,1)}, bf16[128,512]{1,0:T(8,128)(2,1)}, u32[]{:S(2)}, u32[]{:S(2)}) collective-permute-start(bf16[128,512]{1,0:T(8,128)(2,1)} %get-tuple-element.220), channel_id=1, source_target_pairs={{0,2},{2,4},{4,6},{6,0},{1,3},{3,5},{5,7},{7,1},{8,10},{10,12},{12... | collective-permute-start | bytes 393224 | tf_op jit(solution)/shard_map/ppermute | solution.py:72
  264.5 14.7 %collective-permute-start.35 = (bf16[128,512]{1,0:T(8,128)(2,1)}, bf16[128,512]{1,0:T(8,128)(2,1)S(1)}, u32[]{:S(2)}, u32[]{:S(2)}) collective-permute-start(bf16[128,512]{1,0:T(8,128)(2,1)} %get-tuple-element.219), channel_id=1, source_target_pairs={{0,4},{2,6},{4,0},{6,2},{1,5},{3,7},{5,1},{7,3},{8,12},{10,14},{12... | collective-permute-start | bytes 393224 | tf_op jit(solution)/shard_map/ppermute | solution.py:72
  267.1 12.3 %collective-permute-start.36 = (bf16[128,512]{1,0:T(8,128)(2,1)}, bf16[128,512]{1,0:T(8,128)(2,1)S(1)}, u32[]{:S(2)}, u32[]{:S(2)}) collective-permute-start(bf16[128,512]{1,0:T(8,128)(2,1)} %get-tuple-element.218), channel_id=1, source_target_pairs={{0,6},{2,0},{4,2},{6,4},{1,7},{3,1},{5,3},{7,5},{8,14},{10,8},{12,... | collective-permute-start | bytes 393224 | tf_op jit(solution)/shard_map/ppermute | solution.py:72
  269.8 26.5 %collective-permute-start.43 = (bf16[128,2048]{1,0:T(8,128)(2,1)}, bf16[128,2048]{1,0:T(8,128)(2,1)}, u32[]{:S(2)}, u32[]{:S(2)}) collective-permute-start(bf16[128,2048]{1,0:T(8,128)(2,1)} %pad_maximum_fusion.14), channel_id=1, source_target_pairs={{0,24},{8,0},{16,8},{24,16},{1,25},{9,1},{17,9},{25,17},{2,26},{10... | collective-permute-start | bytes 1572872 | tf_op jit(solution)/shard_map/ppermute | solution.py:72
  276.4 21.0 %collective-permute-start.44 = (bf16[128,2048]{1,0:T(8,128)(2,1)}, bf16[128,2048]{1,0:T(8,128)(2,1)}, u32[]{:S(2)}, u32[]{:S(2)}) collective-permute-start(bf16[128,2048]{1,0:T(8,128)(2,1)} %pad_maximum_fusion.14), channel_id=1, source_target_pairs={{0,16},{8,24},{16,0},{24,8},{1,17},{9,25},{17,1},{25,9},{2,18},{10... | collective-permute-start | bytes 1572872 | tf_op jit(solution)/shard_map/ppermute | solution.py:72
  277.5 22.9 %collective-permute-start.45 = (bf16[128,2048]{1,0:T(8,128)(2,1)}, bf16[128,2048]{1,0:T(8,128)(2,1)S(1)}, u32[]{:S(2)}, u32[]{:S(2)}) collective-permute-start(bf16[128,2048]{1,0:T(8,128)(2,1)} %pad_maximum_fusion.14), channel_id=1, source_target_pairs={{0,8},{8,16},{16,24},{24,0},{1,9},{9,17},{17,25},{25,1},{2,10},{10... | collective-permute-start | bytes 1572872 | tf_op jit(solution)/shard_map/ppermute | solution.py:72
  310.0 22.0 %collective-permute-start.39 = (bf16[128,2048]{1,0:T(8,128)(2,1)}, bf16[128,2048]{1,0:T(8,128)(2,1)}, u32[]{:S(2)}, u32[]{:S(2)}) collective-permute-start(bf16[128,2048]{1,0:T(8,128)(2,1)} %multiply_convert_fusion.7), channel_id=1, source_target_pairs={{0,8},{8,16},{16,24},{24,0},{1,9},{9,17},{17,25},{25,1},{2,10},{10... | collective-permute-start | bytes 1572872 | tf_op jit(solution)/shard_map/ppermute | solution.py:72
  310.0 22.0 %collective-permute-start.38 = (bf16[128,2048]{1,0:T(8,128)(2,1)}, bf16[128,2048]{1,0:T(8,128)(2,1)}, u32[]{:S(2)}, u32[]{:S(2)}) collective-permute-start(bf16[128,2048]{1,0:T(8,128)(2,1)} %multiply_convert_fusion.7), channel_id=1, source_target_pairs={{0,16},{8,24},{16,0},{24,8},{1,17},{9,25},{17,1},{25,9},{2,18},{10... | collective-permute-start | bytes 1572872 | tf_op jit(solution)/shard_map/ppermute | solution.py:72
  312.7 19.3 %collective-permute-start.37 = (bf16[128,2048]{1,0:T(8,128)(2,1)}, bf16[128,2048]{1,0:T(8,128)(2,1)}, u32[]{:S(2)}, u32[]{:S(2)}) collective-permute-start(bf16[128,2048]{1,0:T(8,128)(2,1)} %multiply_convert_fusion.7), channel_id=1, source_target_pairs={{0,24},{8,0},{16,8},{24,16},{1,25},{9,1},{17,9},{25,17},{2,26},{10... | collective-permute-start | bytes 1572872 | tf_op jit(solution)/shard_map/ppermute | solution.py:72
  329.3 46.5 %collective-permute-start.40 = (bf16[2048,2048]{1,0:T(8,128)(2,1)}, bf16[2048,2048]{1,0:T(8,128)(2,1)}, u32[]{:S(2)}, u32[]{:S(2)}) collective-permute-start(bf16[2048,2048]{1,0:T(8,128)(2,1)} %bitcast.491), channel_id=1, source_target_pairs={{0,1},{1,0},{2,3},{3,2},{4,5},{5,4},{6,7},{7,6},{8,9},{9,8},{10,11... | collective-permute-start | bytes 25165832 | tf_op jit(solution)/shard_map/ppermute | solution.py:68
  345.4 25.7 %collective-permute-start.41 = (bf16[1024,2048]{1,0:T(8,128)(2,1)S(1)}, bf16[1024,2048]{1,0:T(8,128)(2,1)}, u32[]{:S(2)}, u32[]{:S(2)}) collective-permute-start(bf16[1024,2048]{1,0:T(8,128)(2,1)S(1)} %bitcast.505), channel_id=1, source_target_pairs={{0,1},{1,0},{2,3},{3,2},{4,5},{5,4},{6,7},{7,6},{8,9},{9,8},{10,11... | collective-permute-start | bytes 12582920 | tf_op jit(solution)/shard_map/ppermute | solution.py:68
  399.9 55.9 %collective-permute-start.48 = (bf16[128,2048]{1,0:T(8,128)(2,1)}, bf16[128,2048]{1,0:T(8,128)(2,1)}, u32[]{:S(2)}, u32[]{:S(2)}) collective-permute-start(bf16[128,2048]{1,0:T(8,128)(2,1)} %get-tuple-element.174), channel_id=1, source_target_pairs={{0,24},{8,0},{16,8},{24,16},{1,25},{9,1},{17,9},{25,17},{2,26},{10... | collective-permute-start | bytes 1572872 | tf_op jit(solution)/shard_map/ppermute | solution.py:72
  401.4 17.8 %collective-permute-start.51 = (bf16[128,256]{0,1:T(8,128)(2,1)S(1)}, bf16[128,256]{0,1:T(8,128)(2,1)S(1)}, u32[]{:S(2)}, u32[]{:S(2)}) collective-permute-start(bf16[128,256]{0,1:T(8,128)(2,1)S(1)} %get-tuple-element.236), channel_id=1, source_target_pairs={{0,24},{8,0},{16,8},{24,16},{1,25},{9,1},{17,9},{25,17},{2,26},{10... | collective-permute-start | bytes 196616 | tf_op jit(solution)/shard_map/ppermute | solution.py:72
  406.8 12.1 %collective-permute-start.58 = (bf16[128,128]{1,0:T(8,128)(2,1)S(1)}, bf16[128,128]{1,0:T(8,128)(2,1)S(1)}, u32[]{:S(2)}, u32[]{:S(2)}) collective-permute-start(bf16[128,128]{1,0:T(8,128)(2,1)S(1)} %get-tuple-element.244), channel_id=1, source_target_pairs={{0,16},{8,24},{16,0},{24,8},{1,17},{9,25},{17,1},{25,9},{2,18},{10... | collective-permute-start | bytes 98312 | tf_op jit(solution)/shard_map/ppermute | solution.py:72
  415.9 39.8 %collective-permute-start.47 = (bf16[128,2048]{1,0:T(8,128)(2,1)}, bf16[128,2048]{1,0:T(8,128)(2,1)}, u32[]{:S(2)}, u32[]{:S(2)}) collective-permute-start(bf16[128,2048]{1,0:T(8,128)(2,1)} %get-tuple-element.175), channel_id=1, source_target_pairs={{0,8},{8,16},{16,24},{24,0},{1,9},{9,17},{17,25},{25,1},{2,10},{10... | collective-permute-start | bytes 1572872 | tf_op jit(solution)/shard_map/ppermute | solution.py:72
  417.4 38.4 %collective-permute-start.46 = (bf16[128,2048]{1,0:T(8,128)(2,1)}, bf16[128,2048]{1,0:T(8,128)(2,1)}, u32[]{:S(2)}, u32[]{:S(2)}) collective-permute-start(bf16[128,2048]{1,0:T(8,128)(2,1)} %get-tuple-element.173), channel_id=1, source_target_pairs={{0,16},{8,24},{16,0},{24,8},{1,17},{9,25},{17,1},{25,9},{2,18},{10... | collective-permute-start | bytes 1572872 | tf_op jit(solution)/shard_map/ppermute | solution.py:72
  418.9 21.8 %collective-permute-start.50 = (bf16[128,256]{0,1:T(8,128)(2,1)}, bf16[128,256]{0,1:T(8,128)(2,1)}, u32[]{:S(2)}, u32[]{:S(2)}) collective-permute-start(bf16[128,256]{0,1:T(8,128)(2,1)} %get-tuple-element.237), channel_id=1, source_target_pairs={{0,8},{8,16},{16,24},{24,0},{1,9},{9,17},{17,25},{25,1},{2,10},{10... | collective-permute-start | bytes 196616 | tf_op jit(solution)/shard_map/ppermute | solution.py:72
  419.2 25.0 %collective-permute-start.49 = (bf16[128,256]{0,1:T(8,128)(2,1)}, bf16[128,256]{0,1:T(8,128)(2,1)}, u32[]{:S(2)}, u32[]{:S(2)}) collective-permute-start(bf16[128,256]{0,1:T(8,128)(2,1)} %get-tuple-element.235), channel_id=1, source_target_pairs={{0,16},{8,24},{16,0},{24,8},{1,17},{9,25},{17,1},{25,9},{2,18},{10... | collective-permute-start | bytes 196616 | tf_op jit(solution)/shard_map/ppermute | solution.py:72
  491.4 309.5 %all-gather.10.cloned.1.call-start = ((), (), s32[]{:S(2)}) async-start(), calls=%async_computation.6 | async-start | bytes 8982528 | tf_op jit(solution)/shard_map/all_gather | solution.py:619
  515.0 88.4 %collective-permute-start.57 = (bf16[128,2048]{1,0:T(8,128)(2,1)}, bf16[128,2048]{1,0:T(8,128)(2,1)}, u32[]{:S(2)}, u32[]{:S(2)}) collective-permute-start(bf16[128,2048]{1,0:T(8,128)(2,1)} %get-tuple-element.171), channel_id=1, source_target_pairs={{0,24},{8,0},{16,8},{24,16},{1,25},{9,1},{17,9},{25,17},{2,26},{10... | collective-permute-start | bytes 1572872 | tf_op jit(solution)/shard_map/ppermute | solution.py:72
  515.6 89.4 %collective-permute-start.56 = (bf16[128,2048]{1,0:T(8,128)(2,1)}, bf16[128,2048]{1,0:T(8,128)(2,1)}, u32[]{:S(2)}, u32[]{:S(2)}) collective-permute-start(bf16[128,2048]{1,0:T(8,128)(2,1)} %get-tuple-element.172), channel_id=1, source_target_pairs={{0,8},{8,16},{16,24},{24,0},{1,9},{9,17},{17,25},{25,1},{2,10},{10... | collective-permute-start | bytes 1572872 | tf_op jit(solution)/shard_map/ppermute | solution.py:72
  516.5 89.8 %collective-permute-start.55 = (bf16[128,2048]{1,0:T(8,128)(2,1)}, bf16[128,2048]{1,0:T(8,128)(2,1)}, u32[]{:S(2)}, u32[]{:S(2)}) collective-permute-start(bf16[128,2048]{1,0:T(8,128)(2,1)} %get-tuple-element.170), channel_id=1, source_target_pairs={{0,16},{8,24},{16,0},{24,8},{1,17},{9,25},{17,1},{25,9},{2,18},{10... | collective-permute-start | bytes 1572872 | tf_op jit(solution)/shard_map/ppermute | solution.py:72
  534.2 66.4 %collective-permute-start.62 = (bf16[2,4,512,256]{3,2,1,0:T(8,128)(2,1)}, bf16[2,4,512,256]{3,2,1,0:T(8,128)(2,1)}, u32[]{:S(2)}, u32[]{:S(2)}) collective-permute-start(bf16[2,4,512,256]{3,2,1,0:T(8,128)(2,1)} %get-tuple-element.56), channel_id=1, source_target_pairs={{1,0},{3,2},{5,4},{7,6},{9,8},{11,10},{13,12},{15,14},{17,16},{19,... | collective-permute-start | bytes 6291464 | tf_op jit(solution)/shard_map/ppermute | solution.py:144
  586.7 21.0 %collective-permute-start.66 = (bf16[4,2,512,256]{3,2,1,0:T(8,128)(2,1)}, bf16[4,2,512,256]{3,2,1,0:T(8,128)(2,1)}, u32[]{:S(2)}, u32[]{:S(2)}) collective-permute-start(bf16[4,2,512,256]{3,2,1,0:T(8,128)(2,1)} %copy-done.5), channel_id=1, source_target_pairs={{1,0},{3,2},{5,4},{7,6},{9,8},{11,10},{13,12},{15,14},{17,16},{19,... | collective-permute-start | bytes 6291464 | tf_op jit(solution)/shard_map/ppermute | solution.py:144
  603.4 31.2 %collective-permute-start.64 = (bf16[4,512,256]{2,1,0:T(8,128)(2,1)S(1)}, bf16[4,512,256]{2,1,0:T(8,128)(2,1)S(1)}, u32[]{:S(2)}, u32[]{:S(2)}) collective-permute-start(bf16[4,512,256]{2,1,0:T(8,128)(2,1)S(1)} %get-tuple-element.169), channel_id=1, source_target_pairs={{64,1},{96,33},{66,3},{98,35},{68,5},{100,37},{70,7},{102,39},{72,... | collective-permute-start | bytes 3145736 | tf_op jit(solution)/shard_map/ppermute | solution.py:149
  605.0 35.1 %collective-permute-start.65 = (bf16[4,512,256]{2,1,0:T(8,128)(2,1)S(1)}, bf16[4,512,256]{2,1,0:T(8,128)(2,1)S(1)}, u32[]{:S(2)}, u32[]{:S(2)}) collective-permute-start(bf16[4,512,256]{2,1,0:T(8,128)(2,1)S(1)} %get-tuple-element.168), channel_id=1, source_target_pairs={{96,1},{64,33},{98,3},{66,35},{100,5},{68,37},{102,7},{70,39},{104... | collective-permute-start | bytes 3145736 | tf_op jit(solution)/shard_map/ppermute | solution.py:149
  607.7 35.7 %collective-permute-start.63 = (bf16[4,512,256]{2,1,0:T(8,128)(2,1)S(1)}, bf16[4,512,256]{2,1,0:T(8,128)(2,1)S(1)}, u32[]{:S(2)}, u32[]{:S(2)}) collective-permute-start(bf16[4,512,256]{2,1,0:T(8,128)(2,1)S(1)} %fusion.51), channel_id=1, source_target_pairs={{0,32},{1,33},{32,0},{33,1},{64,96},{65,97},{96,64},{97,65},{2,34}... | collective-permute-start | bytes 3145736 | tf_op jit(solution)/shard_map/ppermute | solution.py:148
  611.1 28.9 %collective-permute-start.67 = (bf16[2,512,256]{2,1,0:T(8,128)(2,1)S(1)}, bf16[2,512,256]{2,1,0:T(8,128)(2,1)S(1)}, u32[]{:S(2)}, u32[]{:S(2)}) collective-permute-start(bf16[2,512,256]{2,1,0:T(8,128)(2,1)S(1)} %get-tuple-element.167), channel_id=1, source_target_pairs={{0,8},{8,16},{16,24},{24,0},{1,9},{9,17},{17,25},{25,1},{2,10},{10... | collective-permute-start | bytes 1572872 | tf_op jit(solution)/shard_map/ppermute | solution.py:72
  612.4 27.7 %collective-permute-start.68 = (bf16[2,512,256]{2,1,0:T(8,128)(2,1)S(1)}, bf16[2,512,256]{2,1,0:T(8,128)(2,1)S(1)}, u32[]{:S(2)}, u32[]{:S(2)}) collective-permute-start(bf16[2,512,256]{2,1,0:T(8,128)(2,1)S(1)} %get-tuple-element.166), channel_id=1, source_target_pairs={{0,16},{8,24},{16,0},{24,8},{1,17},{9,25},{17,1},{25,9},{2,18},{10... | collective-permute-start | bytes 1572872 | tf_op jit(solution)/shard_map/ppermute | solution.py:72
  644.8 40.7 %collective-permute-start.78 = (bf16[512,256]{1,0:T(8,128)(2,1)S(1)}, bf16[512,256]{1,0:T(8,128)(2,1)S(1)}, u32[]{:S(2)}, u32[]{:S(2)}) collective-permute-start(bf16[512,256]{1,0:T(8,128)(2,1)S(1)} %get-tuple-element.209), channel_id=1, source_target_pairs={{96,1},{64,33},{98,3},{66,35},{100,5},{68,37},{102,7},{70,39},{104... | collective-permute-start | bytes 786440 | tf_op jit(solution)/shard_map/ppermute | solution.py:165
  646.1 39.8 %collective-permute-start.77 = (bf16[512,256]{1,0:T(8,128)(2,1)S(1)}, bf16[512,256]{1,0:T(8,128)(2,1)S(1)}, u32[]{:S(2)}, u32[]{:S(2)}) collective-permute-start(bf16[512,256]{1,0:T(8,128)(2,1)S(1)} %get-tuple-element.208), channel_id=1, source_target_pairs={{64,1},{96,33},{66,3},{98,35},{68,5},{100,37},{70,7},{102,39},{72,... | collective-permute-start | bytes 786440 | tf_op jit(solution)/shard_map/ppermute | solution.py:165
  647.6 38.2 %collective-permute-start.76 = (bf16[512,256]{1,0:T(8,128)(2,1)S(1)}, bf16[512,256]{1,0:T(8,128)(2,1)S(1)}, u32[]{:S(2)}, u32[]{:S(2)}) collective-permute-start(bf16[512,256]{1,0:T(8,128)(2,1)S(1)} %fusion.97), channel_id=1, source_target_pairs={{0,32},{1,33},{32,0},{33,1},{64,96},{65,97},{96,64},{97,65},{2,34}... | collective-permute-start | bytes 786440 | tf_op jit(solution)/shard_map/ppermute | solution.py:163
  651.7 35.4 %collective-permute-start.75 = (bf16[512,256]{1,0:T(8,128)(2,1)S(1)}, bf16[512,256]{1,0:T(8,128)(2,1)S(1)}, u32[]{:S(2)}, u32[]{:S(2)}) collective-permute-start(bf16[512,256]{1,0:T(8,128)(2,1)S(1)} %get-tuple-element.188), channel_id=1, source_target_pairs={{0,24},{8,0},{16,8},{24,16},{1,25},{9,1},{17,9},{25,17},{2,26},{10... | collective-permute-start | bytes 786440 | tf_op jit(solution)/shard_map/ppermute | solution.py:72
  655.3 31.8 %collective-permute-start.74 = (bf16[512,256]{1,0:T(8,128)(2,1)S(1)}, bf16[512,256]{1,0:T(8,128)(2,1)S(1)}, u32[]{:S(2)}, u32[]{:S(2)}) collective-permute-start(bf16[512,256]{1,0:T(8,128)(2,1)S(1)} %get-tuple-element.189), channel_id=1, source_target_pairs={{0,16},{8,24},{16,0},{24,8},{1,17},{9,25},{17,1},{25,9},{2,18},{10... | collective-permute-start | bytes 786440 | tf_op jit(solution)/shard_map/ppermute | solution.py:72
  724.8 13.0 %collective-permute-start.81 = (bf16[128,2048]{1,0:T(8,128)(2,1)S(1)}, bf16[128,2048]{1,0:T(8,128)(2,1)S(1)}, u32[]{:S(2)}, u32[]{:S(2)}) collective-permute-start(bf16[128,2048]{1,0:T(8,128)(2,1)S(1)} %get-tuple-element.160), channel_id=1, source_target_pairs={{0,6},{2,0},{4,2},{6,4},{1,7},{3,1},{5,3},{7,5},{8,14},{10,8},{12,... | collective-permute-start | bytes 1572872 | tf_op jit(solution)/shard_map/ppermute | solution.py:72
  727.2 12.5 %collective-permute-start.80 = (bf16[128,2048]{1,0:T(8,128)(2,1)S(1)}, bf16[128,2048]{1,0:T(8,128)(2,1)S(1)}, u32[]{:S(2)}, u32[]{:S(2)}) collective-permute-start(bf16[128,2048]{1,0:T(8,128)(2,1)S(1)} %get-tuple-element.161), channel_id=1, source_target_pairs={{0,2},{2,4},{4,6},{6,0},{1,3},{3,5},{5,7},{7,1},{8,10},{10,12},{12... | collective-permute-start | bytes 1572872 | tf_op jit(solution)/shard_map/ppermute | solution.py:72
  727.2 21.6 %collective-permute-start.79 = (bf16[128,2048]{1,0:T(8,128)(2,1)S(1)}, bf16[128,2048]{1,0:T(8,128)(2,1)S(1)}, u32[]{:S(2)}, u32[]{:S(2)}) collective-permute-start(bf16[128,2048]{1,0:T(8,128)(2,1)S(1)} %get-tuple-element.159), channel_id=1, source_target_pairs={{0,4},{2,6},{4,0},{6,2},{1,5},{3,7},{5,1},{7,3},{8,12},{10,14},{12... | collective-permute-start | bytes 1572872 | tf_op jit(solution)/shard_map/ppermute | solution.py:72
  732.6 49.4 %collective-permute-start.61 = (bf16[64,2048]{1,0:T(8,128)(2,1)S(1)}, bf16[64,2048]{1,0:T(8,128)(2,1)S(1)}, u32[]{:S(2)}, u32[]{:S(2)}) collective-permute-start(bf16[64,2048]{1,0:T(8,128)(2,1)S(1)} %get-tuple-element.211), channel_id=1, source_target_pairs={{0,1},{1,0},{2,3},{3,2},{4,5},{5,4},{6,7},{7,6},{8,9},{9,8},{10,11... | collective-permute-start | bytes 786440 | tf_op jit(solution)/shard_map/ppermute | solution.py:68
  737.3 13.6 %collective-permute-start.96 = (bf16[80,128]{1,0:T(8,128)(2,1)S(1)}, bf16[80,128]{1,0:T(8,128)(2,1)S(1)}, u32[]{:S(2)}, u32[]{:S(2)}) collective-permute-start(bf16[80,128]{1,0:T(8,128)(2,1)S(1)} %get-tuple-element.127), channel_id=1, source_target_pairs={{0,24},{8,0},{16,8},{24,16},{1,25},{9,1},{17,9},{25,17},{2,26},{10... | collective-permute-start | bytes 61448 | tf_op jit(solution)/shard_map/ppermute | solution.py:72
  772.6 12.7 %collective-permute-start.105 = (bf16[4,4,4,80,128]{4,3,2,1,0:T(8,128)(2,1)S(1)}, bf16[4,4,4,80,128]{4,3,2,1,0:T(8,128)(2,1)S(1)}, u32[]{:S(2)}, u32[]{:S(2)}) collective-permute-start(bf16[4,4,4,80,128]{4,3,2,1,0:T(8,128)(2,1)S(1)} %bitcast_dynamic-update-slice_fusion), channel_id=1, source_target_pairs={{0,1},{1,0},{2,3},{3,2},{4,5},{5,4},{6,7},{7,6},{8,9},{9,8},{10,11... | collective-permute-start | bytes 3932168 | tf_op jit(solution)/shard_map/ppermute | solution.py:68
  (177 other events, 1882.4 us)
Sparse Core Ops, SparseCore 0:
  11.0 83.5 all-gather.5
  97.3 127.3 all-gather.7
  491.5 89.6 reduce-scatter.1
  584.0 85.8 all-gather.9
